TPU v7x, 768 devices: a whole 4x8x12 slice. The times are simulated.
768 devices in a mesh: dp: 24 (over z, y_hi), outer: 32 (over y_lo, x, core).
Axes of the slice: x: 4, y: 8 (y_hi: 2, y_lo: 4; y = y_hi * 4 + y_lo), z: 12, core: 2. Of those that a mesh axis runs over, the one named last changes fastest.
Arguments:
- images: bfloat16 [344064, 1152], P(('dp', 'outer')), may hold values from -1.1953125 to 1.1953125
- texts: bfloat16 [344064, 1152], P(('dp', 'outer')), may hold values from -1.1953125 to 1.1953125
- positive_index: int32 [768, 448], P(('dp', 'outer')), may hold values from 0 to 447, each once within a row
- log_scale: float32 [1], replicated, may hold values from 0 to 1
- bias: float32 [1], replicated, may hold values from -5 to -1
Outputs:
- row_loss: float32 [344064], P(('dp', 'outer'))
- image_grad: bfloat16 [344064, 1152], P(('dp', 'outer'))
- text_grad: bfloat16 [344064, 1152], P(('dp', 'outer'))
Inputs may be any that keep to these rules, and one draw needn't show every extreme that they name: Each row of positive_index is a permutation: every text of a block is the positive of exactly one image of that block.
All inputs are finite; a program needn't handle non-finite values.
Results may differ from a plain program's by a relative error of at most 0.008.
Values may be sent and summed in bfloat16 or wider, within the bound.
No kernel may reach another device: no remote copies, remote signals or barrier semaphores. Data moves between devices by JAX's collectives and lax.ppermute only.
A program may use at most 32 MiB of HBM per device.

v0:
```python
import jax
import jax.numpy as jnp
from jax import lax
from jax.sharding import PartitionSpec as P


def passed_along(x, axis, by):
    devices = lax.axis_size(axis)
    return lax.ppermute(x, axis, [(i, (i + by) % devices) for i in range(devices)])


def logit_tile(left, right, temper, offset_b):
    product = lax.dot_general(
        left, right, (((1,), (1,)), ((), ())), preferred_element_type=jnp.float32
    )
    return temper * product + offset_b


def text_part(coeff, image_rows):
    product = lax.dot_general(
        coeff, image_rows, (((0,), (0,)), ((), ())), preferred_element_type=jnp.float32
    )
    return product.astype(jnp.bfloat16)


def local(images, texts, positive_index, log_scale, bias):
    temper = jnp.exp(log_scale[0])
    offset_b = bias[0]
    row_count = images.shape[0]
    positive_mask = positive_index[0][:, None] == lax.broadcasted_iota(
        jnp.int32, (row_count, row_count), 1
    )
    cycle_text = passed_along(texts, "dp", 1)
    pod_text = passed_along(texts, "outer", 1)
    own_logits = logit_tile(images, texts, temper, offset_b)
    cycle_logits = logit_tile(images, cycle_text, temper, offset_b)
    pod_logits = logit_tile(images, pod_text, temper, offset_b)
    signed = jnp.where(positive_mask, own_logits, -own_logits)
    loss_sum = jnp.sum(jax.nn.softplus(-signed), axis=1)
    loss_sum = (
        loss_sum
        + jnp.sum(jax.nn.softplus(cycle_logits), axis=1)
        + jnp.sum(jax.nn.softplus(pod_logits), axis=1)
    )
    row_loss = loss_sum / (3.0 * row_count)
    own_coeff = (temper * (jax.nn.sigmoid(own_logits) - positive_mask.astype(jnp.float32))).astype(
        jnp.bfloat16
    )
    cycle_coeff = (temper * jax.nn.sigmoid(cycle_logits)).astype(jnp.bfloat16)
    pod_coeff = (temper * jax.nn.sigmoid(pod_logits)).astype(jnp.bfloat16)
    image_grad = jnp.dot(own_coeff, texts, preferred_element_type=jnp.float32)
    image_grad = image_grad + jnp.dot(cycle_coeff, cycle_text, preferred_element_type=jnp.float32)
    image_grad = image_grad + jnp.dot(pod_coeff, pod_text, preferred_element_type=jnp.float32)
    own_part = text_part(own_coeff, images)
    cycle_part = text_part(cycle_coeff, images)
    pod_part = text_part(pod_coeff, images)
    cycle_home = passed_along(cycle_part, "dp", -1)
    pod_home = passed_along(pod_part, "outer", -1)
    text_grad = (
        own_part.astype(jnp.float32) + cycle_home.astype(jnp.float32) + pod_home.astype(jnp.float32)
    )
    return (row_loss, image_grad.astype(jnp.bfloat16), text_grad.astype(jnp.bfloat16))


def solution(mesh):
    in_specs = (
        P(("dp", "outer"), None),
        P(("dp", "outer"), None),
        P(("dp", "outer"), None),
        P(),
        P(),
    )
    out_specs = (P(("dp", "outer")), P(("dp", "outer"), None), P(("dp", "outer"), None))
    return jax.shard_map(local, mesh=mesh, in_specs=in_specs, out_specs=out_specs, check_vma=False)
```

profile of v0, /device:TPU:1, one launch (start us, length us, event | category | flops | bytes accessed | tf_op | source)
XLA Modules:
  0.0 140.0 jit_solution(10965043205217183066)
XLA Ops:
  0.6 0.0 copy-start
  0.6 4.6 %collective-permute-start.1 = (bf16[448,1152]{1,0:T(8,128)(2,1)}, bf16[448,1152]{1,0:T(8,128)(2,1)S(1)}, u32[]{:S(2)}, u32[]{:S(2)}) collective-permute-start(bf16[448,1152]{1,0:T(8,128)(2,1)} %param.6), channel_id=1, source_target_pairs={{0,1},{1,2},{2,3},{3,4},{4,5},{5,6},{6,7},{7,8},{8,9},{9,10},{10,1... | collective-permute-start | bytes 3096584 | tf_op jit(solution)/shard_map/ppermute | solution.py:9
  5.3 7.5 %collective-permute-start = (bf16[448,1152]{1,0:T(8,128)(2,1)}, bf16[448,1152]{1,0:T(8,128)(2,1)S(1)}, u32[]{:S(2)}, u32[]{:S(2)}) collective-permute-start(bf16[448,1152]{1,0:T(8,128)(2,1)} %param.6), channel_id=1, source_target_pairs={{0,32},{32,64},{64,96},{96,128},{128,160},{160,192},{192,224},{224... | collective-permute-start | bytes 3096584 | tf_op jit(solution)/shard_map/ppermute | solution.py:9
  14.1 0.0 copy-done
  14.1 2.6 %fusion.10 = (f32[448]{0:T(512)S(1)}, f32[448,448]{0,1:T(8,128)S(1)}) fusion(s32[448]{0:T(512)} %bitcast.18, f32[]{:T(128)} %bitcast.15, bf16[448,1152]{1,0:T(8,128)(2,1)S(1)} %copy-done, bf16[448,1152]{1,0:T(8,128)(2,1)} %param.6, f32[]{:T(128)} %bitcast.1), kind=kOutput, calls=%fused_computation.24 | convolution fusion | flops 465030720 | bytes 2870792 | tf_op jit(solution)/shard_map/dot_general | solution.py:13
  16.7 0.5 collective-permute-done.1
  17.2 1.2 fusion.12
  18.4 0.9 convolution_convert_fusion
  19.3 34.9 %collective-permute-start.3 = (bf16[448,1152]{1,0:T(8,128)(2,1)S(1)}, bf16[448,1152]{1,0:T(8,128)(2,1)S(1)}, u32[]{:S(2)}, u32[]{:S(2)}) collective-permute-start(bf16[448,1152]{1,0:T(8,128)(2,1)S(1)} %convolution_convert_fusion), channel_id=1, source_target_pairs={{0,31},{1,0},{2,1},{3,2},{4,3},{5,4},{6,5},{7,6},{8,7},{9,8},{10,9... | collective-permute-start | bytes 3096584 | tf_op jit(solution)/shard_map/ppermute | solution.py:9
  54.1 14.1 %collective-permute-done = bf16[448,1152]{1,0:T(8,128)(2,1)S(1)} collective-permute-done((bf16[448,1152]{1,0:T(8,128)(2,1)}, bf16[448,1152]{1,0:T(8,128)(2,1)S(1)}, u32[]{:S(2)}, u32[]{:S(2)}) %collective-permute-start) | collective-permute-done | bytes 1032224 | tf_op jit(solution)/shard_map/ppermute | solution.py:9
  68.2 1.2 fusion.11
  69.4 0.0 copy-start.1
  69.4 0.0 copy-start.2
  69.5 0.9 convolution_convert_fusion.1
  70.3 25.6 %collective-permute-start.2 = (bf16[448,1152]{1,0:T(8,128)(2,1)S(1)}, bf16[448,1152]{1,0:T(8,128)(2,1)S(1)}, u32[]{:S(2)}, u32[]{:S(2)}) collective-permute-start(bf16[448,1152]{1,0:T(8,128)(2,1)S(1)} %convolution_convert_fusion.1), channel_id=1, source_target_pairs={{0,736},{32,0},{64,32},{96,64},{128,96},{160,128},{192,160},{224,1... | collective-permute-start | bytes 3096584 | tf_op jit(solution)/shard_map/ppermute | solution.py:9
  95.9 0.0 copy-done.1
  95.9 0.0 copy-done.2
  96.0 0.8 fusion.15
  96.8 0.6 add_multiply_fusion
  97.4 0.8 convolution_add_fusion.1
  98.2 1.8 %fusion = bf16[448,1152]{1,0:T(8,128)(2,1)} fusion(f32[448,1152]{1,0:T(8,128)S(1)} %convolution_add_fusion.1, bf16[448,1152]{1,0:T(8,128)(2,1)S(1)} %collective-permute-done.1, f32[448,448]{0,1:T(8,128)S(1)} %get-tuple-element.4, f32[]{:T(128)} %bitcast.1), kind=kOutput, calls=%fused_computation.2 | convolution fusion | flops 464457728 | bytes 4931588 | tf_op jit(solution)/shard_map/dot_general | solution.py:53
  100.0 0.0 collective-permute-done.3
  100.0 38.1 %collective-permute-done.2 = bf16[448,1152]{1,0:T(8,128)(2,1)S(1)} collective-permute-done((bf16[448,1152]{1,0:T(8,128)(2,1)S(1)}, bf16[448,1152]{1,0:T(8,128)(2,1)S(1)}, u32[]{:S(2)}, u32[]{:S(2)}) %collective-permute-start.2) | collective-permute-done | bytes 1032224 | tf_op jit(solution)/shard_map/ppermute | solution.py:9
  138.1 1.8 %add_convert_fusion = bf16[448,1152]{1,0:T(8,128)(2,1)} fusion(bf16[448,1152]{1,0:T(8,128)(2,1)S(1)} %collective-permute-done.3, bf16[448,1152]{1,0:T(8,128)(2,1)S(1)} %collective-permute-done.2, bf16[448,1152]{1,0:T(8,128)(2,1)S(1)} %copy-done, f32[448,448]{0,1:T(8,128)S(1)} %get-tuple-element.6, f32[]{:T(128)} %bitcast.1, s32[448]{0:T(512)S(1)} %bitcast.20), kind=kOutput, calls=%fused_computation.10 | convolution fusion | flops 467640320 | bytes 4933380 | tf_op jit(solution)/shard_map/dot_general | solution.py:20
Async XLA Ops:
  0.6 13.5 %copy-start = (bf16[448,1152]{1,0:T(8,128)(2,1)S(1)}, bf16[448,1152]{1,0:T(8,128)(2,1)}, u32[]{:S(2)}) copy-start(bf16[448,1152]{1,0:T(8,128)(2,1)} %param.5) | copy-start | bytes 3096580
  0.6 16.5 %collective-permute-start.1 = (bf16[448,1152]{1,0:T(8,128)(2,1)}, bf16[448,1152]{1,0:T(8,128)(2,1)S(1)}, u32[]{:S(2)}, u32[]{:S(2)}) collective-permute-start(bf16[448,1152]{1,0:T(8,128)(2,1)} %param.6), channel_id=1, source_target_pairs={{0,1},{1,2},{2,3},{3,4},{4,5},{5,6},{6,7},{7,8},{8,9},{9,10},{10,1... | collective-permute-start | bytes 3096584 | tf_op jit(solution)/shard_map/ppermute | solution.py:9
  5.3 62.9 %collective-permute-start = (bf16[448,1152]{1,0:T(8,128)(2,1)}, bf16[448,1152]{1,0:T(8,128)(2,1)S(1)}, u32[]{:S(2)}, u32[]{:S(2)}) collective-permute-start(bf16[448,1152]{1,0:T(8,128)(2,1)} %param.6), channel_id=1, source_target_pairs={{0,32},{32,64},{64,96},{96,128},{128,160},{160,192},{192,224},{224... | collective-permute-start | bytes 3096584 | tf_op jit(solution)/shard_map/ppermute | solution.py:9
  19.3 80.8 %collective-permute-start.3 = (bf16[448,1152]{1,0:T(8,128)(2,1)S(1)}, bf16[448,1152]{1,0:T(8,128)(2,1)S(1)}, u32[]{:S(2)}, u32[]{:S(2)}) collective-permute-start(bf16[448,1152]{1,0:T(8,128)(2,1)S(1)} %convolution_convert_fusion), channel_id=1, source_target_pairs={{0,31},{1,0},{2,1},{3,2},{4,3},{5,4},{6,5},{7,6},{8,7},{9,8},{10,9... | collective-permute-start | bytes 3096584 | tf_op jit(solution)/shard_map/ppermute | solution.py:9
  69.4 26.5 %copy-start.1 = (bf16[448,1152]{1,0:T(8,128)(2,1)S(1)}, bf16[448,1152]{1,0:T(8,128)(2,1)}, u32[]{:S(2)}) copy-start(bf16[448,1152]{1,0:T(8,128)(2,1)} %param.6) | copy-start | bytes 3096580
  69.4 26.5 %copy-start.2 = (s32[1,448]{1,0:T(1,128)S(1)}, s32[1,448]{1,0:T(1,128)}, u32[]{:S(2)}) copy-start(s32[1,448]{1,0:T(1,128)} %param.7) | copy-start | bytes 5380
  70.3 67.8 %collective-permute-start.2 = (bf16[448,1152]{1,0:T(8,128)(2,1)S(1)}, bf16[448,1152]{1,0:T(8,128)(2,1)S(1)}, u32[]{:S(2)}, u32[]{:S(2)}) collective-permute-start(bf16[448,1152]{1,0:T(8,128)(2,1)S(1)} %convolution_convert_fusion.1), channel_id=1, source_target_pairs={{0,736},{32,0},{64,32},{96,64},{128,96},{160,128},{192,160},{224,1... | collective-permute-start | bytes 3096584 | tf_op jit(solution)/shard_map/ppermute | solution.py:9
where the time goes:
time: 140 us
  starting transfers between devices  72.6 us (52%)
  waiting for transfers between devices  52.6 us (38%)
  matrix products  12.1 us (9%)
  between operations  2.07 us (1%)
    ppermute x4, starting transfers between devices, passed_along(): lax.ppermute(x, axis, [(i, (i + by) % devices) for i in range(devices)])  72.6 us
    ppermute x4, waiting for transfers between devices, passed_along(): lax.ppermute(x, axis, [(i, (i + by) % devices) for i in range(devices)])  52.6 us
    dot_general x3, matrix products, logit_tile(): lax.dot_general(left, right, (((1,), (1,)), ((), ())), preferred_element_...  5.07 us
    dot_general x3, matrix products, text_part(): lax.dot_general(coeff, image_rows, (((0,), (0,)), ((), ())), preferred_el...  3.56 us
  transfers between devices with their start and end apart: 4, of which 3 were waited for; matrix products, arithmetic and copies ran while one was open for 8% of the time, Pallas kernels for 0%

commit v1 on v0

v1 whole, which is shorter than its diff:
```python
import jax
import jax.numpy as jnp
from jax import lax
from jax.sharding import PartitionSpec as P


def passed_along(x, axis, by):
    devices = lax.axis_size(axis)
    return lax.ppermute(x, axis, [(i, (i + by) % devices) for i in range(devices)])


def logit_tile(left, right, temper, offset_b):
    product = lax.dot_general(
        left, right, (((1,), (1,)), ((), ())), preferred_element_type=jnp.float32
    )
    return temper * product + offset_b


def text_part(coeff, image_rows):
    product = lax.dot_general(
        coeff, image_rows, (((0,), (0,)), ((), ())), preferred_element_type=jnp.float32
    )
    return product.astype(jnp.bfloat16).astype(jnp.float32)


def far_text_part(images, texts, temper, offset_b):
    logits = logit_tile(images, texts, temper, offset_b)
    coeff = (temper * jax.nn.sigmoid(logits)).astype(jnp.bfloat16)
    return text_part(coeff, images)


def near_terms(images, texts, temper, offset_b):
    logits = logit_tile(images, texts, temper, offset_b)
    loss = jnp.sum(jax.nn.softplus(logits), axis=1)
    coeff = (temper * jax.nn.sigmoid(logits)).astype(jnp.bfloat16)
    return loss, jnp.dot(coeff, texts, preferred_element_type=jnp.float32)


def local(images, texts, positive_index, log_scale, bias):
    temper = jnp.exp(log_scale[0])
    offset_b = bias[0]
    row_count = images.shape[0]
    cycle_text = passed_along(texts, "dp", 1)
    cycle_images = passed_along(images, "dp", -1)
    pod_text = passed_along(texts, "outer", 1)
    pod_images = passed_along(images, "outer", -1)

    positive_mask = positive_index[0][:, None] == lax.broadcasted_iota(
        jnp.int32, (row_count, row_count), 1
    )
    own_logits = logit_tile(images, texts, temper, offset_b)
    signed = jnp.where(positive_mask, own_logits, -own_logits)
    loss_sum = jnp.sum(jax.nn.softplus(-signed), axis=1)
    own_coeff = (temper * (jax.nn.sigmoid(own_logits) - positive_mask.astype(jnp.float32))).astype(
        jnp.bfloat16
    )
    image_grad = jnp.dot(own_coeff, texts, preferred_element_type=jnp.float32)
    text_grad = text_part(own_coeff, images)

    pod_loss, pod_grad = near_terms(images, pod_text, temper, offset_b)
    text_grad = text_grad + far_text_part(pod_images, texts, temper, offset_b)
    cycle_loss, cycle_grad = near_terms(images, cycle_text, temper, offset_b)
    text_grad = text_grad + far_text_part(cycle_images, texts, temper, offset_b)
    row_loss = (loss_sum + pod_loss + cycle_loss) / (3.0 * row_count)
    image_grad = image_grad + pod_grad + cycle_grad
    return (row_loss, image_grad.astype(jnp.bfloat16), text_grad.astype(jnp.bfloat16))


def solution(mesh):
    in_specs = (
        P(("dp", "outer"), None),
        P(("dp", "outer"), None),
        P(("dp", "outer"), None),
        P(),
        P(),
    )
    out_specs = (P(("dp", "outer")), P(("dp", "outer"), None), P(("dp", "outer"), None))
    return jax.shard_map(local, mesh=mesh, in_specs=in_specs, out_specs=out_specs, check_vma=False)
```

time: 140 us -> 127 us (0.907)
  the two profiles are of different devices: /device:TPU:1 before, /device:TPU:63 now
where the time goes in v1:
time: 127 us
  waiting for transfers between devices  83.9 us (66%)
  matrix products  20.4 us (16%)
  starting transfers between devices  19.6 us (15%)
  between operations  2.05 us (2%)
    ppermute x4, waiting for transfers between devices, passed_along(): lax.ppermute(x, axis, [(i, (i + by) % devices) for i in range(devices)])  83.9 us
    ppermute x4, starting transfers between devices, passed_along(): lax.ppermute(x, axis, [(i, (i + by) % devices) for i in range(devices)])  19.6 us
    dot_general x3, matrix products, text_part(): lax.dot_general(coeff, image_rows, (((0,), (0,)), ((), ())), preferred_el...  11.4 us
    dot_general x3, matrix products, logit_tile(): lax.dot_general(left, right, (((1,), (1,)), ((), ())), preferred_element_...  5.47 us
    dot_general x2, matrix products, near_terms(): return (loss, jnp.dot(coeff, texts, preferred_element_type=jnp.float32))  2.64 us
  transfers between devices with their start and end apart: 4, of which 2 were waited for; matrix products, arithmetic and copies ran while one was open for 13% of the time, Pallas kernels for 0%

profile of v1, /device:TPU:63, one launch (start us, length us, event | category | flops | bytes accessed | tf_op | source)
XLA Modules:
  0.0 126.6 jit_solution(5796440912891456363)
XLA Ops:
  0.6 5.0 %collective-permute-start = (bf16[448,1152]{1,0:T(8,128)(2,1)}, bf16[448,1152]{1,0:T(8,128)(2,1)S(1)}, u32[]{:S(2)}, u32[]{:S(2)}) collective-permute-start(bf16[448,1152]{1,0:T(8,128)(2,1)} %param.6), channel_id=1, source_target_pairs={{0,1},{1,2},{2,3},{3,4},{4,5},{5,6},{6,7},{7,8},{8,9},{9,10},{10,1... | collective-permute-start | bytes 3096584 | tf_op jit(solution)/shard_map/ppermute | solution.py:9
  5.7 3.5 %collective-permute-start.1 = (bf16[448,1152]{1,0:T(8,128)(2,1)}, bf16[448,1152]{1,0:T(8,128)(2,1)S(1)}, u32[]{:S(2)}, u32[]{:S(2)}) collective-permute-start(bf16[448,1152]{1,0:T(8,128)(2,1)} %param.6), channel_id=1, source_target_pairs={{0,32},{32,64},{64,96},{96,128},{128,160},{160,192},{192,224},{224... | collective-permute-start | bytes 3096584 | tf_op jit(solution)/shard_map/ppermute | solution.py:9
  9.2 2.5 %collective-permute-start.2 = (bf16[448,1152]{1,0:T(8,128)(2,1)}, bf16[448,1152]{1,0:T(8,128)(2,1)}, u32[]{:S(2)}, u32[]{:S(2)}) collective-permute-start(bf16[448,1152]{1,0:T(8,128)(2,1)} %param.5), channel_id=1, source_target_pairs={{0,31},{1,0},{2,1},{3,2},{4,3},{5,4},{6,5},{7,6},{8,7},{9,8},{10,9... | collective-permute-start | bytes 3096584 | tf_op jit(solution)/shard_map/ppermute | solution.py:9
  11.7 8.6 %collective-permute-start.3 = (bf16[448,1152]{1,0:T(8,128)(2,1)}, bf16[448,1152]{1,0:T(8,128)(2,1)S(1)}, u32[]{:S(2)}, u32[]{:S(2)}) collective-permute-start(bf16[448,1152]{1,0:T(8,128)(2,1)} %param.5), channel_id=1, source_target_pairs={{0,736},{32,0},{64,32},{96,64},{128,96},{160,128},{192,160},{224,1... | collective-permute-start | bytes 3096584 | tf_op jit(solution)/shard_map/ppermute | solution.py:9
  21.6 0.0 copy-start
  21.6 0.0 copy-start.2
  21.6 3.0 %fusion.29 = (f32[448]{0:T(512)S(1)}, f32[448,448]{0,1:T(8,128)S(1)}) fusion(s32[448]{0:T(512)} %bitcast.24, f32[]{:T(128)} %bitcast.19, bf16[448,1152]{1,0:T(8,128)(2,1)} %param.5, bf16[448,1152]{1,0:T(8,128)(2,1)} %param.6, f32[]{:T(128)} %bitcast.1), kind=kOutput, calls=%fused_computation.44 | convolution fusion | flops 465030720 | bytes 2870792 | tf_op jit(solution)/shard_map/dot_general | solution.py:13
  24.6 0.0 copy-done
  24.6 0.0 copy-done.2
  24.6 0.0 copy-start.1
  24.7 2.3 %fusion.6 = f32[448,1152]{1,0:T(8,128)} fusion(bf16[448,1152]{1,0:T(8,128)(2,1)S(1)} %copy-done, f32[448,448]{0,1:T(8,128)S(1)} %get-tuple-element.6, f32[]{:T(128)} %bitcast.1, s32[448]{0:T(512)S(1)} %bitcast.25), kind=kOutput, calls=%fused_computation.11 | convolution fusion | flops 465059840 | bytes 3901188 | tf_op jit(solution)/shard_map/dot_general | solution.py:20
  26.9 0.0 copy-done.1
  26.9 0.8 fusion.48
  27.8 37.3 %collective-permute-done = bf16[448,1152]{1,0:T(8,128)(2,1)S(1)} collective-permute-done((bf16[448,1152]{1,0:T(8,128)(2,1)}, bf16[448,1152]{1,0:T(8,128)(2,1)S(1)}, u32[]{:S(2)}, u32[]{:S(2)}) %collective-permute-start) | collective-permute-done | bytes 1032224 | tf_op jit(solution)/shard_map/ppermute | solution.py:9
  65.1 1.2 fusion.30
  66.3 46.6 %collective-permute-done.1 = bf16[448,1152]{1,0:T(8,128)(2,1)S(1)} collective-permute-done((bf16[448,1152]{1,0:T(8,128)(2,1)}, bf16[448,1152]{1,0:T(8,128)(2,1)S(1)}, u32[]{:S(2)}, u32[]{:S(2)}) %collective-permute-start.1) | collective-permute-done | bytes 1032224 | tf_op jit(solution)/shard_map/ppermute | solution.py:9
  112.9 1.2 fusion.31
  114.2 0.8 convolution_add_fusion.1
  115.0 0.6 add_multiply_fusion
  115.6 1.8 %fusion = bf16[448,1152]{1,0:T(8,128)(2,1)} fusion(f32[448,1152]{1,0:T(8,128)S(1)} %convolution_add_fusion.1, bf16[448,1152]{1,0:T(8,128)(2,1)S(1)} %collective-permute-done.1, f32[448,448]{0,1:T(8,128)S(1)} %get-tuple-element.4, f32[]{:T(128)} %bitcast.1), kind=kOutput, calls=%fused_computation.2 | convolution fusion | flops 464457728 | bytes 4931588 | tf_op jit(solution)/shard_map/dot_general | solution.py:36
  117.4 0.0 collective-permute-done.2
  117.4 5.1 %fusion.5 = f32[448,1152]{1,0:T(8,128)} fusion(f32[448,1152]{1,0:T(8,128)} %fusion.6, bf16[448,1152]{1,0:T(8,128)(2,1)} %collective-permute-done.2, bf16[448,1152]{1,0:T(8,128)(2,1)S(1)} %copy-done.1, f32[]{:T(128)} %bitcast.21, f32[]{:T(128)} %bitcast.1), kind=kOutput, calls=%fused_computation.9 | convolution fusion | flops 927797248 | bytes 6193160 | tf_op jit(solution)/shard_map/dot_general | solution.py:20
  122.5 0.0 collective-permute-done.3
  122.5 4.1 %fusion.3 = bf16[448,1152]{1,0:T(8,128)(2,1)} fusion(f32[448,1152]{1,0:T(8,128)} %fusion.5, bf16[448,1152]{1,0:T(8,128)(2,1)S(1)} %collective-permute-done.3, bf16[448,1152]{1,0:T(8,128)(2,1)S(1)} %copy-done.1, f32[]{:T(128)} %bitcast.20, f32[]{:T(128)} %bitcast.1), kind=kOutput, calls=%fused_computation.6 | convolution fusion | flops 928313344 | bytes 5160968 | tf_op jit(solution)/shard_map/dot_general | solution.py:20
Async XLA Ops:
  0.6 64.5 %collective-permute-start = (bf16[448,1152]{1,0:T(8,128)(2,1)}, bf16[448,1152]{1,0:T(8,128)(2,1)S(1)}, u32[]{:S(2)}, u32[]{:S(2)}) collective-permute-start(bf16[448,1152]{1,0:T(8,128)(2,1)} %param.6), channel_id=1, source_target_pairs={{0,1},{1,2},{2,3},{3,4},{4,5},{5,6},{6,7},{7,8},{8,9},{9,10},{10,1... | collective-permute-start | bytes 3096584 | tf_op jit(solution)/shard_map/ppermute | solution.py:9
  5.7 107.3 %collective-permute-start.1 = (bf16[448,1152]{1,0:T(8,128)(2,1)}, bf16[448,1152]{1,0:T(8,128)(2,1)S(1)}, u32[]{:S(2)}, u32[]{:S(2)}) collective-permute-start(bf16[448,1152]{1,0:T(8,128)(2,1)} %param.6), channel_id=1, source_target_pairs={{0,32},{32,64},{64,96},{96,128},{128,160},{160,192},{192,224},{224... | collective-permute-start | bytes 3096584 | tf_op jit(solution)/shard_map/ppermute | solution.py:9
  9.2 108.2 %collective-permute-start.2 = (bf16[448,1152]{1,0:T(8,128)(2,1)}, bf16[448,1152]{1,0:T(8,128)(2,1)}, u32[]{:S(2)}, u32[]{:S(2)}) collective-permute-start(bf16[448,1152]{1,0:T(8,128)(2,1)} %param.5), channel_id=1, source_target_pairs={{0,31},{1,0},{2,1},{3,2},{4,3},{5,4},{6,5},{7,6},{8,7},{9,8},{10,9... | collective-permute-start | bytes 3096584 | tf_op jit(solution)/shard_map/ppermute | solution.py:9
  11.7 110.8 %collective-permute-start.3 = (bf16[448,1152]{1,0:T(8,128)(2,1)}, bf16[448,1152]{1,0:T(8,128)(2,1)S(1)}, u32[]{:S(2)}, u32[]{:S(2)}) collective-permute-start(bf16[448,1152]{1,0:T(8,128)(2,1)} %param.5), channel_id=1, source_target_pairs={{0,736},{32,0},{64,32},{96,64},{128,96},{160,128},{192,160},{224,1... | collective-permute-start | bytes 3096584 | tf_op jit(solution)/shard_map/ppermute | solution.py:9
  21.6 3.0 %copy-start = (bf16[448,1152]{1,0:T(8,128)(2,1)S(1)}, bf16[448,1152]{1,0:T(8,128)(2,1)}, u32[]{:S(2)}) copy-start(bf16[448,1152]{1,0:T(8,128)(2,1)} %param.5) | copy-start | bytes 3096580
  21.6 3.0 %copy-start.2 = (s32[1,448]{1,0:T(1,128)S(1)}, s32[1,448]{1,0:T(1,128)}, u32[]{:S(2)}) copy-start(s32[1,448]{1,0:T(1,128)} %param.7) | copy-start | bytes 5380
  24.6 2.3 %copy-start.1 = (bf16[448,1152]{1,0:T(8,128)(2,1)S(1)}, bf16[448,1152]{1,0:T(8,128)(2,1)}, u32[]{:S(2)}) copy-start(bf16[448,1152]{1,0:T(8,128)(2,1)} %param.6) | copy-start | bytes 3096580

commit v2 on v1

v2 whole, which is shorter than its diff:
```python
import jax
import jax.numpy as jnp
from jax import lax
from jax.experimental import pallas as pl
from jax.experimental.pallas import tpu as pltpu
from jax.sharding import PartitionSpec as P

VMEM = pl.BlockSpec(memory_space=pltpu.VMEM)
SMEM = pl.BlockSpec(memory_space=pltpu.SMEM)
F32 = jnp.float32
BF16 = jnp.bfloat16


def passed_along(x, axis, by):
    devices = lax.axis_size(axis)
    return lax.ppermute(x, axis, [(i, (i + by) % devices) for i in range(devices)])


def nt(left, right):
    return lax.dot_general(left, right, (((1,), (1,)), ((), ())), preferred_element_type=F32)


def tn(left, right):
    return lax.dot_general(left, right, (((0,), (0,)), ((), ())), preferred_element_type=F32)


def nn(left, right):
    return lax.dot_general(left, right, (((1,), (0,)), ((), ())), preferred_element_type=F32)


def tile_logits(scal, texts, images):
    return scal[0] * nt(texts, images) + scal[1]


def small(logits):
    return jnp.exp(-jnp.abs(logits))


def sigmoid(logits, e):
    return jnp.where(logits >= 0.0, 1.0, e) / (1.0 + e)


def softplus(v, e):
    return jnp.maximum(v, 0.0) + jnp.log1p(e)


def negative_tile(scal, texts, images, with_loss):
    logits = tile_logits(scal, texts, images)
    e = small(logits)
    coeff = (scal[0] * sigmoid(logits, e)).astype(BF16)
    if not with_loss:
        return coeff
    return coeff, jnp.sum(softplus(logits, e), axis=0, keepdims=True)


def own_kernel(scal, pos_ref, images_ref, texts_ref, loss_ref, igrad_ref, tgrad_ref):
    images, texts = images_ref[...], texts_ref[...]
    logits = tile_logits(scal, texts, images)
    mask = pos_ref[...] == lax.broadcasted_iota(jnp.int32, logits.shape, 0)
    e = small(logits)
    loss_ref[...] = jnp.sum(
        softplus(jnp.where(mask, -logits, logits), e), axis=0, keepdims=True
    )
    coeff = (scal[0] * (sigmoid(logits, e) - jnp.where(mask, 1.0, 0.0))).astype(BF16)
    igrad_ref[...] = tn(coeff, texts)
    tgrad_ref[...] = nn(coeff, images)


def middle_kernel(
    scal, images_ref, texts_ref, far_texts_ref, far_images_ref, loss_in, igrad_in, tgrad_in,
    loss_ref, igrad_ref, tgrad_ref,
):
    far_texts, far_images = far_texts_ref[...], far_images_ref[...]
    coeff, loss = negative_tile(scal, far_texts, images_ref[...], True)
    loss_ref[...] = loss_in[...] + loss
    igrad_ref[...] = igrad_in[...] + tn(coeff, far_texts)
    coeff = negative_tile(scal, texts_ref[...], far_images, False)
    tgrad_ref[...] = tgrad_in[...] + nn(coeff, far_images)


def last_image_kernel(scal, images_ref, far_texts_ref, loss_in, igrad_in, loss_ref, igrad_ref):
    far_texts = far_texts_ref[...]
    coeff, loss = negative_tile(scal, far_texts, images_ref[...], True)
    loss_ref[...] = loss_in[...] + loss
    igrad_ref[...] = (igrad_in[...] + tn(coeff, far_texts)).astype(BF16)


def last_text_kernel(scal, texts_ref, far_images_ref, loss_in, tgrad_in, loss_ref, tgrad_ref):
    loss_ref[...] = loss_in[...] / (3.0 * loss_in.shape[1])
    far_images = far_images_ref[...]
    coeff = negative_tile(scal, texts_ref[...], far_images, False)
    tgrad_ref[...] = (tgrad_in[...] + nn(coeff, far_images)).astype(BF16)


def call(kernel, outs, *args):
    return pl.pallas_call(
        kernel,
        out_shape=outs,
        in_specs=[SMEM] + [VMEM] * (len(args) - 1),
        out_specs=[VMEM] * len(outs),
        compiler_params=pltpu.CompilerParams(vmem_limit_bytes=40 * 1024 * 1024),
        cost_estimate=pl.CostEstimate(flops=1000, bytes_accessed=1000, transcendentals=0),
    )(*args)


def local(images, texts, positive_index, log_scale, bias):
    rows, width = images.shape
    cut = rows // 2
    scal = jnp.concatenate([jnp.exp(log_scale), bias])
    cycle_text = passed_along(texts, "dp", 1)
    cycle_images = passed_along(images, "dp", -1)
    pod_text = [passed_along(t, "outer", 1) for t in (texts[:cut], texts[cut:])]
    pod_images = [passed_along(i, "outer", -1) for i in (images[:cut], images[cut:])]

    loss_shape = jax.ShapeDtypeStruct((1, rows), F32)
    wide = jax.ShapeDtypeStruct((rows, width), F32)
    narrow = jax.ShapeDtypeStruct((rows, width), BF16)
    sums = call(own_kernel, [loss_shape, wide, wide], scal, positive_index, images, texts)
    for far in zip(pod_text, pod_images):
        sums = call(middle_kernel, [loss_shape, wide, wide], scal, images, texts, *far, *sums)
    loss, igrad, tgrad = sums
    loss, igrad = call(
        last_image_kernel, [loss_shape, narrow], scal, images, cycle_text, loss, igrad
    )
    loss, tgrad = call(
        last_text_kernel, [loss_shape, narrow], scal, texts, cycle_images, loss, tgrad
    )
    return loss.reshape(rows), igrad, tgrad


def solution(mesh):
    in_specs = (
        P(("dp", "outer"), None),
        P(("dp", "outer"), None),
        P(("dp", "outer"), None),
        P(),
        P(),
    )
    out_specs = (P(("dp", "outer")), P(("dp", "outer"), None), P(("dp", "outer"), None))
    return jax.shard_map(local, mesh=mesh, in_specs=in_specs, out_specs=out_specs, check_vma=False)
```

time: 127 us -> 128 us (level)
  the two profiles are of different devices: /device:TPU:63 before, /device:TPU:201 now
where the time goes in v2:
time: 128 us
  starting transfers between devices  108 us (84%)
  Pallas kernels  16.1 us (13%)
  between operations  2.11 us (2%)
  local copies, waits for them, and re-layouts  1.37 us (1%)
    ppermute x6, starting transfers between devices, passed_along(): lax.ppermute(x, axis, [(i, (i + by) % devices) for i in range(devices)])  108 us
    pallas_call x5, Pallas kernels, call(): pl.pallas_call(kernel, out_shape=outs, in_specs=[SMEM] + [VMEM] * (len(ar...  16.1 us
  transfers between devices with their start and end apart: 6, of which 0 were waited for; matrix products, arithmetic and copies ran while one was open for 1% of the time, Pallas kernels for 10%

profile of v2, /device:TPU:201, one launch (start us, length us, event | category | flops | bytes accessed | tf_op | source)
XLA Modules:
  0.0 128.1 jit_solution(4846215957820025744)
XLA Ops:
  0.6 0.0 copy-start.1
  0.6 0.0 copy-start
  0.7 0.0 copy-start.2
  0.7 6.7 %collective-permute-start.1 = (bf16[448,1152]{1,0:T(8,128)(2,1)}, bf16[448,1152]{1,0:T(8,128)(2,1)S(1)}, u32[]{:S(2)}, u32[]{:S(2)}) collective-permute-start(bf16[448,1152]{1,0:T(8,128)(2,1)} %texts_ref.7), channel_id=1, source_target_pairs={{0,32},{32,64},{64,96},{96,128},{128,160},{160,192},{192,224},{224... | collective-permute-start | bytes 3096584 | tf_op jit(solution)/shard_map/ppermute | solution.py:16
  7.4 1.3 fusion.1
  8.6 4.0 %collective-permute-start.4 = (bf16[224,1152]{1,0:T(8,128)(2,1)S(1)}, bf16[224,1152]{1,0:T(8,128)(2,1)S(1)}, u32[]{:S(2)}, u32[]{:S(2)}) collective-permute-start(bf16[224,1152]{1,0:T(8,128)(2,1)S(1)} %get-tuple-element.31), channel_id=1, source_target_pairs={{0,1},{1,2},{2,3},{3,4},{4,5},{5,6},{6,7},{7,8},{8,9},{9,10},{10,1... | collective-permute-start | bytes 1548296 | tf_op jit(solution)/shard_map/ppermute | solution.py:16
  12.6 0.0 copy-done
  12.6 3.5 %collective-permute-start = (bf16[448,1152]{1,0:T(8,128)(2,1)S(1)}, bf16[448,1152]{1,0:T(8,128)(2,1)S(1)}, u32[]{:S(2)}, u32[]{:S(2)}) collective-permute-start(bf16[448,1152]{1,0:T(8,128)(2,1)S(1)} %copy-done), channel_id=1, source_target_pairs={{0,736},{32,0},{64,32},{96,64},{128,96},{160,128},{192,160},{224,1... | collective-permute-start | bytes 3096584 | tf_op jit(solution)/shard_map/ppermute | solution.py:16
  16.2 0.1 fusion
  16.2 1.9 %collective-permute-start.5 = (bf16[224,1152]{1,0:T(8,128)(2,1)S(1)}, bf16[224,1152]{1,0:T(8,128)(2,1)S(1)}, u32[]{:S(2)}, u32[]{:S(2)}) collective-permute-start(bf16[224,1152]{1,0:T(8,128)(2,1)S(1)} %get-tuple-element.29), channel_id=1, source_target_pairs={{0,31},{1,0},{2,1},{3,2},{4,3},{5,4},{6,5},{7,6},{8,7},{9,8},{10,9... | collective-permute-start | bytes 1548296 | tf_op jit(solution)/shard_map/ppermute | solution.py:16
  18.2 3.6 %collective-permute-start.2 = (bf16[224,1152]{1,0:T(8,128)(2,1)S(1)}, bf16[224,1152]{1,0:T(8,128)(2,1)S(1)}, u32[]{:S(2)}, u32[]{:S(2)}) collective-permute-start(bf16[224,1152]{1,0:T(8,128)(2,1)S(1)} %get-tuple-element.32), channel_id=1, source_target_pairs={{0,1},{1,2},{2,3},{3,4},{4,5},{5,6},{6,7},{7,8},{8,9},{9,10},{10,1... | collective-permute-start | bytes 1548296 | tf_op jit(solution)/shard_map/ppermute | solution.py:16
  21.8 0.0 collective-permute-done.4.far_texts_ref
  21.8 88.6 %collective-permute-start.3 = (bf16[224,1152]{1,0:T(8,128)(2,1)S(1)}, bf16[224,1152]{1,0:T(8,128)(2,1)S(1)}, u32[]{:S(2)}, u32[]{:S(2)}) collective-permute-start(bf16[224,1152]{1,0:T(8,128)(2,1)S(1)} %get-tuple-element.30), channel_id=1, source_target_pairs={{0,31},{1,0},{2,1},{3,2},{4,3},{5,4},{6,5},{7,6},{8,7},{9,8},{10,9... | collective-permute-start | bytes 1548296 | tf_op jit(solution)/shard_map/ppermute | solution.py:16
  111.8 0.1 pad_maximum_fusion.scal
  111.9 0.0 copy-done.1
  111.9 0.0 copy-done.2
  111.9 3.4 %shard_map.76 = (f32[1,448]{1,0:T(1,128)S(1)}, f32[448,1152]{1,0:T(8,128)S(1)}, f32[448,1152]{1,0:T(8,128)S(1)}) custom-call(f32[2]{0:T(128)S(1)} %pad_maximum_fusion.scal, s32[1,448]{1,0:T(1,128)S(1)} %copy-done.2, bf16[448,1152]{1,0:T(8,128)(2,1)S(1)} %copy-done, bf16[448,1152]{1,0:T(8,128)(2,1)S(1)} %copy-done.1), custom_call_target="tpu_custom_call" | custom-call | flops 1000 | bytes 1000 | tf_op jit(solution)/shard_map/pallas_call | solution.py:96
  115.3 0.0 collective-permute-done.5.far_images_ref
  115.3 3.0 %shard_map.77 = (f32[1,448]{1,0:T(1,128)S(1)}, f32[448,1152]{1,0:T(8,128)S(1)}, f32[448,1152]{1,0:T(8,128)S(1)}) custom-call(f32[2]{0:T(128)S(1)} %pad_maximum_fusion.scal, bf16[448,1152]{1,0:T(8,128)(2,1)S(1)} %copy-done, bf16[448,1152]{1,0:T(8,128)(2,1)S(1)} %copy-done.1, bf16[224,1152]{1,0:T(8,128)(2,1)S(1)} %collective-permute-done.4.far_texts_ref, ...), custom_call_target="tpu_custom_call" | custom-call | flops 1000 | bytes 1000 | tf_op jit(solution)/shard_map/pallas_call | solution.py:96
  118.3 0.0 collective-permute-done.2.far_texts_ref
  118.3 0.0 collective-permute-done.3.far_images_ref
  118.3 3.0 %shard_map.78 = (f32[1,448]{1,0:T(1,128)S(1)}, f32[448,1152]{1,0:T(8,128)S(1)}, f32[448,1152]{1,0:T(8,128)S(1)}) custom-call(f32[2]{0:T(128)S(1)} %pad_maximum_fusion.scal, bf16[448,1152]{1,0:T(8,128)(2,1)S(1)} %copy-done, bf16[448,1152]{1,0:T(8,128)(2,1)S(1)} %copy-done.1, bf16[224,1152]{1,0:T(8,128)(2,1)S(1)} %collective-permute-done.2.far_texts_ref, ...), custom_call_target="tpu_custom_call" | custom-call | flops 1000 | bytes 1000 | tf_op jit(solution)/shard_map/pallas_call | solution.py:96
  121.4 0.0 collective-permute-done.1.far_texts_ref
  121.4 3.6 %shard_map.79 = (f32[1,448]{1,0:T(1,128)S(1)}, bf16[448,1152]{1,0:T(8,128)(2,1)}) custom-call(f32[2]{0:T(128)S(1)} %pad_maximum_fusion.scal, bf16[448,1152]{1,0:T(8,128)(2,1)S(1)} %copy-done, bf16[448,1152]{1,0:T(8,128)(2,1)S(1)} %collective-permute-done.1.far_texts_ref, f32[1,448]{1,0:T(1,128)S(1)} %get-tuple-element.22.loss_in, ...), custom_call_target="tpu_custom_call" | custom-call | flops 1000 | bytes 1000 | tf_op jit(solution)/shard_map/pallas_call | solution.py:96
  124.9 0.0 collective-permute-done.far_images_ref
  124.9 3.2 %shard_map.80 = (f32[1,448]{1,0:T(1,128)}, bf16[448,1152]{1,0:T(8,128)(2,1)}) custom-call(f32[2]{0:T(128)S(1)} %pad_maximum_fusion.scal, bf16[448,1152]{1,0:T(8,128)(2,1)S(1)} %copy-done.1, bf16[448,1152]{1,0:T(8,128)(2,1)S(1)} %collective-permute-done.far_images_ref, f32[1,448]{1,0:T(1,128)S(1)} %get-tuple-element.24.loss_in, ...), custom_call_target="tpu_custom_call" | custom-call | flops 1000 | bytes 1000 | tf_op jit(solution)/shard_map/pallas_call | solution.py:96
Async XLA Ops:
  0.6 111.3 %copy-start.1 = (bf16[448,1152]{1,0:T(8,128)(2,1)S(1)}, bf16[448,1152]{1,0:T(8,128)(2,1)}, u32[]{:S(2)}) copy-start(bf16[448,1152]{1,0:T(8,128)(2,1)} %texts_ref.7) | copy-start | bytes 3096580
  0.6 12.0 %copy-start = (bf16[448,1152]{1,0:T(8,128)(2,1)S(1)}, bf16[448,1152]{1,0:T(8,128)(2,1)}, u32[]{:S(2)}) copy-start(bf16[448,1152]{1,0:T(8,128)(2,1)} %images_ref.7) | copy-start | bytes 3096580
  0.7 111.2 %copy-start.2 = (s32[1,448]{1,0:T(1,128)S(1)}, s32[1,448]{1,0:T(1,128)}, u32[]{:S(2)}) copy-start(s32[1,448]{1,0:T(1,128)} %pos_ref.1) | copy-start | bytes 5380
  0.7 120.7 %collective-permute-start.1 = (bf16[448,1152]{1,0:T(8,128)(2,1)}, bf16[448,1152]{1,0:T(8,128)(2,1)S(1)}, u32[]{:S(2)}, u32[]{:S(2)}) collective-permute-start(bf16[448,1152]{1,0:T(8,128)(2,1)} %texts_ref.7), channel_id=1, source_target_pairs={{0,32},{32,64},{64,96},{96,128},{128,160},{160,192},{192,224},{224... | collective-permute-start | bytes 3096584 | tf_op jit(solution)/shard_map/ppermute | solution.py:16
  8.6 13.2 %collective-permute-start.4 = (bf16[224,1152]{1,0:T(8,128)(2,1)S(1)}, bf16[224,1152]{1,0:T(8,128)(2,1)S(1)}, u32[]{:S(2)}, u32[]{:S(2)}) collective-permute-start(bf16[224,1152]{1,0:T(8,128)(2,1)S(1)} %get-tuple-element.31), channel_id=1, source_target_pairs={{0,1},{1,2},{2,3},{3,4},{4,5},{5,6},{6,7},{7,8},{8,9},{9,10},{10,1... | collective-permute-start | bytes 1548296 | tf_op jit(solution)/shard_map/ppermute | solution.py:16
  12.6 112.3 %collective-permute-start = (bf16[448,1152]{1,0:T(8,128)(2,1)S(1)}, bf16[448,1152]{1,0:T(8,128)(2,1)S(1)}, u32[]{:S(2)}, u32[]{:S(2)}) collective-permute-start(bf16[448,1152]{1,0:T(8,128)(2,1)S(1)} %copy-done), channel_id=1, source_target_pairs={{0,736},{32,0},{64,32},{96,64},{128,96},{160,128},{192,160},{224,1... | collective-permute-start | bytes 3096584 | tf_op jit(solution)/shard_map/ppermute | solution.py:16
  16.2 99.1 %collective-permute-start.5 = (bf16[224,1152]{1,0:T(8,128)(2,1)S(1)}, bf16[224,1152]{1,0:T(8,128)(2,1)S(1)}, u32[]{:S(2)}, u32[]{:S(2)}) collective-permute-start(bf16[224,1152]{1,0:T(8,128)(2,1)S(1)} %get-tuple-element.29), channel_id=1, source_target_pairs={{0,31},{1,0},{2,1},{3,2},{4,3},{5,4},{6,5},{7,6},{8,7},{9,8},{10,9... | collective-permute-start | bytes 1548296 | tf_op jit(solution)/shard_map/ppermute | solution.py:16
  18.2 100.2 %collective-permute-start.2 = (bf16[224,1152]{1,0:T(8,128)(2,1)S(1)}, bf16[224,1152]{1,0:T(8,128)(2,1)S(1)}, u32[]{:S(2)}, u32[]{:S(2)}) collective-permute-start(bf16[224,1152]{1,0:T(8,128)(2,1)S(1)} %get-tuple-element.32), channel_id=1, source_target_pairs={{0,1},{1,2},{2,3},{3,4},{4,5},{5,6},{6,7},{7,8},{8,9},{9,10},{10,1... | collective-permute-start | bytes 1548296 | tf_op jit(solution)/shard_map/ppermute | solution.py:16
  21.8 96.5 %collective-permute-start.3 = (bf16[224,1152]{1,0:T(8,128)(2,1)S(1)}, bf16[224,1152]{1,0:T(8,128)(2,1)S(1)}, u32[]{:S(2)}, u32[]{:S(2)}) collective-permute-start(bf16[224,1152]{1,0:T(8,128)(2,1)S(1)} %get-tuple-element.30), channel_id=1, source_target_pairs={{0,31},{1,0},{2,1},{3,2},{4,3},{5,4},{6,5},{7,6},{8,7},{9,8},{10,9... | collective-permute-start | bytes 1548296 | tf_op jit(solution)/shard_map/ppermute | solution.py:16

commit v3 on v2

v3 whole, which is shorter than its diff:
```python
import jax
import jax.numpy as jnp
from jax import lax
from jax.experimental import pallas as pl
from jax.experimental.pallas import tpu as pltpu
from jax.sharding import PartitionSpec as P

VMEM = pl.BlockSpec(memory_space=pltpu.VMEM)
SMEM = pl.BlockSpec(memory_space=pltpu.SMEM)
F32 = jnp.float32
BF16 = jnp.bfloat16


def passed_along(x, axis, by):
    devices = lax.axis_size(axis)
    return lax.ppermute(x, axis, [(i, (i + by) % devices) for i in range(devices)])


def nt(left, right):
    return lax.dot_general(left, right, (((1,), (1,)), ((), ())), preferred_element_type=F32)


def tn(left, right):
    return lax.dot_general(left, right, (((0,), (0,)), ((), ())), preferred_element_type=F32)


def nn(left, right):
    return lax.dot_general(left, right, (((1,), (0,)), ((), ())), preferred_element_type=F32)


def tile_logits(scal, texts, images):
    return scal[0] * nt(texts, images) + scal[1]


def small(logits):
    return jnp.exp(-jnp.abs(logits))


def sigmoid(logits, e):
    return jnp.where(logits >= 0.0, 1.0, e) / (1.0 + e)


def softplus(v, e):
    return jnp.maximum(v, 0.0) + jnp.log1p(e)


def image_side(scal, images, far_texts):
    logits = tile_logits(scal, far_texts, images)
    e = small(logits)
    coeff = (scal[0] * sigmoid(logits, e)).astype(BF16)
    return jnp.sum(softplus(logits, e), axis=0, keepdims=True), tn(coeff, far_texts)


def text_side(scal, texts, far_images):
    logits = tile_logits(scal, texts, far_images)
    coeff = (scal[0] * sigmoid(logits, small(logits))).astype(BF16)
    return nn(coeff, far_images)


def own_kernel(scal, pos_ref, images_ref, texts_ref, loss_ref, igrad_ref, tgrad_ref):
    images, texts = images_ref[...], texts_ref[...]
    logits = tile_logits(scal, texts, images)
    mask = pos_ref[...] == lax.broadcasted_iota(jnp.int32, logits.shape, 0)
    e = small(logits)
    loss_ref[...] = jnp.sum(
        softplus(jnp.where(mask, -logits, logits), e), axis=0, keepdims=True
    )
    coeff = (scal[0] * (sigmoid(logits, e) - jnp.where(mask, 1.0, 0.0))).astype(BF16)
    igrad_ref[...] = tn(coeff, texts)
    tgrad_ref[...] = nn(coeff, images)


def outer_kernel(
    scal, flags, images_ref, texts_ref, far_texts_ref, far_images_ref, loss_in, igrad_in, tgrad_in,
    loss_ref, igrad_ref, tgrad_ref,
):
    loss_ref[...] = loss_in[...]
    igrad_ref[...] = igrad_in[...]
    tgrad_ref[...] = tgrad_in[...]

    @pl.when(flags[0] == 0)
    def _():
        loss, grad = image_side(scal, images_ref[...], far_texts_ref[...])
        loss_ref[...] += loss
        igrad_ref[...] += grad

    @pl.when(flags[1] == 0)
    def _():
        tgrad_ref[...] += text_side(scal, texts_ref[...], far_images_ref[...])


def dp_image_kernel(
    scal, images_ref, far_texts_ref, loss_in, igrad_in, loss_ref, igrad_ref
):
    loss, grad = image_side(scal, images_ref[...], far_texts_ref[...])
    loss_ref[...] = loss_in[...] + loss
    igrad_ref[...] = igrad_in[...] + grad


def dp_text_kernel(scal, texts_ref, far_images_ref, loss_in, tgrad_in, loss_ref, tgrad_ref):
    loss_ref[...] = loss_in[...]
    tgrad_ref[...] = tgrad_in[...] + text_side(scal, texts_ref[...], far_images_ref[...])


def last_kernel(
    scal, flags, images_ref, texts_ref, cross_ref, loss_in, igrad_in, tgrad_in,
    loss_ref, igrad_ref, tgrad_ref,
):
    count = 3.0 * loss_in.shape[1]

    @pl.when(flags[0] == 0)
    def _():
        loss_ref[...] = loss_in[...] / count
        igrad_ref[...] = igrad_in[...].astype(BF16)

    @pl.when(flags[0] != 0)
    def _():
        loss, grad = image_side(scal, images_ref[...], cross_ref[...])
        loss_ref[...] = (loss_in[...] + loss) / count
        igrad_ref[...] = (igrad_in[...] + grad).astype(BF16)

    @pl.when(flags[1] == 0)
    def _():
        tgrad_ref[...] = tgrad_in[...].astype(BF16)

    @pl.when(flags[1] != 0)
    def _():
        tgrad_ref[...] = (
            tgrad_in[...] + text_side(scal, texts_ref[...], cross_ref[...])
        ).astype(BF16)


def call(kernel, outs, scalars, *args):
    return pl.pallas_call(
        kernel,
        out_shape=outs,
        in_specs=[SMEM] * len(scalars) + [VMEM] * len(args),
        out_specs=[VMEM] * len(outs),
        compiler_params=pltpu.CompilerParams(vmem_limit_bytes=40 * 1024 * 1024),
        cost_estimate=pl.CostEstimate(flops=1000, bytes_accessed=1000, transcendentals=0),
    )(*scalars, *args)


ROW = 8


def local(images, texts, positive_index, log_scale, bias):
    rows, width = images.shape
    outer = lax.axis_size("outer")
    here = lax.axis_index("outer")
    scal = jnp.concatenate([jnp.exp(log_scale), bias])
    first, last = here % ROW == 0, here % ROW == ROW - 1
    flags = jnp.stack([first, last]).astype(jnp.int32)

    def step(x, pairs):
        return lax.ppermute(x, "outer", pairs)

    ahead = [(o, (o + 1) % outer) for o in range(outer)]
    crossing = [(a, b) for a, b in ahead if b % ROW == 0]
    within = [(a, b) for a, b in ahead if b % ROW != 0]
    cycle_text = passed_along(texts, "dp", 1)
    cycle_images = passed_along(images, "dp", -1)
    cross = step(jnp.where(first, images, texts), crossing + [(b, a) for a, b in crossing])
    pod_text = step(texts, within)
    pod_images = step(images, [(b, a) for a, b in within])

    loss_shape = jax.ShapeDtypeStruct((1, rows), F32)
    wide = jax.ShapeDtypeStruct((rows, width), F32)
    narrow = jax.ShapeDtypeStruct((rows, width), BF16)
    loss, igrad, tgrad = call(
        own_kernel, [loss_shape, wide, wide], [scal], positive_index, images, texts
    )
    loss, igrad, tgrad = call(
        outer_kernel, [loss_shape, wide, wide], [scal, flags],
        images, texts, pod_text, pod_images, loss, igrad, tgrad,
    )
    loss, igrad = call(
        dp_image_kernel, [loss_shape, wide], [scal], images, cycle_text, loss, igrad
    )
    loss, tgrad = call(
        dp_text_kernel, [loss_shape, wide], [scal], texts, cycle_images, loss, tgrad
    )
    loss, igrad, tgrad = call(
        last_kernel, [loss_shape, narrow, narrow], [scal, flags],
        images, texts, cross, loss, igrad, tgrad,
    )
    return loss.reshape(rows), igrad, tgrad


def solution(mesh):
    in_specs = (
        P(("dp", "outer"), None),
        P(("dp", "outer"), None),
        P(("dp", "outer"), None),
        P(),
        P(),
    )
    out_specs = (P(("dp", "outer")), P(("dp", "outer"), None), P(("dp", "outer"), None))
    return jax.shard_map(local, mesh=mesh, in_specs=in_specs, out_specs=out_specs, check_vma=False)
```

time: 128 us -> 127 us (level)
  the two profiles are of different devices: /device:TPU:201 before, /device:TPU:32 now
where the time goes in v3:
time: 127 us; the launch traced here: 126 us
  waiting for transfers between devices  79 us (62%)
  starting transfers between devices  19.5 us (15%)
  Pallas kernels  17.4 us (14%)
  local copies, waits for them, and re-layouts  5.8 us (5%)
  other arithmetic  2.48 us (2%)
  between operations  2.09 us (2%)
    ppermute x2, waiting for transfers between devices, passed_along(): lax.ppermute(x, axis, [(i, (i + by) % devices) for i in range(devices)])  65.2 us
    pallas_call x5, Pallas kernels, call(): pl.pallas_call(kernel, out_shape=outs, in_specs=[SMEM] * len(scalars) + [...  17.4 us
    ppermute x3, waiting for transfers between devices, step(): return lax.ppermute(x, 'outer', pairs)  13.9 us
    ppermute x2, starting transfers between devices, passed_along(): lax.ppermute(x, axis, [(i, (i + by) % devices) for i in range(devices)])  12.5 us
    ppermute x3, starting transfers between devices, step(): return lax.ppermute(x, 'outer', pairs)  7.01 us
    unnamed x14, local copies, waits for them, and re-layouts  5.8 us
  transfers between devices with their start and end apart: 5, of which 2 were waited for; matrix products, arithmetic and copies ran while one was open for 2% of the time, Pallas kernels for 10%

profile of v3, /device:TPU:32, one launch (start us, length us, event | category | flops | bytes accessed | tf_op | source)
XLA Modules:
  0.0 126.3 jit_solution(10631849455055674597)
XLA Ops:
  0.6 0.0 copy-start.1
  0.6 0.0 copy-start
  0.7 0.0 copy-start.6
  0.7 1.9 %collective-permute-start.3 = (bf16[448,1152]{1,0:T(8,128)(2,1)}, bf16[448,1152]{1,0:T(8,128)(2,1)S(1)}, u32[]{:S(2)}, u32[]{:S(2)}) collective-permute-start(bf16[448,1152]{1,0:T(8,128)(2,1)} %texts_ref.7), channel_id=1, source_target_pairs={{0,1},{1,2},{2,3},{3,4},{4,5},{5,6},{6,7},{8,9},{9,10},{10,11},{11... | collective-permute-start | bytes 3096584 | tf_op jit(solution)/shard_map/ppermute | solution.py:156
  2.6 3.8 %collective-permute-start.2 = (bf16[448,1152]{1,0:T(8,128)(2,1)}, bf16[448,1152]{1,0:T(8,128)(2,1)}, u32[]{:S(2)}, u32[]{:S(2)}) collective-permute-start(bf16[448,1152]{1,0:T(8,128)(2,1)} %texts_ref.7), channel_id=1, source_target_pairs={{0,32},{32,64},{64,96},{96,128},{128,160},{160,192},{192,224},{224... | collective-permute-start | bytes 3096584 | tf_op jit(solution)/shard_map/ppermute | solution.py:16
  6.4 1.3 %collective-permute-start.4 = (bf16[448,1152]{1,0:T(8,128)(2,1)}, bf16[448,1152]{1,0:T(8,128)(2,1)}, u32[]{:S(2)}, u32[]{:S(2)}) collective-permute-start(bf16[448,1152]{1,0:T(8,128)(2,1)} %images_ref.7), channel_id=1, source_target_pairs={{1,0},{2,1},{3,2},{4,3},{5,4},{6,5},{7,6},{9,8},{10,9},{11,10},{12... | collective-permute-start | bytes 3096584 | tf_op jit(solution)/shard_map/ppermute | solution.py:156
  7.7 8.7 %collective-permute-start.1 = (bf16[448,1152]{1,0:T(8,128)(2,1)}, bf16[448,1152]{1,0:T(8,128)(2,1)}, u32[]{:S(2)}, u32[]{:S(2)}) collective-permute-start(bf16[448,1152]{1,0:T(8,128)(2,1)} %images_ref.7), channel_id=1, source_target_pairs={{0,736},{32,0},{64,32},{96,64},{128,96},{160,128},{192,160},{224,1... | collective-permute-start | bytes 3096584 | tf_op jit(solution)/shard_map/ppermute | solution.py:16
  16.4 2.3 %broadcast_select_fusion = bf16[448,1152]{1,0:T(8,128)(2,1)} fusion(bf16[448,1152]{1,0:T(8,128)(2,1)} %images_ref.7, bf16[448,1152]{1,0:T(8,128)(2,1)} %texts_ref.7, pred[]{:T(512)} %eq.9), kind=kLoop, calls=%fused_computation | loop fusion | flops 516096 | bytes 3096577 | tf_op jit(solution)/shard_map/jit(_where)/select_n | solution.py:163
  18.8 3.8 %collective-permute-start = (bf16[448,1152]{1,0:T(8,128)(2,1)}, bf16[448,1152]{1,0:T(8,128)(2,1)}, u32[]{:S(2)}, u32[]{:S(2)}) collective-permute-start(bf16[448,1152]{1,0:T(8,128)(2,1)} %broadcast_select_fusion), channel_id=1, source_target_pairs={{7,8},{15,16},{23,24},{31,0},{8,7},{16,15},{24,23},{0,31},{39,40},... | collective-permute-start | bytes 3096584 | tf_op jit(solution)/shard_map/ppermute | solution.py:156
  23.9 0.1 pad_maximum_fusion.scal
  24.0 0.0 copy-done.1
  24.0 0.0 copy-done
  24.0 0.0 copy-done.6
  24.0 3.4 %shard_map.76 = (f32[1,448]{1,0:T(1,128)S(1)}, f32[448,1152]{1,0:T(8,128)S(1)}, f32[448,1152]{1,0:T(8,128)S(1)}) custom-call(f32[2]{0:T(128)S(1)} %pad_maximum_fusion.scal, s32[1,448]{1,0:T(1,128)S(1)} %copy-done.6, bf16[448,1152]{1,0:T(8,128)(2,1)S(1)} %copy-done, bf16[448,1152]{1,0:T(8,128)(2,1)S(1)} %copy-done.1), custom_call_target="tpu_custom_call" | custom-call | flops 1000 | bytes 1000 | tf_op jit(solution)/shard_map/pallas_call | solution.py:134
  27.4 0.0 copy-start.2
  27.4 1.3 %copy-done.2 = f32[448,1152]{1,0:T(8,128)} copy-done((f32[448,1152]{1,0:T(8,128)}, f32[448,1152]{1,0:T(8,128)S(1)}, u32[]{:S(2)}) %copy-start.2) | copy-done | bytes 2064408
  28.7 0.0 copy-start.4
  28.7 1.3 %copy-done.4 = f32[448,1152]{1,0:T(8,128)} copy-done((f32[448,1152]{1,0:T(8,128)}, f32[448,1152]{1,0:T(8,128)S(1)}, u32[]{:S(2)}) %copy-start.4) | copy-done | bytes 2064408
  30.0 0.1 add_convert_fusion.flags
  30.1 0.0 collective-permute-done.3.far_texts_ref
  30.1 0.0 collective-permute-done.4.far_images_ref
  30.1 0.0 copy-start.3
  30.1 1.6 %copy-done.3 = f32[448,1152]{1,0:T(8,128)S(1)} copy-done((f32[448,1152]{1,0:T(8,128)S(1)}, f32[448,1152]{1,0:T(8,128)}, u32[]{:S(2)}) %copy-start.3) | copy-done | bytes 2064408
  31.7 0.0 copy-start.5
  31.7 1.6 %copy-done.5 = f32[448,1152]{1,0:T(8,128)S(1)} copy-done((f32[448,1152]{1,0:T(8,128)S(1)}, f32[448,1152]{1,0:T(8,128)}, u32[]{:S(2)}) %copy-start.5) | copy-done | bytes 2064408
  33.3 3.1 %shard_map.77 = (f32[1,448]{1,0:T(1,128)S(1)}, f32[448,1152]{1,0:T(8,128)S(1)}, f32[448,1152]{1,0:T(8,128)S(1)}) custom-call(f32[2]{0:T(128)S(1)} %pad_maximum_fusion.scal, s32[2]{0:T(128)S(1)} %add_convert_fusion.flags, bf16[448,1152]{1,0:T(8,128)(2,1)S(1)} %copy-done, bf16[448,1152]{1,0:T(8,128)(2,1)S(1)} %copy-done.1, ...), custom_call_target="tpu_custom_call" | custom-call | flops 1000 | bytes 1000 | tf_op jit(solution)/shard_map/pallas_call | solution.py:134
  36.4 65.2 %collective-permute-done.2.far_texts_ref = bf16[448,1152]{1,0:T(8,128)(2,1)} collective-permute-done((bf16[448,1152]{1,0:T(8,128)(2,1)}, bf16[448,1152]{1,0:T(8,128)(2,1)}, u32[]{:S(2)}, u32[]{:S(2)}) %collective-permute-start.2) | collective-permute-done | bytes 1032224 | tf_op jit(solution)/shard_map/ppermute | solution.py:16
  101.6 3.3 %shard_map.78 = (f32[1,448]{1,0:T(1,128)S(1)}, f32[448,1152]{1,0:T(8,128)S(1)}) custom-call(f32[2]{0:T(128)S(1)} %pad_maximum_fusion.scal, bf16[448,1152]{1,0:T(8,128)(2,1)S(1)} %copy-done, bf16[448,1152]{1,0:T(8,128)(2,1)} %collective-permute-done.2.far_texts_ref, f32[1,448]{1,0:T(1,128)S(1)} %get-tuple-element.19.loss_in, ...), custom_call_target="tpu_custom_call" | custom-call | flops 1000 | bytes 1000 | tf_op jit(solution)/shard_map/pallas_call | solution.py:134
  104.8 0.0 collective-permute-done.1.far_images_ref
  104.8 2.9 %shard_map.79 = (f32[1,448]{1,0:T(1,128)S(1)}, f32[448,1152]{1,0:T(8,128)S(1)}) custom-call(f32[2]{0:T(128)S(1)} %pad_maximum_fusion.scal, bf16[448,1152]{1,0:T(8,128)(2,1)S(1)} %copy-done.1, bf16[448,1152]{1,0:T(8,128)(2,1)} %collective-permute-done.1.far_images_ref, f32[1,448]{1,0:T(1,128)S(1)} %get-tuple-element.21.loss_in, ...), custom_call_target="tpu_custom_call" | custom-call | flops 1000 | bytes 1000 | tf_op jit(solution)/shard_map/pallas_call | solution.py:134
  107.7 13.9 %collective-permute-done.cross_ref = bf16[448,1152]{1,0:T(8,128)(2,1)} collective-permute-done((bf16[448,1152]{1,0:T(8,128)(2,1)}, bf16[448,1152]{1,0:T(8,128)(2,1)}, u32[]{:S(2)}, u32[]{:S(2)}) %collective-permute-start) | collective-permute-done | bytes 1032224 | tf_op jit(solution)/shard_map/ppermute | solution.py:156
  121.6 4.7 %shard_map.80 = (f32[1,448]{1,0:T(1,128)}, bf16[448,1152]{1,0:T(8,128)(2,1)}, bf16[448,1152]{1,0:T(8,128)(2,1)}) custom-call(f32[2]{0:T(128)S(1)} %pad_maximum_fusion.scal, s32[2]{0:T(128)S(1)} %add_convert_fusion.flags, bf16[448,1152]{1,0:T(8,128)(2,1)S(1)} %copy-done, bf16[448,1152]{1,0:T(8,128)(2,1)S(1)} %copy-done.1, ...), custom_call_target="tpu_custom_call" | custom-call | flops 1000 | bytes 1000 | tf_op jit(solution)/shard_map/pallas_call | solution.py:134
Async XLA Ops:
  0.6 23.3 %copy-start.1 = (bf16[448,1152]{1,0:T(8,128)(2,1)S(1)}, bf16[448,1152]{1,0:T(8,128)(2,1)}, u32[]{:S(2)}) copy-start(bf16[448,1152]{1,0:T(8,128)(2,1)} %texts_ref.7) | copy-start | bytes 3096580
  0.6 23.3 %copy-start = (bf16[448,1152]{1,0:T(8,128)(2,1)S(1)}, bf16[448,1152]{1,0:T(8,128)(2,1)}, u32[]{:S(2)}) copy-start(bf16[448,1152]{1,0:T(8,128)(2,1)} %images_ref.7) | copy-start | bytes 3096580
  0.7 23.3 %copy-start.6 = (s32[1,448]{1,0:T(1,128)S(1)}, s32[1,448]{1,0:T(1,128)}, u32[]{:S(2)}) copy-start(s32[1,448]{1,0:T(1,128)} %pos_ref.1) | copy-start | bytes 5380
  0.7 29.4 %collective-permute-start.3 = (bf16[448,1152]{1,0:T(8,128)(2,1)}, bf16[448,1152]{1,0:T(8,128)(2,1)S(1)}, u32[]{:S(2)}, u32[]{:S(2)}) collective-permute-start(bf16[448,1152]{1,0:T(8,128)(2,1)} %texts_ref.7), channel_id=1, source_target_pairs={{0,1},{1,2},{2,3},{3,4},{4,5},{5,6},{6,7},{8,9},{9,10},{10,11},{11... | collective-permute-start | bytes 3096584 | tf_op jit(solution)/shard_map/ppermute | solution.py:156
  2.6 98.9 %collective-permute-start.2 = (bf16[448,1152]{1,0:T(8,128)(2,1)}, bf16[448,1152]{1,0:T(8,128)(2,1)}, u32[]{:S(2)}, u32[]{:S(2)}) collective-permute-start(bf16[448,1152]{1,0:T(8,128)(2,1)} %texts_ref.7), channel_id=1, source_target_pairs={{0,32},{32,64},{64,96},{96,128},{128,160},{160,192},{192,224},{224... | collective-permute-start | bytes 3096584 | tf_op jit(solution)/shard_map/ppermute | solution.py:16
  6.4 23.7 %collective-permute-start.4 = (bf16[448,1152]{1,0:T(8,128)(2,1)}, bf16[448,1152]{1,0:T(8,128)(2,1)}, u32[]{:S(2)}, u32[]{:S(2)}) collective-permute-start(bf16[448,1152]{1,0:T(8,128)(2,1)} %images_ref.7), channel_id=1, source_target_pairs={{1,0},{2,1},{3,2},{4,3},{5,4},{6,5},{7,6},{9,8},{10,9},{11,10},{12... | collective-permute-start | bytes 3096584 | tf_op jit(solution)/shard_map/ppermute | solution.py:156
  7.7 97.1 %collective-permute-start.1 = (bf16[448,1152]{1,0:T(8,128)(2,1)}, bf16[448,1152]{1,0:T(8,128)(2,1)}, u32[]{:S(2)}, u32[]{:S(2)}) collective-permute-start(bf16[448,1152]{1,0:T(8,128)(2,1)} %images_ref.7), channel_id=1, source_target_pairs={{0,736},{32,0},{64,32},{96,64},{128,96},{160,128},{192,160},{224,1... | collective-permute-start | bytes 3096584 | tf_op jit(solution)/shard_map/ppermute | solution.py:16
  18.8 102.8 %collective-permute-start = (bf16[448,1152]{1,0:T(8,128)(2,1)}, bf16[448,1152]{1,0:T(8,128)(2,1)}, u32[]{:S(2)}, u32[]{:S(2)}) collective-permute-start(bf16[448,1152]{1,0:T(8,128)(2,1)} %broadcast_select_fusion), channel_id=1, source_target_pairs={{7,8},{15,16},{23,24},{31,0},{8,7},{16,15},{24,23},{0,31},{39,40},... | collective-permute-start | bytes 3096584 | tf_op jit(solution)/shard_map/ppermute | solution.py:156
  27.4 1.3 %copy-start.2 = (f32[448,1152]{1,0:T(8,128)}, f32[448,1152]{1,0:T(8,128)S(1)}, u32[]{:S(2)}) copy-start(f32[448,1152]{1,0:T(8,128)S(1)} %get-tuple-element.17.igrad_in) | copy-start | bytes 6193156
  28.7 1.3 %copy-start.4 = (f32[448,1152]{1,0:T(8,128)}, f32[448,1152]{1,0:T(8,128)S(1)}, u32[]{:S(2)}) copy-start(f32[448,1152]{1,0:T(8,128)S(1)} %get-tuple-element.18.tgrad_in) | copy-start | bytes 6193156
  30.1 1.6 %copy-start.3 = (f32[448,1152]{1,0:T(8,128)S(1)}, f32[448,1152]{1,0:T(8,128)}, u32[]{:S(2)}) copy-start(f32[448,1152]{1,0:T(8,128)} %copy-done.2) | copy-start | bytes 6193156
  31.7 1.6 %copy-start.5 = (f32[448,1152]{1,0:T(8,128)S(1)}, f32[448,1152]{1,0:T(8,128)}, u32[]{:S(2)}) copy-start(f32[448,1152]{1,0:T(8,128)} %copy-done.4) | copy-start | bytes 6193156

commit v4 on v3

--- a/solution.py
+++ b/solution.py
@@ -89,22 +89,19 @@
         tgrad_ref[...] += text_side(scal, texts_ref[...], far_images_ref[...])
 
 
-def dp_image_kernel(
-    scal, images_ref, far_texts_ref, loss_in, igrad_in, loss_ref, igrad_ref
+def dp_kernel(
+    scal, images_ref, texts_ref, far_texts_ref, far_images_ref, loss_in, igrad_in, tgrad_in,
+    loss_ref, igrad_ref, tgrad_ref,
 ):
     loss, grad = image_side(scal, images_ref[...], far_texts_ref[...])
     loss_ref[...] = loss_in[...] + loss
     igrad_ref[...] = igrad_in[...] + grad
-
-
-def dp_text_kernel(scal, texts_ref, far_images_ref, loss_in, tgrad_in, loss_ref, tgrad_ref):
-    loss_ref[...] = loss_in[...]
     tgrad_ref[...] = tgrad_in[...] + text_side(scal, texts_ref[...], far_images_ref[...])
 
 
 def last_kernel(
     scal, flags, images_ref, texts_ref, cross_ref, loss_in, igrad_in, tgrad_in,
-    loss_ref, igrad_ref, tgrad_ref,
+    loss_ref, igrad_out, tgrad_out, igrad_ref, tgrad_ref, sems,
 ):
     count = 3.0 * loss_in.shape[1]
 
@@ -119,6 +116,9 @@
         loss_ref[...] = (loss_in[...] + loss) / count
         igrad_ref[...] = (igrad_in[...] + grad).astype(BF16)
 
+    image_copy = pltpu.make_async_copy(igrad_ref, igrad_out, sems.at[0])
+    image_copy.start()
+
     @pl.when(flags[1] == 0)
     def _():
         tgrad_ref[...] = tgrad_in[...].astype(BF16)
@@ -129,13 +129,19 @@
             tgrad_in[...] + text_side(scal, texts_ref[...], cross_ref[...])
         ).astype(BF16)
 
-
-def call(kernel, outs, scalars, *args):
+    text_copy = pltpu.make_async_copy(tgrad_ref, tgrad_out, sems.at[1])
+    text_copy.start()
+    image_copy.wait()
+    text_copy.wait()
+
+
+def call(kernel, outs, scalars, *args, out_specs=None, scratch=()):
     return pl.pallas_call(
         kernel,
         out_shape=outs,
         in_specs=[SMEM] * len(scalars) + [VMEM] * len(args),
-        out_specs=[VMEM] * len(outs),
+        out_specs=out_specs or [VMEM] * len(outs),
+        scratch_shapes=scratch,
         compiler_params=pltpu.CompilerParams(vmem_limit_bytes=40 * 1024 * 1024),
         cost_estimate=pl.CostEstimate(flops=1000, bytes_accessed=1000, transcendentals=0),
     )(*scalars, *args)
@@ -160,9 +166,11 @@
     within = [(a, b) for a, b in ahead if b % ROW != 0]
     cycle_text = passed_along(texts, "dp", 1)
     cycle_images = passed_along(images, "dp", -1)
+    back = [(b, a) for a, b in within]
+    cut = rows // 2
     cross = step(jnp.where(first, images, texts), crossing + [(b, a) for a, b in crossing])
-    pod_text = step(texts, within)
-    pod_images = step(images, [(b, a) for a, b in within])
+    pod_texts = [step(t, within) for t in (texts[:cut], texts[cut:])]
+    pod_images = [step(i, back) for i in (images[:cut], images[cut:])]
 
     loss_shape = jax.ShapeDtypeStruct((1, rows), F32)
     wide = jax.ShapeDtypeStruct((rows, width), F32)
@@ -170,19 +178,22 @@
     loss, igrad, tgrad = call(
         own_kernel, [loss_shape, wide, wide], [scal], positive_index, images, texts
     )
+    for far in zip(pod_texts, pod_images):
+        loss, igrad, tgrad = call(
+            outer_kernel, [loss_shape, wide, wide], [scal, flags],
+            images, texts, *far, loss, igrad, tgrad,
+        )
     loss, igrad, tgrad = call(
-        outer_kernel, [loss_shape, wide, wide], [scal, flags],
-        images, texts, pod_text, pod_images, loss, igrad, tgrad,
-    )
-    loss, igrad = call(
-        dp_image_kernel, [loss_shape, wide], [scal], images, cycle_text, loss, igrad
-    )
-    loss, tgrad = call(
-        dp_text_kernel, [loss_shape, wide], [scal], texts, cycle_images, loss, tgrad
-    )
+        dp_kernel, [loss_shape, wide, wide], [scal],
+        images, texts, cycle_text, cycle_images, loss, igrad, tgrad,
+    )
+    away = pl.BlockSpec(memory_space=pl.ANY)
+    held = pltpu.VMEM((rows, width), BF16)
     loss, igrad, tgrad = call(
         last_kernel, [loss_shape, narrow, narrow], [scal, flags],
         images, texts, cross, loss, igrad, tgrad,
+        out_specs=[VMEM, away, away],
+        scratch=[held, held, pltpu.SemaphoreType.DMA((2,))],
     )
     return loss.reshape(rows), igrad, tgrad
 

time: 127 us -> 125 us (0.984)
  waiting for transfers between devices: 79 us -> 68.9 us
  starting transfers between devices: 19.5 us -> 23.4 us
  local copies, waits for them, and re-layouts: 5.8 us -> 9.11 us
  Pallas kernels: 17.4 us -> 19.4 us
    ppermute x2, waiting for transfers between devices: 65.2 us -> 58.3 us  [passed_along(): lax.ppermute(x, axis, [(i, (i + by) % devices) for i in range(devices)])]
    ppermute x3 -> x5, starting transfers between devices: 7.01 us -> 10.5 us  [step(): return lax.ppermute(x, 'outer', pairs)]
    ppermute x3 -> x5, waiting for transfers between devices: 13.9 us -> 10.6 us  [step(): return lax.ppermute(x, 'outer', pairs)]
    slice x0 -> x2, local copies, waits for them, and re-layouts: none -> 3.3 us  [the longest x1 2.24 us: local(): pod_texts = [step(t, within) for t in (texts[:cut], texts[cut:])]]
    pallas_call x5, Pallas kernels: 17.4 us -> 19.4 us  [call(): pl.pallas_call(kernel, out_shape=outs, in_specs=[SMEM] * len(scalars) + [...]
  transfers between devices with their start and end apart: 5 -> 7, of which waited for: 2 -> 3; matrix products, arithmetic and copies ran while one was open for 2% -> 4% of each run, Pallas kernels for 10% -> 11%
where the time goes in v4:
time: 125 us; the launch traced here: 124 us
  waiting for transfers between devices  68.9 us (55%)
  starting transfers between devices  23.4 us (19%)
  Pallas kernels  19.4 us (16%)
  local copies, waits for them, and re-layouts  9.11 us (7%)
  between operations  2.26 us (2%)
    ppermute x2, waiting for transfers between devices, passed_along(): lax.ppermute(x, axis, [(i, (i + by) % devices) for i in range(devices)])  58.3 us
    pallas_call x5, Pallas kernels, call(): pl.pallas_call(kernel, out_shape=outs, in_specs=[SMEM] * len(scalars) + [...  19.4 us
    ppermute x2, starting transfers between devices, passed_along(): lax.ppermute(x, axis, [(i, (i + by) % devices) for i in range(devices)])  12.9 us
    ppermute x5, waiting for transfers between devices, step(): return lax.ppermute(x, 'outer', pairs)  10.6 us
    ppermute x5, starting transfers between devices, step(): return lax.ppermute(x, 'outer', pairs)  10.5 us
    unnamed x14, local copies, waits for them, and re-layouts  5.81 us
  transfers between devices with their start and end apart: 7, of which 3 were waited for; matrix products, arithmetic and copies ran while one was open for 4% of the time, Pallas kernels for 11%

profile of v4, /device:TPU:32, one launch (start us, length us, event | category | flops | bytes accessed | tf_op | source)
XLA Modules:
  0.0 124.2 jit_solution(7863698925651192827)
XLA Ops:
  0.6 0.0 copy-start.1
  0.6 0.0 copy-start
  0.6 4.0 %collective-permute-start.1 = (bf16[448,1152]{1,0:T(8,128)(2,1)}, bf16[448,1152]{1,0:T(8,128)(2,1)S(1)}, u32[]{:S(2)}, u32[]{:S(2)}) collective-permute-start(bf16[448,1152]{1,0:T(8,128)(2,1)} %texts_ref.9), channel_id=1, source_target_pairs={{0,32},{32,64},{64,96},{96,128},{128,160},{160,192},{192,224},{224... | collective-permute-start | bytes 3096584 | tf_op jit(solution)/shard_map/ppermute | solution.py:16
  4.6 2.2 %fusion.1 = (bf16[224,1152]{1,0:T(8,128)(2,1)}, bf16[224,1152]{1,0:T(8,128)(2,1)}) fusion(bf16[448,1152]{1,0:T(8,128)(2,1)} %texts_ref.9), kind=kLoop, calls=%fused_computation.4 | loop fusion | bytes 2064384 | tf_op jit(solution)/shard_map/slice | solution.py:172
  6.9 2.3 %collective-permute-start.5 = (bf16[224,1152]{1,0:T(8,128)(2,1)}, bf16[224,1152]{1,0:T(8,128)(2,1)}, u32[]{:S(2)}, u32[]{:S(2)}) collective-permute-start(bf16[224,1152]{1,0:T(8,128)(2,1)} %get-tuple-element.35), channel_id=1, source_target_pairs={{0,1},{1,2},{2,3},{3,4},{4,5},{5,6},{6,7},{8,9},{9,10},{10,11},{11... | collective-permute-start | bytes 1548296 | tf_op jit(solution)/shard_map/ppermute | solution.py:162
  9.1 0.0 copy-done
  9.1 8.9 %collective-permute-start.2 = (bf16[448,1152]{1,0:T(8,128)(2,1)S(1)}, bf16[448,1152]{1,0:T(8,128)(2,1)}, u32[]{:S(2)}, u32[]{:S(2)}) collective-permute-start(bf16[448,1152]{1,0:T(8,128)(2,1)S(1)} %copy-done), channel_id=1, source_target_pairs={{0,736},{32,0},{64,32},{96,64},{128,96},{160,128},{192,160},{224,1... | collective-permute-start | bytes 3096584 | tf_op jit(solution)/shard_map/ppermute | solution.py:16
  18.1 1.1 fusion
  19.1 0.0 copy-start.6
  19.1 1.4 %collective-permute-start.6 = (bf16[224,1152]{1,0:T(8,128)(2,1)}, bf16[224,1152]{1,0:T(8,128)(2,1)}, u32[]{:S(2)}, u32[]{:S(2)}) collective-permute-start(bf16[224,1152]{1,0:T(8,128)(2,1)} %get-tuple-element.33), channel_id=1, source_target_pairs={{1,0},{2,1},{3,2},{4,3},{5,4},{6,5},{7,6},{9,8},{10,9},{11,10},{12... | collective-permute-start | bytes 1548296 | tf_op jit(solution)/shard_map/ppermute | solution.py:162
  20.6 0.0 copy-done.1
  20.6 1.1 broadcast_select_fusion
  21.6 3.2 %collective-permute-start = (bf16[448,1152]{1,0:T(8,128)(2,1)}, bf16[448,1152]{1,0:T(8,128)(2,1)}, u32[]{:S(2)}, u32[]{:S(2)}) collective-permute-start(bf16[448,1152]{1,0:T(8,128)(2,1)} %broadcast_select_fusion), channel_id=1, source_target_pairs={{7,8},{15,16},{23,24},{31,0},{8,7},{16,15},{24,23},{0,31},{39,40},... | collective-permute-start | bytes 3096584 | tf_op jit(solution)/shard_map/ppermute | solution.py:162
  24.8 0.0 collective-permute-done.5.far_texts_ref
  24.8 2.3 %collective-permute-start.3 = (bf16[224,1152]{1,0:T(8,128)(2,1)}, bf16[224,1152]{1,0:T(8,128)(2,1)}, u32[]{:S(2)}, u32[]{:S(2)}) collective-permute-start(bf16[224,1152]{1,0:T(8,128)(2,1)} %get-tuple-element.36), channel_id=1, source_target_pairs={{0,1},{1,2},{2,3},{3,4},{4,5},{5,6},{6,7},{8,9},{9,10},{10,11},{11... | collective-permute-start | bytes 1548296 | tf_op jit(solution)/shard_map/ppermute | solution.py:162
  27.2 0.0 collective-permute-done.6.far_images_ref
  27.2 1.3 %collective-permute-start.4 = (bf16[224,1152]{1,0:T(8,128)(2,1)}, bf16[224,1152]{1,0:T(8,128)(2,1)}, u32[]{:S(2)}, u32[]{:S(2)}) collective-permute-start(bf16[224,1152]{1,0:T(8,128)(2,1)} %get-tuple-element.34), channel_id=1, source_target_pairs={{1,0},{2,1},{3,2},{4,3},{5,4},{6,5},{7,6},{9,8},{10,9},{11,10},{12... | collective-permute-start | bytes 1548296 | tf_op jit(solution)/shard_map/ppermute | solution.py:162
  29.8 0.1 pad_maximum_fusion.scal
  29.9 0.0 copy-done.6
  29.9 3.4 %shard_map.76 = (f32[1,448]{1,0:T(1,128)S(1)}, f32[448,1152]{1,0:T(8,128)S(1)}, f32[448,1152]{1,0:T(8,128)S(1)}) custom-call(f32[2]{0:T(128)S(1)} %pad_maximum_fusion.scal, s32[1,448]{1,0:T(1,128)S(1)} %copy-done.6, bf16[448,1152]{1,0:T(8,128)(2,1)S(1)} %copy-done, bf16[448,1152]{1,0:T(8,128)(2,1)S(1)} %copy-done.1), custom_call_target="tpu_custom_call" | custom-call | flops 1000 | bytes 1000 | tf_op jit(solution)/shard_map/pallas_call | solution.py:139
  33.3 0.0 copy-start.2
  33.3 1.3 %copy-done.2 = f32[448,1152]{1,0:T(8,128)} copy-done((f32[448,1152]{1,0:T(8,128)}, f32[448,1152]{1,0:T(8,128)S(1)}, u32[]{:S(2)}) %copy-start.2) | copy-done | bytes 2064408
  34.6 0.0 copy-start.4
  34.6 1.3 %copy-done.4 = f32[448,1152]{1,0:T(8,128)} copy-done((f32[448,1152]{1,0:T(8,128)}, f32[448,1152]{1,0:T(8,128)S(1)}, u32[]{:S(2)}) %copy-start.4) | copy-done | bytes 2064408
  35.9 0.1 add_convert_fusion.flags
  36.0 0.0 copy-start.3
  36.0 1.6 %copy-done.3 = f32[448,1152]{1,0:T(8,128)S(1)} copy-done((f32[448,1152]{1,0:T(8,128)S(1)}, f32[448,1152]{1,0:T(8,128)}, u32[]{:S(2)}) %copy-start.3) | copy-done | bytes 2064408
  37.6 0.0 copy-start.5
  37.6 1.6 %copy-done.5 = f32[448,1152]{1,0:T(8,128)S(1)} copy-done((f32[448,1152]{1,0:T(8,128)S(1)}, f32[448,1152]{1,0:T(8,128)}, u32[]{:S(2)}) %copy-start.5) | copy-done | bytes 2064408
  39.2 2.9 %shard_map.77 = (f32[1,448]{1,0:T(1,128)S(1)}, f32[448,1152]{1,0:T(8,128)S(1)}, f32[448,1152]{1,0:T(8,128)S(1)}) custom-call(f32[2]{0:T(128)S(1)} %pad_maximum_fusion.scal, s32[2]{0:T(128)S(1)} %add_convert_fusion.flags, bf16[448,1152]{1,0:T(8,128)(2,1)S(1)} %copy-done, bf16[448,1152]{1,0:T(8,128)(2,1)S(1)} %copy-done.1, ...), custom_call_target="tpu_custom_call" | custom-call | flops 1000 | bytes 1000 | tf_op jit(solution)/shard_map/pallas_call | solution.py:139
  42.1 0.0 collective-permute-done.3.far_texts_ref
  42.1 0.0 collective-permute-done.4.far_images_ref
  42.1 2.9 %shard_map.78 = (f32[1,448]{1,0:T(1,128)S(1)}, f32[448,1152]{1,0:T(8,128)S(1)}, f32[448,1152]{1,0:T(8,128)S(1)}) custom-call(f32[2]{0:T(128)S(1)} %pad_maximum_fusion.scal, s32[2]{0:T(128)S(1)} %add_convert_fusion.flags, bf16[448,1152]{1,0:T(8,128)(2,1)S(1)} %copy-done, bf16[448,1152]{1,0:T(8,128)(2,1)S(1)} %copy-done.1, ...), custom_call_target="tpu_custom_call" | custom-call | flops 1000 | bytes 1000 | tf_op jit(solution)/shard_map/pallas_call | solution.py:139
  45.0 48.1 %collective-permute-done.1.far_texts_ref = bf16[448,1152]{1,0:T(8,128)(2,1)S(1)} collective-permute-done((bf16[448,1152]{1,0:T(8,128)(2,1)}, bf16[448,1152]{1,0:T(8,128)(2,1)S(1)}, u32[]{:S(2)}, u32[]{:S(2)}) %collective-permute-start.1) | collective-permute-done | bytes 1032224 | tf_op jit(solution)/shard_map/ppermute | solution.py:16
  93.1 10.2 %collective-permute-done.2.far_images_ref = bf16[448,1152]{1,0:T(8,128)(2,1)} collective-permute-done((bf16[448,1152]{1,0:T(8,128)(2,1)S(1)}, bf16[448,1152]{1,0:T(8,128)(2,1)}, u32[]{:S(2)}, u32[]{:S(2)}) %collective-permute-start.2) | collective-permute-done | bytes 1032224 | tf_op jit(solution)/shard_map/ppermute | solution.py:16
  103.4 4.8 %shard_map.79 = (f32[1,448]{1,0:T(1,128)S(1)}, f32[448,1152]{1,0:T(8,128)S(1)}, f32[448,1152]{1,0:T(8,128)S(1)}) custom-call(f32[2]{0:T(128)S(1)} %pad_maximum_fusion.scal, bf16[448,1152]{1,0:T(8,128)(2,1)S(1)} %copy-done, bf16[448,1152]{1,0:T(8,128)(2,1)S(1)} %copy-done.1, bf16[448,1152]{1,0:T(8,128)(2,1)S(1)} %collective-permute-done.1.far_texts_ref, ...), custom_call_target="tpu_custom_call" | custom-call | flops 1000 | bytes 1000 | tf_op jit(solution)/shard_map/pallas_call | solution.py:139
  108.1 10.6 %collective-permute-done.cross_ref = bf16[448,1152]{1,0:T(8,128)(2,1)} collective-permute-done((bf16[448,1152]{1,0:T(8,128)(2,1)}, bf16[448,1152]{1,0:T(8,128)(2,1)}, u32[]{:S(2)}, u32[]{:S(2)}) %collective-permute-start) | collective-permute-done | bytes 1032224 | tf_op jit(solution)/shard_map/ppermute | solution.py:162
  118.7 5.4 %shard_map.80 = (f32[1,448]{1,0:T(1,128)}, bf16[448,1152]{1,0:T(8,128)(2,1)}, bf16[448,1152]{1,0:T(8,128)(2,1)}) custom-call(f32[2]{0:T(128)S(1)} %pad_maximum_fusion.scal, s32[2]{0:T(128)S(1)} %add_convert_fusion.flags, bf16[448,1152]{1,0:T(8,128)(2,1)S(1)} %copy-done, bf16[448,1152]{1,0:T(8,128)(2,1)S(1)} %copy-done.1, ...), custom_call_target="tpu_custom_call" | custom-call | flops 1000 | bytes 1000 | tf_op jit(solution)/shard_map/pallas_call | solution.py:139
Async XLA Ops:
  0.6 19.9 %copy-start.1 = (bf16[448,1152]{1,0:T(8,128)(2,1)S(1)}, bf16[448,1152]{1,0:T(8,128)(2,1)}, u32[]{:S(2)}) copy-start(bf16[448,1152]{1,0:T(8,128)(2,1)} %texts_ref.9) | copy-start | bytes 3096580
  0.6 8.5 %copy-start = (bf16[448,1152]{1,0:T(8,128)(2,1)S(1)}, bf16[448,1152]{1,0:T(8,128)(2,1)}, u32[]{:S(2)}) copy-start(bf16[448,1152]{1,0:T(8,128)(2,1)} %images_ref.9) | copy-start | bytes 3096580
  0.6 92.5 %collective-permute-start.1 = (bf16[448,1152]{1,0:T(8,128)(2,1)}, bf16[448,1152]{1,0:T(8,128)(2,1)S(1)}, u32[]{:S(2)}, u32[]{:S(2)}) collective-permute-start(bf16[448,1152]{1,0:T(8,128)(2,1)} %texts_ref.9), channel_id=1, source_target_pairs={{0,32},{32,64},{64,96},{96,128},{128,160},{160,192},{192,224},{224... | collective-permute-start | bytes 3096584 | tf_op jit(solution)/shard_map/ppermute | solution.py:16
  6.9 18.0 %collective-permute-start.5 = (bf16[224,1152]{1,0:T(8,128)(2,1)}, bf16[224,1152]{1,0:T(8,128)(2,1)}, u32[]{:S(2)}, u32[]{:S(2)}) collective-permute-start(bf16[224,1152]{1,0:T(8,128)(2,1)} %get-tuple-element.35), channel_id=1, source_target_pairs={{0,1},{1,2},{2,3},{3,4},{4,5},{5,6},{6,7},{8,9},{9,10},{10,11},{11... | collective-permute-start | bytes 1548296 | tf_op jit(solution)/shard_map/ppermute | solution.py:162
  9.1 94.2 %collective-permute-start.2 = (bf16[448,1152]{1,0:T(8,128)(2,1)S(1)}, bf16[448,1152]{1,0:T(8,128)(2,1)}, u32[]{:S(2)}, u32[]{:S(2)}) collective-permute-start(bf16[448,1152]{1,0:T(8,128)(2,1)S(1)} %copy-done), channel_id=1, source_target_pairs={{0,736},{32,0},{64,32},{96,64},{128,96},{160,128},{192,160},{224,1... | collective-permute-start | bytes 3096584 | tf_op jit(solution)/shard_map/ppermute | solution.py:16
  19.1 10.8 %copy-start.6 = (s32[1,448]{1,0:T(1,128)S(1)}, s32[1,448]{1,0:T(1,128)}, u32[]{:S(2)}) copy-start(s32[1,448]{1,0:T(1,128)} %pos_ref.1) | copy-start | bytes 5380
  19.1 8.0 %collective-permute-start.6 = (bf16[224,1152]{1,0:T(8,128)(2,1)}, bf16[224,1152]{1,0:T(8,128)(2,1)}, u32[]{:S(2)}, u32[]{:S(2)}) collective-permute-start(bf16[224,1152]{1,0:T(8,128)(2,1)} %get-tuple-element.33), channel_id=1, source_target_pairs={{1,0},{2,1},{3,2},{4,3},{5,4},{6,5},{7,6},{9,8},{10,9},{11,10},{12... | collective-permute-start | bytes 1548296 | tf_op jit(solution)/shard_map/ppermute | solution.py:162
  21.6 97.0 %collective-permute-start = (bf16[448,1152]{1,0:T(8,128)(2,1)}, bf16[448,1152]{1,0:T(8,128)(2,1)}, u32[]{:S(2)}, u32[]{:S(2)}) collective-permute-start(bf16[448,1152]{1,0:T(8,128)(2,1)} %broadcast_select_fusion), channel_id=1, source_target_pairs={{7,8},{15,16},{23,24},{31,0},{8,7},{16,15},{24,23},{0,31},{39,40},... | collective-permute-start | bytes 3096584 | tf_op jit(solution)/shard_map/ppermute | solution.py:162
  24.8 17.2 %collective-permute-start.3 = (bf16[224,1152]{1,0:T(8,128)(2,1)}, bf16[224,1152]{1,0:T(8,128)(2,1)}, u32[]{:S(2)}, u32[]{:S(2)}) collective-permute-start(bf16[224,1152]{1,0:T(8,128)(2,1)} %get-tuple-element.36), channel_id=1, source_target_pairs={{0,1},{1,2},{2,3},{3,4},{4,5},{5,6},{6,7},{8,9},{9,10},{10,11},{11... | collective-permute-start | bytes 1548296 | tf_op jit(solution)/shard_map/ppermute | solution.py:162
  27.2 14.9 %collective-permute-start.4 = (bf16[224,1152]{1,0:T(8,128)(2,1)}, bf16[224,1152]{1,0:T(8,128)(2,1)}, u32[]{:S(2)}, u32[]{:S(2)}) collective-permute-start(bf16[224,1152]{1,0:T(8,128)(2,1)} %get-tuple-element.34), channel_id=1, source_target_pairs={{1,0},{2,1},{3,2},{4,3},{5,4},{6,5},{7,6},{9,8},{10,9},{11,10},{12... | collective-permute-start | bytes 1548296 | tf_op jit(solution)/shard_map/ppermute | solution.py:162
  33.3 1.3 %copy-start.2 = (f32[448,1152]{1,0:T(8,128)}, f32[448,1152]{1,0:T(8,128)S(1)}, u32[]{:S(2)}) copy-start(f32[448,1152]{1,0:T(8,128)S(1)} %get-tuple-element.19.igrad_in) | copy-start | bytes 6193156
  34.6 1.3 %copy-start.4 = (f32[448,1152]{1,0:T(8,128)}, f32[448,1152]{1,0:T(8,128)S(1)}, u32[]{:S(2)}) copy-start(f32[448,1152]{1,0:T(8,128)S(1)} %get-tuple-element.20.tgrad_in) | copy-start | bytes 6193156
  36.0 1.6 %copy-start.3 = (f32[448,1152]{1,0:T(8,128)S(1)}, f32[448,1152]{1,0:T(8,128)}, u32[]{:S(2)}) copy-start(f32[448,1152]{1,0:T(8,128)} %copy-done.2) | copy-start | bytes 6193156
  37.6 1.6 %copy-start.5 = (f32[448,1152]{1,0:T(8,128)S(1)}, f32[448,1152]{1,0:T(8,128)}, u32[]{:S(2)}) copy-start(f32[448,1152]{1,0:T(8,128)} %copy-done.4) | copy-start | bytes 6193156

commit v5 on v4

--- a/solution.py
+++ b/solution.py
@@ -57,7 +57,10 @@
     return nn(coeff, far_images)
 
 
-def own_kernel(scal, pos_ref, images_ref, texts_ref, loss_ref, igrad_ref, tgrad_ref):
+def own_kernel(
+    scal, flags, pos_ref, images_ref, texts_ref, cross_texts_ref, cross_images_ref,
+    loss_ref, igrad_ref, tgrad_ref,
+):
     images, texts = images_ref[...], texts_ref[...]
     logits = tile_logits(scal, texts, images)
     mask = pos_ref[...] == lax.broadcasted_iota(jnp.int32, logits.shape, 0)
@@ -68,6 +71,16 @@
     coeff = (scal[0] * (sigmoid(logits, e) - jnp.where(mask, 1.0, 0.0))).astype(BF16)
     igrad_ref[...] = tn(coeff, texts)
     tgrad_ref[...] = nn(coeff, images)
+
+    @pl.when(flags[0] != 0)
+    def _():
+        loss, grad = image_side(scal, images_ref[...], cross_texts_ref[...])
+        loss_ref[...] += loss
+        igrad_ref[...] += grad
+
+    @pl.when(flags[1] != 0)
+    def _():
+        tgrad_ref[...] += text_side(scal, texts_ref[...], cross_images_ref[...])
 
 
 def outer_kernel(
@@ -89,46 +102,17 @@
         tgrad_ref[...] += text_side(scal, texts_ref[...], far_images_ref[...])
 
 
-def dp_kernel(
+def last_kernel(
     scal, images_ref, texts_ref, far_texts_ref, far_images_ref, loss_in, igrad_in, tgrad_in,
-    loss_ref, igrad_ref, tgrad_ref,
+    loss_ref, igrad_out, tgrad_out, igrad_ref, tgrad_ref, sems,
 ):
     loss, grad = image_side(scal, images_ref[...], far_texts_ref[...])
-    loss_ref[...] = loss_in[...] + loss
-    igrad_ref[...] = igrad_in[...] + grad
-    tgrad_ref[...] = tgrad_in[...] + text_side(scal, texts_ref[...], far_images_ref[...])
-
-
-def last_kernel(
-    scal, flags, images_ref, texts_ref, cross_ref, loss_in, igrad_in, tgrad_in,
-    loss_ref, igrad_out, tgrad_out, igrad_ref, tgrad_ref, sems,
-):
-    count = 3.0 * loss_in.shape[1]
-
-    @pl.when(flags[0] == 0)
-    def _():
-        loss_ref[...] = loss_in[...] / count
-        igrad_ref[...] = igrad_in[...].astype(BF16)
-
-    @pl.when(flags[0] != 0)
-    def _():
-        loss, grad = image_side(scal, images_ref[...], cross_ref[...])
-        loss_ref[...] = (loss_in[...] + loss) / count
-        igrad_ref[...] = (igrad_in[...] + grad).astype(BF16)
-
+    loss_ref[...] = (loss_in[...] + loss) / (3.0 * loss_in.shape[1])
+    igrad_ref[...] = (igrad_in[...] + grad).astype(BF16)
     image_copy = pltpu.make_async_copy(igrad_ref, igrad_out, sems.at[0])
     image_copy.start()
-
-    @pl.when(flags[1] == 0)
-    def _():
-        tgrad_ref[...] = tgrad_in[...].astype(BF16)
-
-    @pl.when(flags[1] != 0)
-    def _():
-        tgrad_ref[...] = (
-            tgrad_in[...] + text_side(scal, texts_ref[...], cross_ref[...])
-        ).astype(BF16)
-
+    grad = text_side(scal, texts_ref[...], far_images_ref[...])
+    tgrad_ref[...] = (tgrad_in[...] + grad).astype(BF16)
     text_copy = pltpu.make_async_copy(tgrad_ref, tgrad_out, sems.at[1])
     text_copy.start()
     image_copy.wait()
@@ -164,34 +148,35 @@
     ahead = [(o, (o + 1) % outer) for o in range(outer)]
     crossing = [(a, b) for a, b in ahead if b % ROW == 0]
     within = [(a, b) for a, b in ahead if b % ROW != 0]
+    turned = [(b, a) for a, b in crossing]
+    back = [(b, a) for a, b in within]
+    cross_texts = step(texts, crossing)
+    cross_images = step(images, turned)
+    cross_texts, cross_images, texts, images = lax.optimization_barrier(
+        (cross_texts, cross_images, texts, images)
+    )
     cycle_text = passed_along(texts, "dp", 1)
     cycle_images = passed_along(images, "dp", -1)
-    back = [(b, a) for a, b in within]
     cut = rows // 2
-    cross = step(jnp.where(first, images, texts), crossing + [(b, a) for a, b in crossing])
     pod_texts = [step(t, within) for t in (texts[:cut], texts[cut:])]
     pod_images = [step(i, back) for i in (images[:cut], images[cut:])]
 
     loss_shape = jax.ShapeDtypeStruct((1, rows), F32)
     wide = jax.ShapeDtypeStruct((rows, width), F32)
     narrow = jax.ShapeDtypeStruct((rows, width), BF16)
-    loss, igrad, tgrad = call(
-        own_kernel, [loss_shape, wide, wide], [scal], positive_index, images, texts
+    sums = call(
+        own_kernel, [loss_shape, wide, wide], [scal, flags],
+        positive_index, images, texts, cross_texts, cross_images,
     )
     for far in zip(pod_texts, pod_images):
-        loss, igrad, tgrad = call(
-            outer_kernel, [loss_shape, wide, wide], [scal, flags],
-            images, texts, *far, loss, igrad, tgrad,
+        sums = call(
+            outer_kernel, [loss_shape, wide, wide], [scal, flags], images, texts, *far, *sums
         )
-    loss, igrad, tgrad = call(
-        dp_kernel, [loss_shape, wide, wide], [scal],
-        images, texts, cycle_text, cycle_images, loss, igrad, tgrad,
-    )
     away = pl.BlockSpec(memory_space=pl.ANY)
     held = pltpu.VMEM((rows, width), BF16)
     loss, igrad, tgrad = call(
-        last_kernel, [loss_shape, narrow, narrow], [scal, flags],
-        images, texts, cross, loss, igrad, tgrad,
+        last_kernel, [loss_shape, narrow, narrow], [scal],
+        images, texts, cycle_text, cycle_images, *sums,
         out_specs=[VMEM, away, away],
         scratch=[held, held, pltpu.SemaphoreType.DMA((2,))],
     )

time: 125 us -> 159 us (1.27)
  the two profiles are of different devices: /device:TPU:32 before, /device:TPU:319 now
where the time goes in v5:
time: 159 us; the launch traced here: 158 us
  waiting for transfers between devices  105 us (66%)
  starting transfers between devices  26.2 us (16%)
  Pallas kernels  16.8 us (11%)
  local copies, waits for them, and re-layouts  8.29 us (5%)
  between operations  2.29 us (1%)
    ppermute x6, waiting for transfers between devices, step(): return lax.ppermute(x, 'outer', pairs)  96.1 us
    ppermute x6, starting transfers between devices, step(): return lax.ppermute(x, 'outer', pairs)  17 us
    pallas_call x4, Pallas kernels, call(): pl.pallas_call(kernel, out_shape=outs, in_specs=[SMEM] * len(scalars) + [...  16.8 us
    ppermute x2, starting transfers between devices, passed_along(): lax.ppermute(x, axis, [(i, (i + by) % devices) for i in range(devices)])  9.18 us
    ppermute x2, waiting for transfers between devices, passed_along(): lax.ppermute(x, axis, [(i, (i + by) % devices) for i in range(devices)])  8.72 us
    unnamed x18, local copies, waits for them, and re-layouts  5.16 us
  transfers between devices with their start and end apart: 8, of which 3 were waited for; matrix products, arithmetic and copies ran while one was open for 1% of the time, Pallas kernels for 7%

profile of v5, /device:TPU:319, one launch (start us, length us, event | category | flops | bytes accessed | tf_op | source)
XLA Modules:
  0.0 158.5 jit_solution(7668161283819067986)
XLA Ops:
  0.6 0.0 copy-start.1
  0.6 0.0 copy-start
  0.7 0.0 copy-start.8
  0.7 5.2 %collective-permute-start = (bf16[448,1152]{1,0:T(8,128)(2,1)}, bf16[448,1152]{1,0:T(8,128)(2,1)S(1)}, u32[]{:S(2)}, u32[]{:S(2)}) collective-permute-start(bf16[448,1152]{1,0:T(8,128)(2,1)} %texts_ref.3), channel_id=1, source_target_pairs={{7,8},{15,16},{23,24},{31,0},{39,40},{47,48},{55,56},{63,32},{71,7... | collective-permute-start | bytes 3096584 | tf_op jit(solution)/shard_map/ppermute | solution.py:146
  5.9 1.3 collective-permute-start.1
  7.2 37.2 %collective-permute-done.cross_texts_ref = bf16[448,1152]{1,0:T(8,128)(2,1)S(1)} collective-permute-done((bf16[448,1152]{1,0:T(8,128)(2,1)}, bf16[448,1152]{1,0:T(8,128)(2,1)S(1)}, u32[]{:S(2)}, u32[]{:S(2)}) %collective-permute-start) | collective-permute-done | bytes 1032224 | tf_op jit(solution)/shard_map/ppermute | solution.py:146
  44.3 0.0 copy-start.2
  44.3 1.0 copy-done.2
  45.3 58.9 %collective-permute-done.1.cross_images_ref = bf16[448,1152]{1,0:T(8,128)(2,1)S(1)} collective-permute-done((bf16[448,1152]{1,0:T(8,128)(2,1)}, bf16[448,1152]{1,0:T(8,128)(2,1)S(1)}, u32[]{:S(2)}, u32[]{:S(2)}) %collective-permute-start.1) | collective-permute-done | bytes 1032224 | tf_op jit(solution)/shard_map/ppermute | solution.py:146
  104.2 0.0 copy-start.4
  104.2 1.0 copy-done.4
  105.2 2.1 %fusion.1 = (bf16[224,1152]{1,0:T(8,128)(2,1)S(1)}, bf16[224,1152]{1,0:T(8,128)(2,1)}) fusion(bf16[448,1152]{1,0:T(8,128)(2,1)} %texts_ref.3), kind=kLoop, calls=%fused_computation.3 | loop fusion | bytes 2064384 | tf_op jit(solution)/shard_map/slice | solution.py:161
  107.2 0.0 copy-done.1
  107.2 1.9 %collective-permute-start.2 = (bf16[448,1152]{1,0:T(8,128)(2,1)S(1)}, bf16[448,1152]{1,0:T(8,128)(2,1)S(1)}, u32[]{:S(2)}, u32[]{:S(2)}) collective-permute-start(bf16[448,1152]{1,0:T(8,128)(2,1)S(1)} %copy-done.1), channel_id=1, source_target_pairs={{0,32},{32,64},{64,96},{96,128},{128,160},{160,192},{192,224},{224... | collective-permute-start | bytes 3096584 | tf_op jit(solution)/shard_map/ppermute | solution.py:16
  109.1 1.3 collective-permute-start.6
  110.4 0.0 copy-done
  110.5 7.3 %collective-permute-start.3 = (bf16[448,1152]{1,0:T(8,128)(2,1)S(1)}, bf16[448,1152]{1,0:T(8,128)(2,1)}, u32[]{:S(2)}, u32[]{:S(2)}) collective-permute-start(bf16[448,1152]{1,0:T(8,128)(2,1)S(1)} %copy-done), channel_id=1, source_target_pairs={{0,736},{32,0},{64,32},{96,64},{128,96},{160,128},{192,160},{224,1... | collective-permute-start | bytes 3096584 | tf_op jit(solution)/shard_map/ppermute | solution.py:16
  117.7 1.1 fusion
  118.8 4.1 %collective-permute-start.7 = (bf16[224,1152]{1,0:T(8,128)(2,1)}, bf16[224,1152]{1,0:T(8,128)(2,1)}, u32[]{:S(2)}, u32[]{:S(2)}) collective-permute-start(bf16[224,1152]{1,0:T(8,128)(2,1)} %get-tuple-element.35), channel_id=1, source_target_pairs={{1,0},{2,1},{3,2},{4,3},{5,4},{6,5},{7,6},{9,8},{10,9},{11,10},{12... | collective-permute-start | bytes 1548296 | tf_op jit(solution)/shard_map/ppermute | solution.py:146
  122.9 1.3 collective-permute-start.4
  124.2 0.0 collective-permute-done.6.far_texts_ref
  124.2 0.0 copy-start.6
  124.2 0.8 copy-done.6
  125.0 3.8 %collective-permute-start.5 = (bf16[224,1152]{1,0:T(8,128)(2,1)}, bf16[224,1152]{1,0:T(8,128)(2,1)}, u32[]{:S(2)}, u32[]{:S(2)}) collective-permute-start(bf16[224,1152]{1,0:T(8,128)(2,1)} %get-tuple-element.36), channel_id=1, source_target_pairs={{1,0},{2,1},{3,2},{4,3},{5,4},{6,5},{7,6},{9,8},{10,9},{11,10},{12... | collective-permute-start | bytes 1548296 | tf_op jit(solution)/shard_map/ppermute | solution.py:146
  130.1 0.1 add_convert_fusion.flags
  130.2 0.1 pad_maximum_fusion.scal
  130.3 0.0 copy-done.8
  130.3 0.0 copy-start.3
  130.3 1.2 copy-done.3
  131.5 0.0 copy-start.5
  131.5 1.2 copy-done.5
  132.7 0.0 copy-start.7
  132.7 5.0 %shard_map.76 = (f32[1,448]{1,0:T(1,128)S(1)}, f32[448,1152]{1,0:T(8,128)S(1)}, f32[448,1152]{1,0:T(8,128)S(1)}) custom-call(f32[2]{0:T(128)S(1)} %pad_maximum_fusion.scal, s32[2]{0:T(128)S(1)} %add_convert_fusion.flags, s32[1,448]{1,0:T(1,128)S(1)} %copy-done.8, bf16[448,1152]{1,0:T(8,128)(2,1)S(1)} %copy-done, bf16[448,1152]{1,0:T(8,128)(2,1)S(1)} %copy-done.1, ...), custom_call_target="tpu_custom_call" | custom-call | flops 1000 | bytes 1000 | tf_op jit(solution)/shard_map/pallas_call | solution.py:123
  137.8 0.0 collective-permute-done.7.far_images_ref
  137.8 0.0 copy-done.7
  137.8 2.6 %shard_map.77 = (f32[1,448]{1,0:T(1,128)S(1)}, f32[448,1152]{1,0:T(8,128)S(1)}, f32[448,1152]{1,0:T(8,128)S(1)}) custom-call(f32[2]{0:T(128)S(1)} %pad_maximum_fusion.scal, s32[2]{0:T(128)S(1)} %add_convert_fusion.flags, bf16[448,1152]{1,0:T(8,128)(2,1)S(1)} %copy-done, bf16[448,1152]{1,0:T(8,128)(2,1)S(1)} %copy-done.1, bf16[224,1152]{1,0:T(8,128)(2,1)S(1)} %copy-done.7, ...), custom_call_target="tpu_custom_call" | custom-call | flops 1000 | bytes 1000 | tf_op jit(solution)/shard_map/pallas_call | solution.py:123
  140.4 0.0 collective-permute-done.4.far_texts_ref
  140.4 0.0 collective-permute-done.5.far_images_ref
  140.4 2.9 %shard_map.78 = (f32[1,448]{1,0:T(1,128)S(1)}, f32[448,1152]{1,0:T(8,128)S(1)}, f32[448,1152]{1,0:T(8,128)S(1)}) custom-call(f32[2]{0:T(128)S(1)} %pad_maximum_fusion.scal, s32[2]{0:T(128)S(1)} %add_convert_fusion.flags, bf16[448,1152]{1,0:T(8,128)(2,1)S(1)} %copy-done, bf16[448,1152]{1,0:T(8,128)(2,1)S(1)} %copy-done.1, ...), custom_call_target="tpu_custom_call" | custom-call | flops 1000 | bytes 1000 | tf_op jit(solution)/shard_map/pallas_call | solution.py:123
  143.3 8.7 %collective-permute-done.2.far_texts_ref = bf16[448,1152]{1,0:T(8,128)(2,1)S(1)} collective-permute-done((bf16[448,1152]{1,0:T(8,128)(2,1)S(1)}, bf16[448,1152]{1,0:T(8,128)(2,1)S(1)}, u32[]{:S(2)}, u32[]{:S(2)}) %collective-permute-start.2) | collective-permute-done | bytes 1032224 | tf_op jit(solution)/shard_map/ppermute | solution.py:16
  152.0 0.0 collective-permute-done.3.far_images_ref
  152.0 6.3 %shard_map.79 = (f32[1,448]{1,0:T(1,128)}, bf16[448,1152]{1,0:T(8,128)(2,1)}, bf16[448,1152]{1,0:T(8,128)(2,1)}) custom-call(f32[2]{0:T(128)S(1)} %pad_maximum_fusion.scal, bf16[448,1152]{1,0:T(8,128)(2,1)S(1)} %copy-done, bf16[448,1152]{1,0:T(8,128)(2,1)S(1)} %copy-done.1, bf16[448,1152]{1,0:T(8,128)(2,1)S(1)} %collective-permute-done.2.far_texts_ref, ...), custom_call_target="tpu_custom_call" | custom-call | flops 1000 | bytes 1000 | tf_op jit(solution)/shard_map/pallas_call | solution.py:123
Async XLA Ops:
  0.6 106.6 %copy-start.1 = (bf16[448,1152]{1,0:T(8,128)(2,1)S(1)}, bf16[448,1152]{1,0:T(8,128)(2,1)}, u32[]{:S(2)}) copy-start(bf16[448,1152]{1,0:T(8,128)(2,1)} %texts_ref.3) | copy-start | bytes 3096580
  0.6 109.8 %copy-start = (bf16[448,1152]{1,0:T(8,128)(2,1)S(1)}, bf16[448,1152]{1,0:T(8,128)(2,1)}, u32[]{:S(2)}) copy-start(bf16[448,1152]{1,0:T(8,128)(2,1)} %images_ref.3) | copy-start | bytes 3096580
  0.7 129.6 %copy-start.8 = (s32[1,448]{1,0:T(1,128)S(1)}, s32[1,448]{1,0:T(1,128)}, u32[]{:S(2)}) copy-start(s32[1,448]{1,0:T(1,128)} %pos_ref.1) | copy-start | bytes 5380
  0.7 43.7 %collective-permute-start = (bf16[448,1152]{1,0:T(8,128)(2,1)}, bf16[448,1152]{1,0:T(8,128)(2,1)S(1)}, u32[]{:S(2)}, u32[]{:S(2)}) collective-permute-start(bf16[448,1152]{1,0:T(8,128)(2,1)} %texts_ref.3), channel_id=1, source_target_pairs={{7,8},{15,16},{23,24},{31,0},{39,40},{47,48},{55,56},{63,32},{71,7... | collective-permute-start | bytes 3096584 | tf_op jit(solution)/shard_map/ppermute | solution.py:146
  5.9 98.3 %collective-permute-start.1 = (bf16[448,1152]{1,0:T(8,128)(2,1)}, bf16[448,1152]{1,0:T(8,128)(2,1)S(1)}, u32[]{:S(2)}, u32[]{:S(2)}) collective-permute-start(bf16[448,1152]{1,0:T(8,128)(2,1)} %images_ref.3), channel_id=1, source_target_pairs={{8,7},{16,15},{24,23},{0,31},{40,39},{48,47},{56,55},{32,63},{72,7... | collective-permute-start | bytes 3096584 | tf_op jit(solution)/shard_map/ppermute | solution.py:146
  44.3 1.0 copy-start.2
  104.2 1.0 copy-start.4
  107.2 44.8 %collective-permute-start.2 = (bf16[448,1152]{1,0:T(8,128)(2,1)S(1)}, bf16[448,1152]{1,0:T(8,128)(2,1)S(1)}, u32[]{:S(2)}, u32[]{:S(2)}) collective-permute-start(bf16[448,1152]{1,0:T(8,128)(2,1)S(1)} %copy-done.1), channel_id=1, source_target_pairs={{0,32},{32,64},{64,96},{96,128},{128,160},{160,192},{192,224},{224... | collective-permute-start | bytes 3096584 | tf_op jit(solution)/shard_map/ppermute | solution.py:16
  109.1 15.0 %collective-permute-start.6 = (bf16[224,1152]{1,0:T(8,128)(2,1)S(1)}, bf16[224,1152]{1,0:T(8,128)(2,1)S(1)}, u32[]{:S(2)}, u32[]{:S(2)}) collective-permute-start(bf16[224,1152]{1,0:T(8,128)(2,1)S(1)} %get-tuple-element.37), channel_id=1, source_target_pairs={{0,1},{1,2},{2,3},{3,4},{4,5},{5,6},{6,7},{8,9},{9,10},{10,11},{11... | collective-permute-start | bytes 1548296 | tf_op jit(solution)/shard_map/ppermute | solution.py:146
  110.5 41.6 %collective-permute-start.3 = (bf16[448,1152]{1,0:T(8,128)(2,1)S(1)}, bf16[448,1152]{1,0:T(8,128)(2,1)}, u32[]{:S(2)}, u32[]{:S(2)}) collective-permute-start(bf16[448,1152]{1,0:T(8,128)(2,1)S(1)} %copy-done), channel_id=1, source_target_pairs={{0,736},{32,0},{64,32},{96,64},{128,96},{160,128},{192,160},{224,1... | collective-permute-start | bytes 3096584 | tf_op jit(solution)/shard_map/ppermute | solution.py:16
  118.8 19.0 %collective-permute-start.7 = (bf16[224,1152]{1,0:T(8,128)(2,1)}, bf16[224,1152]{1,0:T(8,128)(2,1)}, u32[]{:S(2)}, u32[]{:S(2)}) collective-permute-start(bf16[224,1152]{1,0:T(8,128)(2,1)} %get-tuple-element.35), channel_id=1, source_target_pairs={{1,0},{2,1},{3,2},{4,3},{5,4},{6,5},{7,6},{9,8},{10,9},{11,10},{12... | collective-permute-start | bytes 1548296 | tf_op jit(solution)/shard_map/ppermute | solution.py:146
  122.9 17.5 %collective-permute-start.4 = (bf16[224,1152]{1,0:T(8,128)(2,1)}, bf16[224,1152]{1,0:T(8,128)(2,1)}, u32[]{:S(2)}, u32[]{:S(2)}) collective-permute-start(bf16[224,1152]{1,0:T(8,128)(2,1)} %get-tuple-element.38), channel_id=1, source_target_pairs={{0,1},{1,2},{2,3},{3,4},{4,5},{5,6},{6,7},{8,9},{9,10},{10,11},{11... | collective-permute-start | bytes 1548296 | tf_op jit(solution)/shard_map/ppermute | solution.py:146
  124.2 0.8 copy-start.6
  125.0 15.4 %collective-permute-start.5 = (bf16[224,1152]{1,0:T(8,128)(2,1)}, bf16[224,1152]{1,0:T(8,128)(2,1)}, u32[]{:S(2)}, u32[]{:S(2)}) collective-permute-start(bf16[224,1152]{1,0:T(8,128)(2,1)} %get-tuple-element.36), channel_id=1, source_target_pairs={{1,0},{2,1},{3,2},{4,3},{5,4},{6,5},{7,6},{9,8},{10,9},{11,10},{12... | collective-permute-start | bytes 1548296 | tf_op jit(solution)/shard_map/ppermute | solution.py:146
  130.3 1.2 copy-start.3
  131.5 1.2 copy-start.5
  132.7 5.1 %copy-start.7 = (bf16[224,1152]{1,0:T(8,128)(2,1)S(1)}, bf16[224,1152]{1,0:T(8,128)(2,1)}, u32[]{:S(2)}) copy-start(bf16[224,1152]{1,0:T(8,128)(2,1)} %copy-done.6) | copy-start | bytes 1548292

commit v6 on v5

--- a/solution.py
+++ b/solution.py
@@ -58,8 +58,7 @@
 
 
 def own_kernel(
-    scal, flags, pos_ref, images_ref, texts_ref, cross_texts_ref, cross_images_ref,
-    loss_ref, igrad_ref, tgrad_ref,
+    scal, flags, pos_ref, images_ref, texts_ref, cross_ref, loss_ref, igrad_ref, tgrad_ref
 ):
     images, texts = images_ref[...], texts_ref[...]
     logits = tile_logits(scal, texts, images)
@@ -74,13 +73,13 @@
 
     @pl.when(flags[0] != 0)
     def _():
-        loss, grad = image_side(scal, images_ref[...], cross_texts_ref[...])
+        loss, grad = image_side(scal, images_ref[...], cross_ref[...])
         loss_ref[...] += loss
         igrad_ref[...] += grad
 
     @pl.when(flags[1] != 0)
     def _():
-        tgrad_ref[...] += text_side(scal, texts_ref[...], cross_images_ref[...])
+        tgrad_ref[...] += text_side(scal, texts_ref[...], cross_ref[...])
 
 
 def outer_kernel(
@@ -148,30 +147,27 @@
     ahead = [(o, (o + 1) % outer) for o in range(outer)]
     crossing = [(a, b) for a, b in ahead if b % ROW == 0]
     within = [(a, b) for a, b in ahead if b % ROW != 0]
-    turned = [(b, a) for a, b in crossing]
     back = [(b, a) for a, b in within]
-    cross_texts = step(texts, crossing)
-    cross_images = step(images, turned)
-    cross_texts, cross_images, texts, images = lax.optimization_barrier(
-        (cross_texts, cross_images, texts, images)
+    mixed, texts, images = lax.optimization_barrier(
+        (jnp.where(first, images, texts), texts, images)
     )
+    cross = step(mixed, crossing + [(b, a) for a, b in crossing])
     cycle_text = passed_along(texts, "dp", 1)
     cycle_images = passed_along(images, "dp", -1)
-    cut = rows // 2
-    pod_texts = [step(t, within) for t in (texts[:cut], texts[cut:])]
-    pod_images = [step(i, back) for i in (images[:cut], images[cut:])]
+    pod_text = step(texts, within)
+    pod_images = step(images, back)
 
     loss_shape = jax.ShapeDtypeStruct((1, rows), F32)
     wide = jax.ShapeDtypeStruct((rows, width), F32)
     narrow = jax.ShapeDtypeStruct((rows, width), BF16)
     sums = call(
         own_kernel, [loss_shape, wide, wide], [scal, flags],
-        positive_index, images, texts, cross_texts, cross_images,
+        positive_index, images, texts, cross,
     )
-    for far in zip(pod_texts, pod_images):
-        sums = call(
-            outer_kernel, [loss_shape, wide, wide], [scal, flags], images, texts, *far, *sums
-        )
+    sums = call(
+        outer_kernel, [loss_shape, wide, wide], [scal, flags],
+        images, texts, pod_text, pod_images, *sums,
+    )
     away = pl.BlockSpec(memory_space=pl.ANY)
     held = pltpu.VMEM((rows, width), BF16)
     loss, igrad, tgrad = call(

time: 159 us -> 126 us (0.79)
  the two profiles are of different devices: /device:TPU:319 before, /device:TPU:47 now
where the time goes in v6:
time: 126 us
  waiting for transfers between devices  87.8 us (70%)
  starting transfers between devices  17.3 us (14%)
  Pallas kernels  15.9 us (13%)
  other arithmetic  2.6 us (2%)
  between operations  2.09 us (2%)
    ppermute x2, waiting for transfers between devices, passed_along(): lax.ppermute(x, axis, [(i, (i + by) % devices) for i in range(devices)])  87.1 us
    pallas_call x3, Pallas kernels, call(): pl.pallas_call(kernel, out_shape=outs, in_specs=[SMEM] * len(scalars) + [...  15.9 us
    ppermute x2, starting transfers between devices, passed_along(): lax.ppermute(x, axis, [(i, (i + by) % devices) for i in range(devices)])  9.18 us
    ppermute x3, starting transfers between devices, step(): return lax.ppermute(x, 'outer', pairs)  8.08 us
  transfers between devices with their start and end apart: 5, of which 2 were waited for; matrix products, arithmetic and copies ran while one was open for 0% of the time, Pallas kernels for 8%

profile of v6, /device:TPU:47, one launch (start us, length us, event | category | flops | bytes accessed | tf_op | source)
XLA Modules:
  0.0 125.6 jit_solution(8213583462362710786)
XLA Ops:
  0.6 0.0 copy-start
  0.6 0.0 copy-start.1
  0.7 0.0 copy-start.2
  0.7 2.4 %broadcast_select_fusion = bf16[448,1152]{1,0:T(8,128)(2,1)} fusion(bf16[448,1152]{1,0:T(8,128)(2,1)} %images_ref.2, bf16[448,1152]{1,0:T(8,128)(2,1)} %texts_ref.2, pred[]{:T(512)} %eq.9), kind=kLoop, calls=%fused_computation | loop fusion | flops 516096 | bytes 3096577 | tf_op jit(solution)/shard_map/jit(_where)/select_n | solution.py:152
  3.1 2.8 %collective-permute-start.4 = (bf16[448,1152]{1,0:T(8,128)(2,1)}, bf16[448,1152]{1,0:T(8,128)(2,1)}, u32[]{:S(2)}, u32[]{:S(2)}) collective-permute-start(bf16[448,1152]{1,0:T(8,128)(2,1)} %broadcast_select_fusion), channel_id=1, source_target_pairs={{7,8},{15,16},{23,24},{31,0},{8,7},{16,15},{24,23},{0,31},{39,40},... | collective-permute-start | bytes 3096584 | tf_op jit(solution)/shard_map/ppermute | solution.py:145
  5.9 0.0 copy-done.1
  5.9 1.3 %collective-permute-start.2 = (bf16[448,1152]{1,0:T(8,128)(2,1)S(1)}, bf16[448,1152]{1,0:T(8,128)(2,1)}, u32[]{:S(2)}, u32[]{:S(2)}) collective-permute-start(bf16[448,1152]{1,0:T(8,128)(2,1)S(1)} %copy-done.1), channel_id=1, source_target_pairs={{0,1},{1,2},{2,3},{3,4},{4,5},{5,6},{6,7},{8,9},{9,10},{10,11},{11... | collective-permute-start | bytes 3096584 | tf_op jit(solution)/shard_map/ppermute | solution.py:145
  7.2 0.0 copy-done
  7.2 4.0 %collective-permute-start.3 = (bf16[448,1152]{1,0:T(8,128)(2,1)S(1)}, bf16[448,1152]{1,0:T(8,128)(2,1)}, u32[]{:S(2)}, u32[]{:S(2)}) collective-permute-start(bf16[448,1152]{1,0:T(8,128)(2,1)S(1)} %copy-done), channel_id=1, source_target_pairs={{1,0},{2,1},{3,2},{4,3},{5,4},{6,5},{7,6},{9,8},{10,9},{11,10},{12... | collective-permute-start | bytes 3096584 | tf_op jit(solution)/shard_map/ppermute | solution.py:145
  11.2 5.3 %collective-permute-start = (bf16[448,1152]{1,0:T(8,128)(2,1)S(1)}, bf16[448,1152]{1,0:T(8,128)(2,1)S(1)}, u32[]{:S(2)}, u32[]{:S(2)}) collective-permute-start(bf16[448,1152]{1,0:T(8,128)(2,1)S(1)} %copy-done.1), channel_id=1, source_target_pairs={{0,32},{32,64},{64,96},{96,128},{128,160},{160,192},{192,224},{224... | collective-permute-start | bytes 3096584 | tf_op jit(solution)/shard_map/ppermute | solution.py:16
  16.6 3.8 %collective-permute-start.1 = (bf16[448,1152]{1,0:T(8,128)(2,1)S(1)}, bf16[448,1152]{1,0:T(8,128)(2,1)}, u32[]{:S(2)}, u32[]{:S(2)}) collective-permute-start(bf16[448,1152]{1,0:T(8,128)(2,1)S(1)} %copy-done), channel_id=1, source_target_pairs={{0,736},{32,0},{64,32},{96,64},{128,96},{160,128},{192,160},{224,1... | collective-permute-start | bytes 3096584 | tf_op jit(solution)/shard_map/ppermute | solution.py:16
  21.8 0.1 add_convert_fusion.flags
  21.9 0.1 pad_maximum_fusion.scal
  21.9 0.7 collective-permute-done.4.cross_ref
  22.6 0.0 copy-done.2
  22.6 5.7 %shard_map.76 = (f32[1,448]{1,0:T(1,128)S(1)}, f32[448,1152]{1,0:T(8,128)S(1)}, f32[448,1152]{1,0:T(8,128)S(1)}) custom-call(f32[2]{0:T(128)S(1)} %pad_maximum_fusion.scal, s32[2]{0:T(128)S(1)} %add_convert_fusion.flags, s32[1,448]{1,0:T(1,128)S(1)} %copy-done.2, bf16[448,1152]{1,0:T(8,128)(2,1)S(1)} %copy-done, bf16[448,1152]{1,0:T(8,128)(2,1)S(1)} %copy-done.1, ...), custom_call_target="tpu_custom_call" | custom-call | flops 1000 | bytes 1000 | tf_op jit(solution)/shard_map/pallas_call | solution.py:122
  28.3 0.0 collective-permute-done.2.far_texts_ref
  28.3 0.0 collective-permute-done.3.far_images_ref
  28.3 3.8 %shard_map.77 = (f32[1,448]{1,0:T(1,128)S(1)}, f32[448,1152]{1,0:T(8,128)S(1)}, f32[448,1152]{1,0:T(8,128)S(1)}) custom-call(f32[2]{0:T(128)S(1)} %pad_maximum_fusion.scal, s32[2]{0:T(128)S(1)} %add_convert_fusion.flags, bf16[448,1152]{1,0:T(8,128)(2,1)S(1)} %copy-done, bf16[448,1152]{1,0:T(8,128)(2,1)S(1)} %copy-done.1, ...), custom_call_target="tpu_custom_call" | custom-call | flops 1000 | bytes 1000 | tf_op jit(solution)/shard_map/pallas_call | solution.py:122
  32.2 87.1 %collective-permute-done.far_texts_ref = bf16[448,1152]{1,0:T(8,128)(2,1)S(1)} collective-permute-done((bf16[448,1152]{1,0:T(8,128)(2,1)S(1)}, bf16[448,1152]{1,0:T(8,128)(2,1)S(1)}, u32[]{:S(2)}, u32[]{:S(2)}) %collective-permute-start) | collective-permute-done | bytes 1032224 | tf_op jit(solution)/shard_map/ppermute | solution.py:16
  119.3 0.0 collective-permute-done.1.far_images_ref
  119.3 6.3 %shard_map.78 = (f32[1,448]{1,0:T(1,128)}, bf16[448,1152]{1,0:T(8,128)(2,1)}, bf16[448,1152]{1,0:T(8,128)(2,1)}) custom-call(f32[2]{0:T(128)S(1)} %pad_maximum_fusion.scal, bf16[448,1152]{1,0:T(8,128)(2,1)S(1)} %copy-done, bf16[448,1152]{1,0:T(8,128)(2,1)S(1)} %copy-done.1, bf16[448,1152]{1,0:T(8,128)(2,1)S(1)} %collective-permute-done.far_texts_ref, ...), custom_call_target="tpu_custom_call" | custom-call | flops 1000 | bytes 1000 | tf_op jit(solution)/shard_map/pallas_call | solution.py:122
Async XLA Ops:
  0.6 6.6 %copy-start = (bf16[448,1152]{1,0:T(8,128)(2,1)S(1)}, bf16[448,1152]{1,0:T(8,128)(2,1)}, u32[]{:S(2)}) copy-start(bf16[448,1152]{1,0:T(8,128)(2,1)} %images_ref.2) | copy-start | bytes 3096580
  0.6 5.3 %copy-start.1 = (bf16[448,1152]{1,0:T(8,128)(2,1)S(1)}, bf16[448,1152]{1,0:T(8,128)(2,1)}, u32[]{:S(2)}) copy-start(bf16[448,1152]{1,0:T(8,128)(2,1)} %texts_ref.2) | copy-start | bytes 3096580
  0.7 21.9 %copy-start.2 = (s32[1,448]{1,0:T(1,128)S(1)}, s32[1,448]{1,0:T(1,128)}, u32[]{:S(2)}) copy-start(s32[1,448]{1,0:T(1,128)} %pos_ref.1) | copy-start | bytes 5380
  3.1 19.5 %collective-permute-start.4 = (bf16[448,1152]{1,0:T(8,128)(2,1)}, bf16[448,1152]{1,0:T(8,128)(2,1)}, u32[]{:S(2)}, u32[]{:S(2)}) collective-permute-start(bf16[448,1152]{1,0:T(8,128)(2,1)} %broadcast_select_fusion), channel_id=1, source_target_pairs={{7,8},{15,16},{23,24},{31,0},{8,7},{16,15},{24,23},{0,31},{39,40},... | collective-permute-start | bytes 3096584 | tf_op jit(solution)/shard_map/ppermute | solution.py:145
  5.9 22.4 %collective-permute-start.2 = (bf16[448,1152]{1,0:T(8,128)(2,1)S(1)}, bf16[448,1152]{1,0:T(8,128)(2,1)}, u32[]{:S(2)}, u32[]{:S(2)}) collective-permute-start(bf16[448,1152]{1,0:T(8,128)(2,1)S(1)} %copy-done.1), channel_id=1, source_target_pairs={{0,1},{1,2},{2,3},{3,4},{4,5},{5,6},{6,7},{8,9},{9,10},{10,11},{11... | collective-permute-start | bytes 3096584 | tf_op jit(solution)/shard_map/ppermute | solution.py:145
  7.2 21.1 %collective-permute-start.3 = (bf16[448,1152]{1,0:T(8,128)(2,1)S(1)}, bf16[448,1152]{1,0:T(8,128)(2,1)}, u32[]{:S(2)}, u32[]{:S(2)}) collective-permute-start(bf16[448,1152]{1,0:T(8,128)(2,1)S(1)} %copy-done), channel_id=1, source_target_pairs={{1,0},{2,1},{3,2},{4,3},{5,4},{6,5},{7,6},{9,8},{10,9},{11,10},{12... | collective-permute-start | bytes 3096584 | tf_op jit(solution)/shard_map/ppermute | solution.py:145
  11.2 108.1 %collective-permute-start = (bf16[448,1152]{1,0:T(8,128)(2,1)S(1)}, bf16[448,1152]{1,0:T(8,128)(2,1)S(1)}, u32[]{:S(2)}, u32[]{:S(2)}) collective-permute-start(bf16[448,1152]{1,0:T(8,128)(2,1)S(1)} %copy-done.1), channel_id=1, source_target_pairs={{0,32},{32,64},{64,96},{96,128},{128,160},{160,192},{192,224},{224... | collective-permute-start | bytes 3096584 | tf_op jit(solution)/shard_map/ppermute | solution.py:16
  16.6 102.8 %collective-permute-start.1 = (bf16[448,1152]{1,0:T(8,128)(2,1)S(1)}, bf16[448,1152]{1,0:T(8,128)(2,1)}, u32[]{:S(2)}, u32[]{:S(2)}) collective-permute-start(bf16[448,1152]{1,0:T(8,128)(2,1)S(1)} %copy-done), channel_id=1, source_target_pairs={{0,736},{32,0},{64,32},{96,64},{128,96},{160,128},{192,160},{224,1... | collective-permute-start | bytes 3096584 | tf_op jit(solution)/shard_map/ppermute | solution.py:16

commit v7 on v6

--- a/solution.py
+++ b/solution.py
@@ -57,9 +57,7 @@
     return nn(coeff, far_images)
 
 
-def own_kernel(
-    scal, flags, pos_ref, images_ref, texts_ref, cross_ref, loss_ref, igrad_ref, tgrad_ref
-):
+def own_kernel(scal, pos_ref, images_ref, texts_ref, loss_ref, igrad_ref, tgrad_ref):
     images, texts = images_ref[...], texts_ref[...]
     logits = tile_logits(scal, texts, images)
     mask = pos_ref[...] == lax.broadcasted_iota(jnp.int32, logits.shape, 0)
@@ -71,34 +69,15 @@
     igrad_ref[...] = tn(coeff, texts)
     tgrad_ref[...] = nn(coeff, images)
 
-    @pl.when(flags[0] != 0)
-    def _():
-        loss, grad = image_side(scal, images_ref[...], cross_ref[...])
-        loss_ref[...] += loss
-        igrad_ref[...] += grad
-
-    @pl.when(flags[1] != 0)
-    def _():
-        tgrad_ref[...] += text_side(scal, texts_ref[...], cross_ref[...])
-
 
 def outer_kernel(
-    scal, flags, images_ref, texts_ref, far_texts_ref, far_images_ref, loss_in, igrad_in, tgrad_in,
+    scal, images_ref, texts_ref, far_texts_ref, far_images_ref, loss_in, igrad_in, tgrad_in,
     loss_ref, igrad_ref, tgrad_ref,
 ):
-    loss_ref[...] = loss_in[...]
-    igrad_ref[...] = igrad_in[...]
-    tgrad_ref[...] = tgrad_in[...]
-
-    @pl.when(flags[0] == 0)
-    def _():
-        loss, grad = image_side(scal, images_ref[...], far_texts_ref[...])
-        loss_ref[...] += loss
-        igrad_ref[...] += grad
-
-    @pl.when(flags[1] == 0)
-    def _():
-        tgrad_ref[...] += text_side(scal, texts_ref[...], far_images_ref[...])
+    loss, grad = image_side(scal, images_ref[...], far_texts_ref[...])
+    loss_ref[...] = loss_in[...] + loss
+    igrad_ref[...] = igrad_in[...] + grad
+    tgrad_ref[...] = tgrad_in[...] + text_side(scal, texts_ref[...], far_images_ref[...])
 
 
 def last_kernel(
@@ -130,43 +109,20 @@
     )(*scalars, *args)
 
 
-ROW = 8
-
-
 def local(images, texts, positive_index, log_scale, bias):
     rows, width = images.shape
-    outer = lax.axis_size("outer")
-    here = lax.axis_index("outer")
     scal = jnp.concatenate([jnp.exp(log_scale), bias])
-    first, last = here % ROW == 0, here % ROW == ROW - 1
-    flags = jnp.stack([first, last]).astype(jnp.int32)
-
-    def step(x, pairs):
-        return lax.ppermute(x, "outer", pairs)
-
-    ahead = [(o, (o + 1) % outer) for o in range(outer)]
-    crossing = [(a, b) for a, b in ahead if b % ROW == 0]
-    within = [(a, b) for a, b in ahead if b % ROW != 0]
-    back = [(b, a) for a, b in within]
-    mixed, texts, images = lax.optimization_barrier(
-        (jnp.where(first, images, texts), texts, images)
-    )
-    cross = step(mixed, crossing + [(b, a) for a, b in crossing])
+    pod_text = passed_along(texts, "outer", 1)
+    pod_images = passed_along(images, "outer", -1)
     cycle_text = passed_along(texts, "dp", 1)
     cycle_images = passed_along(images, "dp", -1)
-    pod_text = step(texts, within)
-    pod_images = step(images, back)
 
     loss_shape = jax.ShapeDtypeStruct((1, rows), F32)
     wide = jax.ShapeDtypeStruct((rows, width), F32)
     narrow = jax.ShapeDtypeStruct((rows, width), BF16)
+    sums = call(own_kernel, [loss_shape, wide, wide], [scal], positive_index, images, texts)
     sums = call(
-        own_kernel, [loss_shape, wide, wide], [scal, flags],
-        positive_index, images, texts, cross,
-    )
-    sums = call(
-        outer_kernel, [loss_shape, wide, wide], [scal, flags],
-        images, texts, pod_text, pod_images, *sums,
+        outer_kernel, [loss_shape, wide, wide], [scal], images, texts, pod_text, pod_images, *sums
     )
     away = pl.BlockSpec(memory_space=pl.ANY)
     held = pltpu.VMEM((rows, width), BF16)

time: 126 us -> 125 us (level)
  the two profiles are of different devices: /device:TPU:47 before, /device:TPU:16 now
where the time goes in v7:
time: 125 us
  waiting for transfers between devices  78.7 us (63%)
  starting transfers between devices  27.6 us (22%)
  Pallas kernels  13.1 us (10%)
  local copies, waits for them, and re-layouts  3.13 us (3%)
  between operations  2.02 us (2%)
    ppermute x4, waiting for transfers between devices, passed_along(): lax.ppermute(x, axis, [(i, (i + by) % devices) for i in range(devices)])  78.7 us
    ppermute x4, starting transfers between devices, passed_along(): lax.ppermute(x, axis, [(i, (i + by) % devices) for i in range(devices)])  27.6 us
    pallas_call x3, Pallas kernels, call(): pl.pallas_call(kernel, out_shape=outs, in_specs=[SMEM] * len(scalars) + [...  13.1 us
    unnamed x10, local copies, waits for them, and re-layouts  3.13 us
  transfers between devices with their start and end apart: 4, of which 2 were waited for; matrix products, arithmetic and copies ran while one was open for 0% of the time, Pallas kernels for 6%

profile of v7, /device:TPU:16, one launch (start us, length us, event | category | flops | bytes accessed | tf_op | source)
XLA Modules:
  0.0 124.7 jit_solution(14316291738933474338)
XLA Ops:
  0.6 1.9 %collective-permute-start.2 = (bf16[448,1152]{1,0:T(8,128)(2,1)}, bf16[448,1152]{1,0:T(8,128)(2,1)S(1)}, u32[]{:S(2)}, u32[]{:S(2)}) collective-permute-start(bf16[448,1152]{1,0:T(8,128)(2,1)} %texts_ref.5), channel_id=1, source_target_pairs={{0,1},{1,2},{2,3},{3,4},{4,5},{5,6},{6,7},{7,8},{8,9},{9,10},{10,1... | collective-permute-start | bytes 3096584 | tf_op jit(solution)/shard_map/ppermute | solution.py:16
  2.6 5.8 %collective-permute-start.3 = (bf16[448,1152]{1,0:T(8,128)(2,1)}, bf16[448,1152]{1,0:T(8,128)(2,1)S(1)}, u32[]{:S(2)}, u32[]{:S(2)}) collective-permute-start(bf16[448,1152]{1,0:T(8,128)(2,1)} %images_ref.5), channel_id=1, source_target_pairs={{0,31},{1,0},{2,1},{3,2},{4,3},{5,4},{6,5},{7,6},{8,7},{9,8},{10,9... | collective-permute-start | bytes 3096584 | tf_op jit(solution)/shard_map/ppermute | solution.py:16
  8.3 5.9 %collective-permute-start = (bf16[448,1152]{1,0:T(8,128)(2,1)}, bf16[448,1152]{1,0:T(8,128)(2,1)S(1)}, u32[]{:S(2)}, u32[]{:S(2)}) collective-permute-start(bf16[448,1152]{1,0:T(8,128)(2,1)} %texts_ref.5), channel_id=1, source_target_pairs={{0,32},{32,64},{64,96},{96,128},{128,160},{160,192},{192,224},{224... | collective-permute-start | bytes 3096584 | tf_op jit(solution)/shard_map/ppermute | solution.py:16
  14.3 14.0 %collective-permute-start.1 = (bf16[448,1152]{1,0:T(8,128)(2,1)}, bf16[448,1152]{1,0:T(8,128)(2,1)S(1)}, u32[]{:S(2)}, u32[]{:S(2)}) collective-permute-start(bf16[448,1152]{1,0:T(8,128)(2,1)} %images_ref.5), channel_id=1, source_target_pairs={{0,736},{32,0},{64,32},{96,64},{128,96},{160,128},{192,160},{224,1... | collective-permute-start | bytes 3096584 | tf_op jit(solution)/shard_map/ppermute | solution.py:16
  29.6 0.1 pad_maximum_fusion.scal
  29.7 0.0 copy-start
  29.7 1.2 copy-done
  30.9 0.0 copy-start.2
  30.9 1.2 copy-done.2
  32.2 0.0 copy-start.4
  32.2 0.7 copy-done.4
  32.8 0.0 copy-start.1
  32.8 0.0 copy-start.3
  32.8 3.4 %shard_map.76 = (f32[1,448]{1,0:T(1,128)S(1)}, f32[448,1152]{1,0:T(8,128)S(1)}, f32[448,1152]{1,0:T(8,128)S(1)}) custom-call(f32[2]{0:T(128)S(1)} %pad_maximum_fusion.scal, s32[1,448]{1,0:T(1,128)S(1)} %copy-done.4, bf16[448,1152]{1,0:T(8,128)(2,1)S(1)} %copy-done, bf16[448,1152]{1,0:T(8,128)(2,1)S(1)} %copy-done.2), custom_call_target="tpu_custom_call" | custom-call | flops 1000 | bytes 1000 | tf_op jit(solution)/shard_map/pallas_call | solution.py:101
  36.2 58.4 %collective-permute-done.2.far_texts_ref = bf16[448,1152]{1,0:T(8,128)(2,1)S(1)} collective-permute-done((bf16[448,1152]{1,0:T(8,128)(2,1)}, bf16[448,1152]{1,0:T(8,128)(2,1)S(1)}, u32[]{:S(2)}, u32[]{:S(2)}) %collective-permute-start.2) | collective-permute-done | bytes 1032224 | tf_op jit(solution)/shard_map/ppermute | solution.py:16
  94.7 0.0 collective-permute-done.3.far_images_ref
  94.7 0.0 copy-done.1
  94.7 0.0 copy-done.3
  94.7 4.1 %shard_map.77 = (f32[1,448]{1,0:T(1,128)S(1)}, f32[448,1152]{1,0:T(8,128)S(1)}, f32[448,1152]{1,0:T(8,128)S(1)}) custom-call(f32[2]{0:T(128)S(1)} %pad_maximum_fusion.scal, bf16[448,1152]{1,0:T(8,128)(2,1)S(1)} %copy-done.1, bf16[448,1152]{1,0:T(8,128)(2,1)S(1)} %copy-done.3, bf16[448,1152]{1,0:T(8,128)(2,1)S(1)} %collective-permute-done.2.far_texts_ref, ...), custom_call_target="tpu_custom_call" | custom-call | flops 1000 | bytes 1000 | tf_op jit(solution)/shard_map/pallas_call | solution.py:101
  98.8 0.0 collective-permute-done.far_texts_ref
  98.8 20.3 %collective-permute-done.1.far_images_ref = bf16[448,1152]{1,0:T(8,128)(2,1)S(1)} collective-permute-done((bf16[448,1152]{1,0:T(8,128)(2,1)}, bf16[448,1152]{1,0:T(8,128)(2,1)S(1)}, u32[]{:S(2)}, u32[]{:S(2)}) %collective-permute-start.1) | collective-permute-done | bytes 1032224 | tf_op jit(solution)/shard_map/ppermute | solution.py:16
  119.1 5.7 %shard_map.78 = (f32[1,448]{1,0:T(1,128)}, bf16[448,1152]{1,0:T(8,128)(2,1)}, bf16[448,1152]{1,0:T(8,128)(2,1)}) custom-call(f32[2]{0:T(128)S(1)} %pad_maximum_fusion.scal, bf16[448,1152]{1,0:T(8,128)(2,1)S(1)} %copy-done.1, bf16[448,1152]{1,0:T(8,128)(2,1)S(1)} %copy-done.3, bf16[448,1152]{1,0:T(8,128)(2,1)S(1)} %collective-permute-done.far_texts_ref, ...), custom_call_target="tpu_custom_call" | custom-call | flops 1000 | bytes 1000 | tf_op jit(solution)/shard_map/pallas_call | solution.py:101
Async XLA Ops:
  0.6 94.0 %collective-permute-start.2 = (bf16[448,1152]{1,0:T(8,128)(2,1)}, bf16[448,1152]{1,0:T(8,128)(2,1)S(1)}, u32[]{:S(2)}, u32[]{:S(2)}) collective-permute-start(bf16[448,1152]{1,0:T(8,128)(2,1)} %texts_ref.5), channel_id=1, source_target_pairs={{0,1},{1,2},{2,3},{3,4},{4,5},{5,6},{6,7},{7,8},{8,9},{9,10},{10,1... | collective-permute-start | bytes 3096584 | tf_op jit(solution)/shard_map/ppermute | solution.py:16
  2.6 92.1 %collective-permute-start.3 = (bf16[448,1152]{1,0:T(8,128)(2,1)}, bf16[448,1152]{1,0:T(8,128)(2,1)S(1)}, u32[]{:S(2)}, u32[]{:S(2)}) collective-permute-start(bf16[448,1152]{1,0:T(8,128)(2,1)} %images_ref.5), channel_id=1, source_target_pairs={{0,31},{1,0},{2,1},{3,2},{4,3},{5,4},{6,5},{7,6},{8,7},{9,8},{10,9... | collective-permute-start | bytes 3096584 | tf_op jit(solution)/shard_map/ppermute | solution.py:16
  8.3 90.4 %collective-permute-start = (bf16[448,1152]{1,0:T(8,128)(2,1)}, bf16[448,1152]{1,0:T(8,128)(2,1)S(1)}, u32[]{:S(2)}, u32[]{:S(2)}) collective-permute-start(bf16[448,1152]{1,0:T(8,128)(2,1)} %texts_ref.5), channel_id=1, source_target_pairs={{0,32},{32,64},{64,96},{96,128},{128,160},{160,192},{192,224},{224... | collective-permute-start | bytes 3096584 | tf_op jit(solution)/shard_map/ppermute | solution.py:16
  14.3 104.8 %collective-permute-start.1 = (bf16[448,1152]{1,0:T(8,128)(2,1)}, bf16[448,1152]{1,0:T(8,128)(2,1)S(1)}, u32[]{:S(2)}, u32[]{:S(2)}) collective-permute-start(bf16[448,1152]{1,0:T(8,128)(2,1)} %images_ref.5), channel_id=1, source_target_pairs={{0,736},{32,0},{64,32},{96,64},{128,96},{160,128},{192,160},{224,1... | collective-permute-start | bytes 3096584 | tf_op jit(solution)/shard_map/ppermute | solution.py:16
  29.7 1.2 copy-start
  30.9 1.2 copy-start.2
  32.2 0.7 copy-start.4
  32.8 61.8 %copy-start.1 = (bf16[448,1152]{1,0:T(8,128)(2,1)S(1)}, bf16[448,1152]{1,0:T(8,128)(2,1)}, u32[]{:S(2)}) copy-start(bf16[448,1152]{1,0:T(8,128)(2,1)} %images_ref.5) | copy-start | bytes 3096580
  32.8 61.8 %copy-start.3 = (bf16[448,1152]{1,0:T(8,128)(2,1)S(1)}, bf16[448,1152]{1,0:T(8,128)(2,1)}, u32[]{:S(2)}) copy-start(bf16[448,1152]{1,0:T(8,128)(2,1)} %texts_ref.5) | copy-start | bytes 3096580

commit v8 on v7

--- a/solution.py
+++ b/solution.py
@@ -70,31 +70,29 @@
     tgrad_ref[...] = nn(coeff, images)
 
 
-def outer_kernel(
+def outer_text_kernel(scal, images_ref, far_texts_ref, loss_in, igrad_in, loss_ref, igrad_ref):
+    loss, grad = image_side(scal, images_ref[...], far_texts_ref[...])
+    loss_ref[...] = loss_in[...] + loss
+    igrad_ref[...] = igrad_in[...] + grad
+
+
+def middle_kernel(
     scal, images_ref, texts_ref, far_texts_ref, far_images_ref, loss_in, igrad_in, tgrad_in,
-    loss_ref, igrad_ref, tgrad_ref,
+    loss_ref, igrad_out, tgrad_ref, igrad_ref, sem,
 ):
     loss, grad = image_side(scal, images_ref[...], far_texts_ref[...])
     loss_ref[...] = loss_in[...] + loss
-    igrad_ref[...] = igrad_in[...] + grad
+    igrad_ref[...] = (igrad_in[...] + grad).astype(BF16)
+    copy = pltpu.make_async_copy(igrad_ref, igrad_out, sem)
+    copy.start()
     tgrad_ref[...] = tgrad_in[...] + text_side(scal, texts_ref[...], far_images_ref[...])
+    copy.wait()
 
 
-def last_kernel(
-    scal, images_ref, texts_ref, far_texts_ref, far_images_ref, loss_in, igrad_in, tgrad_in,
-    loss_ref, igrad_out, tgrad_out, igrad_ref, tgrad_ref, sems,
-):
-    loss, grad = image_side(scal, images_ref[...], far_texts_ref[...])
-    loss_ref[...] = (loss_in[...] + loss) / (3.0 * loss_in.shape[1])
-    igrad_ref[...] = (igrad_in[...] + grad).astype(BF16)
-    image_copy = pltpu.make_async_copy(igrad_ref, igrad_out, sems.at[0])
-    image_copy.start()
+def last_kernel(scal, texts_ref, far_images_ref, loss_in, tgrad_in, loss_ref, tgrad_ref):
+    loss_ref[...] = loss_in[...] / (3.0 * loss_in.shape[1])
     grad = text_side(scal, texts_ref[...], far_images_ref[...])
     tgrad_ref[...] = (tgrad_in[...] + grad).astype(BF16)
-    text_copy = pltpu.make_async_copy(tgrad_ref, tgrad_out, sems.at[1])
-    text_copy.start()
-    image_copy.wait()
-    text_copy.wait()
 
 
 def call(kernel, outs, scalars, *args, out_specs=None, scratch=()):
@@ -120,17 +118,20 @@
     loss_shape = jax.ShapeDtypeStruct((1, rows), F32)
     wide = jax.ShapeDtypeStruct((rows, width), F32)
     narrow = jax.ShapeDtypeStruct((rows, width), BF16)
-    sums = call(own_kernel, [loss_shape, wide, wide], [scal], positive_index, images, texts)
-    sums = call(
-        outer_kernel, [loss_shape, wide, wide], [scal], images, texts, pod_text, pod_images, *sums
+    loss, igrad, tgrad = call(
+        own_kernel, [loss_shape, wide, wide], [scal], positive_index, images, texts
     )
-    away = pl.BlockSpec(memory_space=pl.ANY)
-    held = pltpu.VMEM((rows, width), BF16)
+    loss, igrad = call(
+        outer_text_kernel, [loss_shape, wide], [scal], images, pod_text, loss, igrad
+    )
     loss, igrad, tgrad = call(
-        last_kernel, [loss_shape, narrow, narrow], [scal],
-        images, texts, cycle_text, cycle_images, *sums,
-        out_specs=[VMEM, away, away],
-        scratch=[held, held, pltpu.SemaphoreType.DMA((2,))],
+        middle_kernel, [loss_shape, narrow, wide], [scal],
+        images, texts, cycle_text, pod_images, loss, igrad, tgrad,
+        out_specs=[VMEM, pl.BlockSpec(memory_space=pl.ANY), VMEM],
+        scratch=[pltpu.VMEM((rows, width), BF16), pltpu.SemaphoreType.DMA(())],
+    )
+    loss, tgrad = call(
+        last_kernel, [loss_shape, narrow], [scal], texts, cycle_images, loss, tgrad
     )
     return loss.reshape(rows), igrad, tgrad
 

time: 125 us -> 124 us (level)
  the two profiles are of different devices: /device:TPU:16 before, /device:TPU:24 now
where the time goes in v8:
time: 124 us; the launch traced here: 123 us
  waiting for transfers between devices  78.1 us (63%)
  starting transfers between devices  26.8 us (22%)
  Pallas kernels  13.3 us (11%)
  local copies, waits for them, and re-layouts  3.13 us (3%)
  between operations  2.02 us (2%)
    ppermute x4, waiting for transfers between devices, passed_along(): lax.ppermute(x, axis, [(i, (i + by) % devices) for i in range(devices)])  78.1 us
    ppermute x4, starting transfers between devices, passed_along(): lax.ppermute(x, axis, [(i, (i + by) % devices) for i in range(devices)])  26.8 us
    pallas_call x4, Pallas kernels, call(): pl.pallas_call(kernel, out_shape=outs, in_specs=[SMEM] * len(scalars) + [...  13.3 us
    unnamed x10, local copies, waits for them, and re-layouts  3.13 us
  transfers between devices with their start and end apart: 4, of which 3 were waited for; matrix products, arithmetic and copies ran while one was open for 0% of the time, Pallas kernels for 8%

profile of v8, /device:TPU:24, one launch (start us, length us, event | category | flops | bytes accessed | tf_op | source)
XLA Modules:
  0.0 123.4 jit_solution(1097084010514184128)
XLA Ops:
  0.6 1.9 %collective-permute-start.3 = (bf16[448,1152]{1,0:T(8,128)(2,1)}, bf16[448,1152]{1,0:T(8,128)(2,1)S(1)}, u32[]{:S(2)}, u32[]{:S(2)}) collective-permute-start(bf16[448,1152]{1,0:T(8,128)(2,1)} %texts_ref.5), channel_id=1, source_target_pairs={{0,1},{1,2},{2,3},{3,4},{4,5},{5,6},{6,7},{7,8},{8,9},{9,10},{10,1... | collective-permute-start | bytes 3096584 | tf_op jit(solution)/shard_map/ppermute | solution.py:16
  2.6 5.0 %collective-permute-start.1 = (bf16[448,1152]{1,0:T(8,128)(2,1)}, bf16[448,1152]{1,0:T(8,128)(2,1)S(1)}, u32[]{:S(2)}, u32[]{:S(2)}) collective-permute-start(bf16[448,1152]{1,0:T(8,128)(2,1)} %texts_ref.5), channel_id=1, source_target_pairs={{0,32},{32,64},{64,96},{96,128},{128,160},{160,192},{192,224},{224... | collective-permute-start | bytes 3096584 | tf_op jit(solution)/shard_map/ppermute | solution.py:16
  7.6 5.5 %collective-permute-start.2 = (bf16[448,1152]{1,0:T(8,128)(2,1)}, bf16[448,1152]{1,0:T(8,128)(2,1)S(1)}, u32[]{:S(2)}, u32[]{:S(2)}) collective-permute-start(bf16[448,1152]{1,0:T(8,128)(2,1)} %images_ref.5), channel_id=1, source_target_pairs={{0,31},{1,0},{2,1},{3,2},{4,3},{5,4},{6,5},{7,6},{8,7},{9,8},{10,9... | collective-permute-start | bytes 3096584 | tf_op jit(solution)/shard_map/ppermute | solution.py:16
  13.1 14.3 %collective-permute-start = (bf16[448,1152]{1,0:T(8,128)(2,1)}, bf16[448,1152]{1,0:T(8,128)(2,1)S(1)}, u32[]{:S(2)}, u32[]{:S(2)}) collective-permute-start(bf16[448,1152]{1,0:T(8,128)(2,1)} %images_ref.5), channel_id=1, source_target_pairs={{0,736},{32,0},{64,32},{96,64},{128,96},{160,128},{192,160},{224,1... | collective-permute-start | bytes 3096584 | tf_op jit(solution)/shard_map/ppermute | solution.py:16
  28.7 0.1 pad_maximum_fusion.scal
  28.8 0.0 copy-start
  28.8 1.2 copy-done
  30.0 0.0 copy-start.2
  30.0 1.2 copy-done.2
  31.3 0.0 copy-start.4
  31.3 0.7 copy-done.4
  31.9 0.0 copy-start.1
  31.9 3.4 %shard_map.76 = (f32[1,448]{1,0:T(1,128)S(1)}, f32[448,1152]{1,0:T(8,128)S(1)}, f32[448,1152]{1,0:T(8,128)S(1)}) custom-call(f32[2]{0:T(128)S(1)} %pad_maximum_fusion.scal, s32[1,448]{1,0:T(1,128)S(1)} %copy-done.4, bf16[448,1152]{1,0:T(8,128)(2,1)S(1)} %copy-done, bf16[448,1152]{1,0:T(8,128)(2,1)S(1)} %copy-done.2), custom_call_target="tpu_custom_call" | custom-call | flops 1000 | bytes 1000 | tf_op jit(solution)/shard_map/pallas_call | solution.py:99
  35.3 46.8 %collective-permute-done.3.far_texts_ref = bf16[448,1152]{1,0:T(8,128)(2,1)S(1)} collective-permute-done((bf16[448,1152]{1,0:T(8,128)(2,1)}, bf16[448,1152]{1,0:T(8,128)(2,1)S(1)}, u32[]{:S(2)}, u32[]{:S(2)}) %collective-permute-start.3) | collective-permute-done | bytes 1032224 | tf_op jit(solution)/shard_map/ppermute | solution.py:16
  82.1 0.0 copy-done.1
  82.1 0.0 copy-start.3
  82.1 2.6 %shard_map.77 = (f32[1,448]{1,0:T(1,128)S(1)}, f32[448,1152]{1,0:T(8,128)S(1)}) custom-call(f32[2]{0:T(128)S(1)} %pad_maximum_fusion.scal, bf16[448,1152]{1,0:T(8,128)(2,1)S(1)} %copy-done.1, bf16[448,1152]{1,0:T(8,128)(2,1)S(1)} %collective-permute-done.3.far_texts_ref, f32[1,448]{1,0:T(1,128)S(1)} %get-tuple-element.13.loss_in, ...), custom_call_target="tpu_custom_call" | custom-call | flops 1000 | bytes 1000 | tf_op jit(solution)/shard_map/pallas_call | solution.py:99
  84.7 0.0 collective-permute-done.1.far_texts_ref
  84.7 24.5 %collective-permute-done.2.far_images_ref = bf16[448,1152]{1,0:T(8,128)(2,1)S(1)} collective-permute-done((bf16[448,1152]{1,0:T(8,128)(2,1)}, bf16[448,1152]{1,0:T(8,128)(2,1)S(1)}, u32[]{:S(2)}, u32[]{:S(2)}) %collective-permute-start.2) | collective-permute-done | bytes 1032224 | tf_op jit(solution)/shard_map/ppermute | solution.py:16
  109.3 0.0 copy-done.3
  109.3 4.1 %shard_map.78 = (f32[1,448]{1,0:T(1,128)S(1)}, bf16[448,1152]{1,0:T(8,128)(2,1)}, f32[448,1152]{1,0:T(8,128)S(1)}) custom-call(f32[2]{0:T(128)S(1)} %pad_maximum_fusion.scal, bf16[448,1152]{1,0:T(8,128)(2,1)S(1)} %copy-done.1, bf16[448,1152]{1,0:T(8,128)(2,1)S(1)} %copy-done.3, bf16[448,1152]{1,0:T(8,128)(2,1)S(1)} %collective-permute-done.1.far_texts_ref, ...), custom_call_target="tpu_custom_call" | custom-call | flops 1000 | bytes 1000 | tf_op jit(solution)/shard_map/pallas_call | solution.py:99
  113.4 6.8 %collective-permute-done.far_images_ref = bf16[448,1152]{1,0:T(8,128)(2,1)S(1)} collective-permute-done((bf16[448,1152]{1,0:T(8,128)(2,1)}, bf16[448,1152]{1,0:T(8,128)(2,1)S(1)}, u32[]{:S(2)}, u32[]{:S(2)}) %collective-permute-start) | collective-permute-done | bytes 1032224 | tf_op jit(solution)/shard_map/ppermute | solution.py:16
  120.2 3.2 %shard_map.79 = (f32[1,448]{1,0:T(1,128)}, bf16[448,1152]{1,0:T(8,128)(2,1)}) custom-call(f32[2]{0:T(128)S(1)} %pad_maximum_fusion.scal, bf16[448,1152]{1,0:T(8,128)(2,1)S(1)} %copy-done.3, bf16[448,1152]{1,0:T(8,128)(2,1)S(1)} %collective-permute-done.far_images_ref, f32[1,448]{1,0:T(1,128)S(1)} %get-tuple-element.18.loss_in, ...), custom_call_target="tpu_custom_call" | custom-call | flops 1000 | bytes 1000 | tf_op jit(solution)/shard_map/pallas_call | solution.py:99
Async XLA Ops:
  0.6 81.5 %collective-permute-start.3 = (bf16[448,1152]{1,0:T(8,128)(2,1)}, bf16[448,1152]{1,0:T(8,128)(2,1)S(1)}, u32[]{:S(2)}, u32[]{:S(2)}) collective-permute-start(bf16[448,1152]{1,0:T(8,128)(2,1)} %texts_ref.5), channel_id=1, source_target_pairs={{0,1},{1,2},{2,3},{3,4},{4,5},{5,6},{6,7},{7,8},{8,9},{9,10},{10,1... | collective-permute-start | bytes 3096584 | tf_op jit(solution)/shard_map/ppermute | solution.py:16
  2.6 82.2 %collective-permute-start.1 = (bf16[448,1152]{1,0:T(8,128)(2,1)}, bf16[448,1152]{1,0:T(8,128)(2,1)S(1)}, u32[]{:S(2)}, u32[]{:S(2)}) collective-permute-start(bf16[448,1152]{1,0:T(8,128)(2,1)} %texts_ref.5), channel_id=1, source_target_pairs={{0,32},{32,64},{64,96},{96,128},{128,160},{160,192},{192,224},{224... | collective-permute-start | bytes 3096584 | tf_op jit(solution)/shard_map/ppermute | solution.py:16
  7.6 101.7 %collective-permute-start.2 = (bf16[448,1152]{1,0:T(8,128)(2,1)}, bf16[448,1152]{1,0:T(8,128)(2,1)S(1)}, u32[]{:S(2)}, u32[]{:S(2)}) collective-permute-start(bf16[448,1152]{1,0:T(8,128)(2,1)} %images_ref.5), channel_id=1, source_target_pairs={{0,31},{1,0},{2,1},{3,2},{4,3},{5,4},{6,5},{7,6},{8,7},{9,8},{10,9... | collective-permute-start | bytes 3096584 | tf_op jit(solution)/shard_map/ppermute | solution.py:16
  13.1 107.1 %collective-permute-start = (bf16[448,1152]{1,0:T(8,128)(2,1)}, bf16[448,1152]{1,0:T(8,128)(2,1)S(1)}, u32[]{:S(2)}, u32[]{:S(2)}) collective-permute-start(bf16[448,1152]{1,0:T(8,128)(2,1)} %images_ref.5), channel_id=1, source_target_pairs={{0,736},{32,0},{64,32},{96,64},{128,96},{160,128},{192,160},{224,1... | collective-permute-start | bytes 3096584 | tf_op jit(solution)/shard_map/ppermute | solution.py:16
  28.8 1.2 copy-start
  30.0 1.2 copy-start.2
  31.3 0.7 copy-start.4
  31.9 50.2 %copy-start.1 = (bf16[448,1152]{1,0:T(8,128)(2,1)S(1)}, bf16[448,1152]{1,0:T(8,128)(2,1)}, u32[]{:S(2)}) copy-start(bf16[448,1152]{1,0:T(8,128)(2,1)} %images_ref.5) | copy-start | bytes 3096580
  82.1 27.2 %copy-start.3 = (bf16[448,1152]{1,0:T(8,128)(2,1)S(1)}, bf16[448,1152]{1,0:T(8,128)(2,1)}, u32[]{:S(2)}) copy-start(bf16[448,1152]{1,0:T(8,128)(2,1)} %texts_ref.5) | copy-start | bytes 3096580

commit v9 on v7

--- a/solution.py
+++ b/solution.py
@@ -71,13 +71,23 @@
 
 
 def outer_kernel(
-    scal, images_ref, texts_ref, far_texts_ref, far_images_ref, loss_in, igrad_in, tgrad_in,
+    scal, role, images_ref, texts_ref, pair_ref, loss_in, igrad_in, tgrad_in,
     loss_ref, igrad_ref, tgrad_ref,
 ):
-    loss, grad = image_side(scal, images_ref[...], far_texts_ref[...])
-    loss_ref[...] = loss_in[...] + loss
-    igrad_ref[...] = igrad_in[...] + grad
-    tgrad_ref[...] = tgrad_in[...] + text_side(scal, texts_ref[...], far_images_ref[...])
+    far_ref = pair_ref.at[role[1]]
+    loss_ref[...] = loss_in[...]
+
+    @pl.when(role[0] != 0)
+    def _():
+        loss, grad = image_side(scal, images_ref[...], far_ref[...])
+        loss_ref[...] += loss
+        igrad_ref[...] = igrad_in[...] + grad
+        tgrad_ref[...] = tgrad_in[...]
+
+    @pl.when(role[0] == 0)
+    def _():
+        igrad_ref[...] = igrad_in[...]
+        tgrad_ref[...] = tgrad_in[...] + text_side(scal, texts_ref[...], far_ref[...])
 
 
 def last_kernel(
@@ -111,19 +121,30 @@
 
 def local(images, texts, positive_index, log_scale, bias):
     rows, width = images.shape
+    outer = lax.axis_size("outer")
+    core = lax.axis_index("outer") % 2
     scal = jnp.concatenate([jnp.exp(log_scale), bias])
-    pod_text = passed_along(texts, "outer", 1)
-    pod_images = passed_along(images, "outer", -1)
     cycle_text = passed_along(texts, "dp", 1)
     cycle_images = passed_along(images, "dp", -1)
+    chips = [[o, o + 1] for o in range(0, outer, 2)]
+    links = [[o, (o + 1) % outer] for o in range(1, outer, 2)]
+    even = core == 0
+    link_pair = lax.all_gather(
+        jnp.where(even, images, texts), "outer", axis_index_groups=links
+    )
+    chip_pair = lax.all_gather(
+        jnp.where(even, texts, images), "outer", axis_index_groups=chips
+    )
 
     loss_shape = jax.ShapeDtypeStruct((1, rows), F32)
     wide = jax.ShapeDtypeStruct((rows, width), F32)
     narrow = jax.ShapeDtypeStruct((rows, width), BF16)
     sums = call(own_kernel, [loss_shape, wide, wide], [scal], positive_index, images, texts)
-    sums = call(
-        outer_kernel, [loss_shape, wide, wide], [scal], images, texts, pod_text, pod_images, *sums
-    )
+    for pair, role in ((chip_pair, [core, 1 - core]), (link_pair, [1 - core, core])):
+        role = jnp.stack(role).astype(jnp.int32)
+        sums = call(
+            outer_kernel, [loss_shape, wide, wide], [scal, role], images, texts, pair, *sums
+        )
     away = pl.BlockSpec(memory_space=pl.ANY)
     held = pltpu.VMEM((rows, width), BF16)
     loss, igrad, tgrad = call(

time: 125 us -> 147 us (1.18)
  the two profiles are of different devices: /device:TPU:16 before, /device:TPU:32 now
where the time goes in v9:
time: 147 us; the launch traced here: 146 us
  waiting for transfers between devices  84.3 us (57%)
  between operations  15.5 us (11%)
  local copies, waits for them, and re-layouts  15.2 us (10%)
  Pallas kernels  14.9 us (10%)
  starting transfers between devices  13 us (9%)
  other arithmetic  3.17 us (2%)
    all_gather x1, waiting for transfers between devices, local(): lax.all_gather(jnp.where(even, images, texts), 'outer', axis_index_groups...  76.9 us
    unnamed x26, local copies, waits for them, and re-layouts  15.2 us
    pallas_call x4, Pallas kernels, call(): pl.pallas_call(kernel, out_shape=outs, in_specs=[SMEM] * len(scalars) + [...  14.9 us
    ppermute x2, starting transfers between devices, passed_along(): lax.ppermute(x, axis, [(i, (i + by) % devices) for i in range(devices)])  12.9 us
    all_gather x1, waiting for transfers between devices, local(): lax.all_gather(jnp.where(even, texts, images), 'outer', axis_index_groups...  6.75 us
    select_n x1, other arithmetic, local(): jnp.where(even, texts, images)  3.02 us
  transfers between devices with their start and end apart: 4, of which 2 were waited for; matrix products, arithmetic and copies ran while one was open for 0% of the time, Pallas kernels for 6%

profile of v9, /device:TPU:32, one launch (start us, length us, event | category | flops | bytes accessed | tf_op | source)
XLA Modules:
  0.0 146.2 jit_solution(17578186164010506310)
XLA Ops:
  7.2 0.0 all-gather.7.cloned.1.call-start
  7.2 3.0 %broadcast_select_fusion = (bf16[448,1152]{1,0:T(8,128)(2,1)}, bf16[448,1152]{1,0:T(8,128)(2,1)}) fusion(bf16[448,1152]{1,0:T(8,128)(2,1)} %texts_ref.7, bf16[448,1152]{1,0:T(8,128)(2,1)} %images_ref.7, pred[]{:T(512)S(6)} %eq.5), kind=kLoop, calls=%fused_computation | loop fusion | flops 1032192 | bytes 4128769 | tf_op jit(solution)/shard_map/jit(_where)/select_n | solution.py:136
  10.2 0.0 copy-start.1
  10.2 0.0 copy-start
  10.2 0.0 copy-start.12
  10.3 0.0 all-gather.7.cloned.1.call-update
  10.3 0.0 all-gather.5.cloned.1.call-start
  10.3 0.7 all-gather.5.cloned.1.call-update
  11.0 0.4 copy-done.1
  11.5 3.8 %collective-permute-start = (bf16[448,1152]{1,0:T(8,128)(2,1)S(1)}, bf16[448,1152]{1,0:T(8,128)(2,1)S(1)}, u32[]{:S(2)}, u32[]{:S(2)}) collective-permute-start(bf16[448,1152]{1,0:T(8,128)(2,1)S(1)} %copy-done.1), channel_id=1, source_target_pairs={{0,32},{32,64},{64,96},{96,128},{128,160},{160,192},{192,224},{224... | collective-permute-start | bytes 3096584 | tf_op jit(solution)/shard_map/ppermute | solution.py:16
  15.3 0.0 copy-done
  15.3 9.1 %collective-permute-start.1 = (bf16[448,1152]{1,0:T(8,128)(2,1)S(1)}, bf16[448,1152]{1,0:T(8,128)(2,1)}, u32[]{:S(2)}, u32[]{:S(2)}) collective-permute-start(bf16[448,1152]{1,0:T(8,128)(2,1)S(1)} %copy-done), channel_id=1, source_target_pairs={{0,736},{32,0},{64,32},{96,64},{128,96},{160,128},{192,160},{224,1... | collective-permute-start | bytes 3096584 | tf_op jit(solution)/shard_map/ppermute | solution.py:16
  25.8 0.1 pad_maximum_fusion.scal
  25.8 0.0 copy-done.12
  25.8 3.4 %shard_map.76 = (f32[1,448]{1,0:T(1,128)S(1)}, f32[448,1152]{1,0:T(8,128)S(1)}, f32[448,1152]{1,0:T(8,128)S(1)}) custom-call(f32[2]{0:T(128)S(1)} %pad_maximum_fusion.scal, s32[1,448]{1,0:T(1,128)S(1)} %copy-done.12, bf16[448,1152]{1,0:T(8,128)(2,1)S(1)} %copy-done, bf16[448,1152]{1,0:T(8,128)(2,1)S(1)} %copy-done.1), custom_call_target="tpu_custom_call" | custom-call | flops 1000 | bytes 1000 | tf_op jit(solution)/shard_map/pallas_call | solution.py:111
  29.2 0.0 copy-start.4
  29.2 1.3 copy-done.4
  30.6 0.0 copy-start.6
  30.6 1.3 copy-done.6
  31.9 0.1 pad_add_fusion
  32.0 6.7 %all-gather.7.cloned.1.call-done = bf16[896,1152]{1,0:T(8,128)(2,1)} async-done(((bf16[448,1152]{1,0:T(8,128)(2,1)}), bf16[896,1152]{1,0:T(8,128)(2,1)}) %all-gather.7.cloned.1.call-update) | async-done | bytes 2064400 | tf_op jit(solution)/shard_map/all_gather | solution.py:135
  38.8 0.0 copy-start.3
  38.8 1.6 %copy-done.3 = bf16[896,1152]{1,0:T(8,128)(2,1)S(1)} copy-done((bf16[896,1152]{1,0:T(8,128)(2,1)S(1)}, bf16[896,1152]{1,0:T(8,128)(2,1)}, u32[]{:S(2)}) %copy-start.3) | copy-done | bytes 2064408
  40.3 0.0 copy-start.5
  40.3 1.6 %copy-done.5 = f32[448,1152]{1,0:T(8,128)S(1)} copy-done((f32[448,1152]{1,0:T(8,128)S(1)}, f32[448,1152]{1,0:T(8,128)}, u32[]{:S(2)}) %copy-start.5) | copy-done | bytes 2064408
  41.9 0.0 copy-start.7
  41.9 1.6 %copy-done.7 = f32[448,1152]{1,0:T(8,128)S(1)} copy-done((f32[448,1152]{1,0:T(8,128)S(1)}, f32[448,1152]{1,0:T(8,128)}, u32[]{:S(2)}) %copy-start.7) | copy-done | bytes 2064408
  43.5 2.4 %shard_map.77 = (f32[1,448]{1,0:T(1,128)S(1)}, f32[448,1152]{1,0:T(8,128)S(1)}, f32[448,1152]{1,0:T(8,128)S(1)}) custom-call(f32[2]{0:T(128)S(1)} %pad_maximum_fusion.scal, s32[2]{0:T(128)S(1)} %get-tuple-element.30.role, bf16[448,1152]{1,0:T(8,128)(2,1)S(1)} %copy-done, bf16[448,1152]{1,0:T(8,128)(2,1)S(1)} %copy-done.1, bf16[2,448,1152]{2,1,0:T(8,128)(2,1)S(1)} %bitcast.6, ...), custom_call_target="tpu_custom_call" | custom-call | flops 1000 | bytes 1000 | tf_op jit(solution)/shard_map/pallas_call | solution.py:111
  45.9 0.0 copy-start.8
  45.9 1.3 copy-done.8
  47.2 0.0 copy-start.10
  47.2 1.3 copy-done.10
  48.5 76.9 %all-gather.5.cloned.1.call-done = bf16[896,1152]{1,0:T(8,128)(2,1)} async-done(((bf16[448,1152]{1,0:T(8,128)(2,1)}), bf16[896,1152]{1,0:T(8,128)(2,1)}) %all-gather.5.cloned.1.call-update) | async-done | bytes 2064400 | tf_op jit(solution)/shard_map/all_gather | solution.py:132
  125.4 0.0 copy-start.2
  125.4 1.6 %copy-done.2 = bf16[896,1152]{1,0:T(8,128)(2,1)S(1)} copy-done((bf16[896,1152]{1,0:T(8,128)(2,1)S(1)}, bf16[896,1152]{1,0:T(8,128)(2,1)}, u32[]{:S(2)}) %copy-start.2) | copy-done | bytes 2064408
  127.0 0.0 copy-start.9
  127.0 1.6 %copy-done.9 = f32[448,1152]{1,0:T(8,128)S(1)} copy-done((f32[448,1152]{1,0:T(8,128)S(1)}, f32[448,1152]{1,0:T(8,128)}, u32[]{:S(2)}) %copy-start.9) | copy-done | bytes 2064408
  128.5 0.0 copy-start.11
  128.5 1.6 %copy-done.11 = f32[448,1152]{1,0:T(8,128)S(1)} copy-done((f32[448,1152]{1,0:T(8,128)S(1)}, f32[448,1152]{1,0:T(8,128)}, u32[]{:S(2)}) %copy-start.11) | copy-done | bytes 2064408
  130.1 2.9 %shard_map.78 = (f32[1,448]{1,0:T(1,128)S(1)}, f32[448,1152]{1,0:T(8,128)S(1)}, f32[448,1152]{1,0:T(8,128)S(1)}) custom-call(f32[2]{0:T(128)S(1)} %pad_maximum_fusion.scal, s32[2]{0:T(128)S(1)} %get-tuple-element.29.role, bf16[448,1152]{1,0:T(8,128)(2,1)S(1)} %copy-done, bf16[448,1152]{1,0:T(8,128)(2,1)S(1)} %copy-done.1, bf16[2,448,1152]{2,1,0:T(8,128)(2,1)S(1)} %bitcast.5, ...), custom_call_target="tpu_custom_call" | custom-call | flops 1000 | bytes 1000 | tf_op jit(solution)/shard_map/pallas_call | solution.py:111
  133.0 0.0 collective-permute-done.far_texts_ref
  133.0 0.0 collective-permute-done.1.far_images_ref
  133.0 6.3 %shard_map.79 = (f32[1,448]{1,0:T(1,128)}, bf16[448,1152]{1,0:T(8,128)(2,1)}, bf16[448,1152]{1,0:T(8,128)(2,1)}) custom-call(f32[2]{0:T(128)S(1)} %pad_maximum_fusion.scal, bf16[448,1152]{1,0:T(8,128)(2,1)S(1)} %copy-done, bf16[448,1152]{1,0:T(8,128)(2,1)S(1)} %copy-done.1, bf16[448,1152]{1,0:T(8,128)(2,1)S(1)} %collective-permute-done.far_texts_ref, ...), custom_call_target="tpu_custom_call" | custom-call | flops 1000 | bytes 1000 | tf_op jit(solution)/shard_map/pallas_call | solution.py:111
Async XLA Ops:
  7.2 31.6 %all-gather.7.cloned.1.call-start = ((), (), s32[]{:S(2)}) async-start(), calls=%async_computation.1 | async-start | bytes 3096576 | tf_op jit(solution)/shard_map/all_gather | solution.py:135
  10.2 1.2 copy-start.1
  10.2 5.0 %copy-start = (bf16[448,1152]{1,0:T(8,128)(2,1)S(1)}, bf16[448,1152]{1,0:T(8,128)(2,1)}, u32[]{:S(2)}) copy-start(bf16[448,1152]{1,0:T(8,128)(2,1)} %images_ref.7) | copy-start | bytes 3096580
  10.2 15.6 %copy-start.12 = (s32[1,448]{1,0:T(1,128)S(1)}, s32[1,448]{1,0:T(1,128)}, u32[]{:S(2)}) copy-start(s32[1,448]{1,0:T(1,128)} %pos_ref.1) | copy-start | bytes 5380
  10.3 115.1 %all-gather.5.cloned.1.call-start = ((), (), s32[]{:S(2)}) async-start(), calls=%async_computation | async-start | bytes 3096576 | tf_op jit(solution)/shard_map/all_gather | solution.py:132
  11.5 121.5 %collective-permute-start = (bf16[448,1152]{1,0:T(8,128)(2,1)S(1)}, bf16[448,1152]{1,0:T(8,128)(2,1)S(1)}, u32[]{:S(2)}, u32[]{:S(2)}) collective-permute-start(bf16[448,1152]{1,0:T(8,128)(2,1)S(1)} %copy-done.1), channel_id=1, source_target_pairs={{0,32},{32,64},{64,96},{96,128},{128,160},{160,192},{192,224},{224... | collective-permute-start | bytes 3096584 | tf_op jit(solution)/shard_map/ppermute | solution.py:16
  15.3 117.7 %collective-permute-start.1 = (bf16[448,1152]{1,0:T(8,128)(2,1)S(1)}, bf16[448,1152]{1,0:T(8,128)(2,1)}, u32[]{:S(2)}, u32[]{:S(2)}) collective-permute-start(bf16[448,1152]{1,0:T(8,128)(2,1)S(1)} %copy-done), channel_id=1, source_target_pairs={{0,736},{32,0},{64,32},{96,64},{128,96},{160,128},{192,160},{224,1... | collective-permute-start | bytes 3096584 | tf_op jit(solution)/shard_map/ppermute | solution.py:16
  29.2 1.3 copy-start.4
  30.6 1.4 copy-start.6
  38.8 1.6 %copy-start.3 = (bf16[896,1152]{1,0:T(8,128)(2,1)S(1)}, bf16[896,1152]{1,0:T(8,128)(2,1)}, u32[]{:S(2)}) copy-start(bf16[896,1152]{1,0:T(8,128)(2,1)} %all-gather.7.cloned.1.call-done) | copy-start | bytes 6193156
  40.3 1.6 %copy-start.5 = (f32[448,1152]{1,0:T(8,128)S(1)}, f32[448,1152]{1,0:T(8,128)}, u32[]{:S(2)}) copy-start(f32[448,1152]{1,0:T(8,128)} %copy-done.4) | copy-start | bytes 6193156
  41.9 1.6 %copy-start.7 = (f32[448,1152]{1,0:T(8,128)S(1)}, f32[448,1152]{1,0:T(8,128)}, u32[]{:S(2)}) copy-start(f32[448,1152]{1,0:T(8,128)} %copy-done.6) | copy-start | bytes 6193156
  45.9 1.3 copy-start.8
  47.2 1.3 copy-start.10
  125.4 1.6 %copy-start.2 = (bf16[896,1152]{1,0:T(8,128)(2,1)S(1)}, bf16[896,1152]{1,0:T(8,128)(2,1)}, u32[]{:S(2)}) copy-start(bf16[896,1152]{1,0:T(8,128)(2,1)} %all-gather.5.cloned.1.call-done) | copy-start | bytes 6193156
  127.0 1.6 %copy-start.9 = (f32[448,1152]{1,0:T(8,128)S(1)}, f32[448,1152]{1,0:T(8,128)}, u32[]{:S(2)}) copy-start(f32[448,1152]{1,0:T(8,128)} %copy-done.8) | copy-start | bytes 6193156
  128.5 1.6 %copy-start.11 = (f32[448,1152]{1,0:T(8,128)S(1)}, f32[448,1152]{1,0:T(8,128)}, u32[]{:S(2)}) copy-start(f32[448,1152]{1,0:T(8,128)} %copy-done.10) | copy-start | bytes 6193156
Sparse Core Ops, SparseCore 0:
  11.0 27.7 all-gather.6
  41.7 83.6 all-gather.4

commit v10 on v8

--- a/solution.py
+++ b/solution.py
@@ -70,23 +70,67 @@
     tgrad_ref[...] = nn(coeff, images)
 
 
-def outer_text_kernel(scal, images_ref, far_texts_ref, loss_in, igrad_in, loss_ref, igrad_ref):
+def pick_kernel(role, images_ref, texts_ref, out_ref, sem):
+    @pl.when(role[0] != 0)
+    def _():
+        copy = pltpu.make_async_copy(texts_ref, out_ref, sem)
+        copy.start()
+        copy.wait()
+
+    @pl.when(role[0] == 0)
+    def _():
+        copy = pltpu.make_async_copy(images_ref, out_ref, sem)
+        copy.start()
+        copy.wait()
+
+
+def link_kernel(
+    scal, role, images_ref, texts_ref, far_ref, loss_in, igrad_in, tgrad_in,
+    loss_ref, igrad_ref, tgrad_ref,
+):
+    @pl.when(role[0] == 0)
+    def _():
+        loss, grad = image_side(scal, images_ref[...], far_ref[...])
+        loss_ref[...] = loss_in[...] + loss
+        igrad_ref[...] = igrad_in[...] + grad
+        tgrad_ref[...] = tgrad_in[...]
+
+    @pl.when(role[0] != 0)
+    def _():
+        loss_ref[...] = loss_in[...]
+        igrad_ref[...] = igrad_in[...]
+        tgrad_ref[...] = tgrad_in[...] + text_side(scal, texts_ref[...], far_ref[...])
+
+
+def dp_text_kernel(scal, images_ref, far_texts_ref, loss_in, igrad_in, loss_ref, igrad_ref):
     loss, grad = image_side(scal, images_ref[...], far_texts_ref[...])
     loss_ref[...] = loss_in[...] + loss
     igrad_ref[...] = igrad_in[...] + grad
 
 
-def middle_kernel(
-    scal, images_ref, texts_ref, far_texts_ref, far_images_ref, loss_in, igrad_in, tgrad_in,
+def chip_kernel(
+    scal, role, images_ref, texts_ref, far_ref, loss_in, igrad_in, tgrad_in,
     loss_ref, igrad_out, tgrad_ref, igrad_ref, sem,
 ):
-    loss, grad = image_side(scal, images_ref[...], far_texts_ref[...])
-    loss_ref[...] = loss_in[...] + loss
-    igrad_ref[...] = (igrad_in[...] + grad).astype(BF16)
-    copy = pltpu.make_async_copy(igrad_ref, igrad_out, sem)
-    copy.start()
-    tgrad_ref[...] = tgrad_in[...] + text_side(scal, texts_ref[...], far_images_ref[...])
-    copy.wait()
+    def send():
+        return pltpu.make_async_copy(igrad_ref, igrad_out, sem)
+
+    @pl.when(role[0] != 0)
+    def _():
+        loss, grad = image_side(scal, images_ref[...], far_ref[...])
+        loss_ref[...] = loss_in[...] + loss
+        igrad_ref[...] = (igrad_in[...] + grad).astype(BF16)
+        send().start()
+        tgrad_ref[...] = tgrad_in[...]
+
+    @pl.when(role[0] == 0)
+    def _():
+        loss_ref[...] = loss_in[...]
+        igrad_ref[...] = igrad_in[...].astype(BF16)
+        send().start()
+        tgrad_ref[...] = tgrad_in[...] + text_side(scal, texts_ref[...], far_ref[...])
+
+    send().wait()
 
 
 def last_kernel(scal, texts_ref, far_images_ref, loss_in, tgrad_in, loss_ref, tgrad_ref):
@@ -95,39 +139,54 @@
     tgrad_ref[...] = (tgrad_in[...] + grad).astype(BF16)
 
 
-def call(kernel, outs, scalars, *args, out_specs=None, scratch=()):
+def call(kernel, outs, scalars, *args, in_specs=None, out_specs=None, scratch=(), room=40):
     return pl.pallas_call(
         kernel,
         out_shape=outs,
-        in_specs=[SMEM] * len(scalars) + [VMEM] * len(args),
+        in_specs=[SMEM] * len(scalars) + (in_specs or [VMEM] * len(args)),
         out_specs=out_specs or [VMEM] * len(outs),
         scratch_shapes=scratch,
-        compiler_params=pltpu.CompilerParams(vmem_limit_bytes=40 * 1024 * 1024),
+        compiler_params=pltpu.CompilerParams(vmem_limit_bytes=room * 1024 * 1024),
         cost_estimate=pl.CostEstimate(flops=1000, bytes_accessed=1000, transcendentals=0),
     )(*scalars, *args)
 
 
 def local(images, texts, positive_index, log_scale, bias):
     rows, width = images.shape
+    outer = lax.axis_size("outer")
+    core = lax.axis_index("outer") % 2
+    role = core.astype(jnp.int32).reshape(1)
     scal = jnp.concatenate([jnp.exp(log_scale), bias])
-    pod_text = passed_along(texts, "outer", 1)
-    pod_images = passed_along(images, "outer", -1)
-    cycle_text = passed_along(texts, "dp", 1)
-    cycle_images = passed_along(images, "dp", -1)
-
     loss_shape = jax.ShapeDtypeStruct((1, rows), F32)
     wide = jax.ShapeDtypeStruct((rows, width), F32)
     narrow = jax.ShapeDtypeStruct((rows, width), BF16)
+    away = pl.BlockSpec(memory_space=pl.ANY)
+
+    def swap(x, shift):
+        pairs = [((o + shift) % outer, (o + 1 + shift) % outer) for o in range(0, outer, 2)]
+        return lax.ppermute(x, "outer", pairs + [(b, a) for a, b in pairs])
+
+    (over_link,) = call(
+        pick_kernel, [narrow], [role], images, texts,
+        in_specs=[away, away], scratch=[pltpu.SemaphoreType.DMA(())], room=40,
+    )
+    over_link, texts, images = lax.optimization_barrier((over_link, texts, images))
+    link = swap(over_link, 1)
+    cycle_text = passed_along(texts, "dp", 1)
+    chip = swap(jnp.where(core == 0, texts, images), 0)
+    cycle_images = passed_along(images, "dp", -1)
+
+    sums = call(own_kernel, [loss_shape, wide, wide], [scal], positive_index, images, texts)
     loss, igrad, tgrad = call(
-        own_kernel, [loss_shape, wide, wide], [scal], positive_index, images, texts
+        link_kernel, [loss_shape, wide, wide], [scal, role], images, texts, link, *sums
     )
     loss, igrad = call(
-        outer_text_kernel, [loss_shape, wide], [scal], images, pod_text, loss, igrad
+        dp_text_kernel, [loss_shape, wide], [scal], images, cycle_text, loss, igrad
     )
     loss, igrad, tgrad = call(
-        middle_kernel, [loss_shape, narrow, wide], [scal],
-        images, texts, cycle_text, pod_images, loss, igrad, tgrad,
-        out_specs=[VMEM, pl.BlockSpec(memory_space=pl.ANY), VMEM],
+        chip_kernel, [loss_shape, narrow, wide], [scal, role],
+        images, texts, chip, loss, igrad, tgrad,
+        out_specs=[VMEM, away, VMEM],
         scratch=[pltpu.VMEM((rows, width), BF16), pltpu.SemaphoreType.DMA(())],
     )
     loss, tgrad = call(

time: 124 us -> 126 us (1.016)
  the two profiles are of different devices: /device:TPU:24 before, /device:TPU:63 now
where the time goes in v10:
time: 126 us
  waiting for transfers between devices  84.2 us (67%)
  Pallas kernels  19.5 us (15%)
  starting transfers between devices  18.7 us (15%)
  between operations  2.09 us (2%)
    ppermute x2, waiting for transfers between devices, swap(): return lax.ppermute(x, 'outer', pairs + [(b, a) for a, b in pairs])  43.9 us
    ppermute x2, waiting for transfers between devices, passed_along(): lax.ppermute(x, axis, [(i, (i + by) % devices) for i in range(devices)])  40.3 us
    pallas_call x6, Pallas kernels, call(): pl.pallas_call(kernel, out_shape=outs, in_specs=[SMEM] * len(scalars) + (...  19.5 us
    ppermute x2, starting transfers between devices, passed_along(): lax.ppermute(x, axis, [(i, (i + by) % devices) for i in range(devices)])  10.2 us
    ppermute x2, starting transfers between devices, swap(): return lax.ppermute(x, 'outer', pairs + [(b, a) for a, b in pairs])  8.44 us
  transfers between devices with their start and end apart: 4, of which 2 were waited for; matrix products, arithmetic and copies ran while one was open for 0% of the time, Pallas kernels for 11%

profile of v10, /device:TPU:63, one launch (start us, length us, event | category | flops | bytes accessed | tf_op | source)
XLA Modules:
  0.0 125.9 jit_solution(17717590006201696868)
XLA Ops:
  0.6 0.0 copy-start
  0.6 1.2 copy-done
  1.9 0.0 copy-start.1
  1.9 1.3 %shard_map.76 = bf16[448,1152]{1,0:T(8,128)(2,1)S(1)} custom-call(s32[1]{0:T(128)} %bitcast.role, bf16[448,1152]{1,0:T(8,128)(2,1)S(1)} %copy-done, bf16[448,1152]{1,0:T(8,128)(2,1)} %texts_ref.5), custom_call_target="tpu_custom_call" | custom-call | flops 1000 | bytes 1000 | tf_op jit(solution)/shard_map/pallas_call | solution.py:143
  3.2 0.0 copy-start.2
  3.2 4.1 %collective-permute-start.3 = (bf16[448,1152]{1,0:T(8,128)(2,1)S(1)}, bf16[448,1152]{1,0:T(8,128)(2,1)}, u32[]{:S(2)}, u32[]{:S(2)}) collective-permute-start(bf16[448,1152]{1,0:T(8,128)(2,1)S(1)} %shard_map.76), channel_id=1, source_target_pairs={{1,2},{3,4},{5,6},{7,8},{9,10},{11,12},{13,14},{15,16},{17,18},{19... | collective-permute-start | bytes 3096584 | tf_op jit(solution)/shard_map/ppermute | solution.py:167
  7.3 4.1 %collective-permute-start.2 = (bf16[448,1152]{1,0:T(8,128)(2,1)}, bf16[448,1152]{1,0:T(8,128)(2,1)S(1)}, u32[]{:S(2)}, u32[]{:S(2)}) collective-permute-start(bf16[448,1152]{1,0:T(8,128)(2,1)} %texts_ref.5), channel_id=1, source_target_pairs={{0,32},{32,64},{64,96},{96,128},{128,160},{160,192},{192,224},{224... | collective-permute-start | bytes 3096584 | tf_op jit(solution)/shard_map/ppermute | solution.py:16
  11.4 0.0 copy-done.1
  11.4 0.1 broadcast_select_fusion
  11.5 4.4 %collective-permute-start.1 = (bf16[448,1152]{1,0:T(8,128)(2,1)S(1)}, bf16[448,1152]{1,0:T(8,128)(2,1)S(1)}, u32[]{:S(2)}, u32[]{:S(2)}) collective-permute-start(bf16[448,1152]{1,0:T(8,128)(2,1)S(1)} %broadcast_select_fusion), channel_id=1, source_target_pairs={{0,1},{2,3},{4,5},{6,7},{8,9},{10,11},{12,13},{14,15},{16,17},{18,... | collective-permute-start | bytes 3096584 | tf_op jit(solution)/shard_map/ppermute | solution.py:167
  15.9 6.2 %collective-permute-start = (bf16[448,1152]{1,0:T(8,128)(2,1)S(1)}, bf16[448,1152]{1,0:T(8,128)(2,1)S(1)}, u32[]{:S(2)}, u32[]{:S(2)}) collective-permute-start(bf16[448,1152]{1,0:T(8,128)(2,1)S(1)} %copy-done.1), channel_id=1, source_target_pairs={{0,736},{32,0},{64,32},{96,64},{128,96},{160,128},{192,160},{224,1... | collective-permute-start | bytes 3096584 | tf_op jit(solution)/shard_map/ppermute | solution.py:16
  23.4 0.1 pad_maximum_fusion.scal
  23.5 0.0 copy-done.2
  23.5 4.1 %shard_map.77 = (f32[1,448]{1,0:T(1,128)S(1)}, f32[448,1152]{1,0:T(8,128)S(1)}, f32[448,1152]{1,0:T(8,128)S(1)}) custom-call(f32[2]{0:T(128)S(1)} %pad_maximum_fusion.scal, s32[1,448]{1,0:T(1,128)S(1)} %copy-done.2, bf16[448,1152]{1,0:T(8,128)(2,1)S(1)} %copy-done.1, bf16[448,1152]{1,0:T(8,128)(2,1)} %texts_ref.5), custom_call_target="tpu_custom_call" | custom-call | flops 1000 | bytes 1000 | tf_op jit(solution)/shard_map/pallas_call | solution.py:143
  27.5 43.9 %collective-permute-done.3.far_ref = bf16[448,1152]{1,0:T(8,128)(2,1)} collective-permute-done((bf16[448,1152]{1,0:T(8,128)(2,1)S(1)}, bf16[448,1152]{1,0:T(8,128)(2,1)}, u32[]{:S(2)}, u32[]{:S(2)}) %collective-permute-start.3) | collective-permute-done | bytes 1032224 | tf_op jit(solution)/shard_map/ppermute | solution.py:167
  71.5 3.3 %shard_map.78 = (f32[1,448]{1,0:T(1,128)S(1)}, f32[448,1152]{1,0:T(8,128)S(1)}, f32[448,1152]{1,0:T(8,128)S(1)}) custom-call(f32[2]{0:T(128)S(1)} %pad_maximum_fusion.scal, s32[1]{0:T(128)} %bitcast.role, bf16[448,1152]{1,0:T(8,128)(2,1)S(1)} %copy-done.1, bf16[448,1152]{1,0:T(8,128)(2,1)} %texts_ref.5, bf16[448,1152]{1,0:T(8,128)(2,1)} %collective-permute-done.3.far_ref, ...), custom_call_target="tpu_custom_call" | custom-call | flops 1000 | bytes 1000 | tf_op jit(solution)/shard_map/pallas_call | solution.py:143
  74.8 40.3 %collective-permute-done.2.far_texts_ref = bf16[448,1152]{1,0:T(8,128)(2,1)S(1)} collective-permute-done((bf16[448,1152]{1,0:T(8,128)(2,1)}, bf16[448,1152]{1,0:T(8,128)(2,1)S(1)}, u32[]{:S(2)}, u32[]{:S(2)}) %collective-permute-start.2) | collective-permute-done | bytes 1032224 | tf_op jit(solution)/shard_map/ppermute | solution.py:16
  115.1 2.6 %shard_map.79 = (f32[1,448]{1,0:T(1,128)S(1)}, f32[448,1152]{1,0:T(8,128)S(1)}) custom-call(f32[2]{0:T(128)S(1)} %pad_maximum_fusion.scal, bf16[448,1152]{1,0:T(8,128)(2,1)S(1)} %copy-done.1, bf16[448,1152]{1,0:T(8,128)(2,1)S(1)} %collective-permute-done.2.far_texts_ref, f32[1,448]{1,0:T(1,128)S(1)} %get-tuple-element.25.loss_in, ...), custom_call_target="tpu_custom_call" | custom-call | flops 1000 | bytes 1000 | tf_op jit(solution)/shard_map/pallas_call | solution.py:143
  117.7 0.0 collective-permute-done.1.far_ref
  117.7 4.3 %shard_map.80 = (f32[1,448]{1,0:T(1,128)S(1)}, bf16[448,1152]{1,0:T(8,128)(2,1)}, f32[448,1152]{1,0:T(8,128)S(1)}) custom-call(f32[2]{0:T(128)S(1)} %pad_maximum_fusion.scal, s32[1]{0:T(128)} %bitcast.role, bf16[448,1152]{1,0:T(8,128)(2,1)S(1)} %copy-done.1, bf16[448,1152]{1,0:T(8,128)(2,1)} %texts_ref.5, ...), custom_call_target="tpu_custom_call" | custom-call | flops 1000 | bytes 1000 | tf_op jit(solution)/shard_map/pallas_call | solution.py:143
  122.0 0.0 collective-permute-done.far_images_ref
  122.1 3.8 %shard_map.81 = (f32[1,448]{1,0:T(1,128)}, bf16[448,1152]{1,0:T(8,128)(2,1)}) custom-call(f32[2]{0:T(128)S(1)} %pad_maximum_fusion.scal, bf16[448,1152]{1,0:T(8,128)(2,1)} %texts_ref.5, bf16[448,1152]{1,0:T(8,128)(2,1)S(1)} %collective-permute-done.far_images_ref, f32[1,448]{1,0:T(1,128)S(1)} %get-tuple-element.30.loss_in, ...), custom_call_target="tpu_custom_call" | custom-call | flops 1000 | bytes 1000 | tf_op jit(solution)/shard_map/pallas_call | solution.py:143
Async XLA Ops:
  0.6 1.2 copy-start
  1.9 9.5 %copy-start.1 = (bf16[448,1152]{1,0:T(8,128)(2,1)S(1)}, bf16[448,1152]{1,0:T(8,128)(2,1)}, u32[]{:S(2)}) copy-start(bf16[448,1152]{1,0:T(8,128)(2,1)} %images_ref.5) | copy-start | bytes 3096580
  3.2 20.3 %copy-start.2 = (s32[1,448]{1,0:T(1,128)S(1)}, s32[1,448]{1,0:T(1,128)}, u32[]{:S(2)}) copy-start(s32[1,448]{1,0:T(1,128)} %pos_ref.1) | copy-start | bytes 5380
  3.2 68.3 %collective-permute-start.3 = (bf16[448,1152]{1,0:T(8,128)(2,1)S(1)}, bf16[448,1152]{1,0:T(8,128)(2,1)}, u32[]{:S(2)}, u32[]{:S(2)}) collective-permute-start(bf16[448,1152]{1,0:T(8,128)(2,1)S(1)} %shard_map.76), channel_id=1, source_target_pairs={{1,2},{3,4},{5,6},{7,8},{9,10},{11,12},{13,14},{15,16},{17,18},{19... | collective-permute-start | bytes 3096584 | tf_op jit(solution)/shard_map/ppermute | solution.py:167
  7.3 107.8 %collective-permute-start.2 = (bf16[448,1152]{1,0:T(8,128)(2,1)}, bf16[448,1152]{1,0:T(8,128)(2,1)S(1)}, u32[]{:S(2)}, u32[]{:S(2)}) collective-permute-start(bf16[448,1152]{1,0:T(8,128)(2,1)} %texts_ref.5), channel_id=1, source_target_pairs={{0,32},{32,64},{64,96},{96,128},{128,160},{160,192},{192,224},{224... | collective-permute-start | bytes 3096584 | tf_op jit(solution)/shard_map/ppermute | solution.py:16
  11.5 106.2 %collective-permute-start.1 = (bf16[448,1152]{1,0:T(8,128)(2,1)S(1)}, bf16[448,1152]{1,0:T(8,128)(2,1)S(1)}, u32[]{:S(2)}, u32[]{:S(2)}) collective-permute-start(bf16[448,1152]{1,0:T(8,128)(2,1)S(1)} %broadcast_select_fusion), channel_id=1, source_target_pairs={{0,1},{2,3},{4,5},{6,7},{8,9},{10,11},{12,13},{14,15},{16,17},{18,... | collective-permute-start | bytes 3096584 | tf_op jit(solution)/shard_map/ppermute | solution.py:167
  15.9 106.2 %collective-permute-start = (bf16[448,1152]{1,0:T(8,128)(2,1)S(1)}, bf16[448,1152]{1,0:T(8,128)(2,1)S(1)}, u32[]{:S(2)}, u32[]{:S(2)}) collective-permute-start(bf16[448,1152]{1,0:T(8,128)(2,1)S(1)} %copy-done.1), channel_id=1, source_target_pairs={{0,736},{32,0},{64,32},{96,64},{128,96},{160,128},{192,160},{224,1... | collective-permute-start | bytes 3096584 | tf_op jit(solution)/shard_map/ppermute | solution.py:16

commit v11 on v10

--- a/solution.py
+++ b/solution.py
@@ -102,51 +102,51 @@
         tgrad_ref[...] = tgrad_in[...] + text_side(scal, texts_ref[...], far_ref[...])
 
 
-def dp_text_kernel(scal, images_ref, far_texts_ref, loss_in, igrad_in, loss_ref, igrad_ref):
+def chip_kernel(
+    scal, role, images_ref, texts_ref, far_a, far_b, loss_in, igrad_in, tgrad_in,
+    loss_ref, igrad_ref, tgrad_ref,
+):
+    @pl.when(role[0] != 0)
+    def _():
+        loss_a, grad_a = image_side(scal, images_ref[...], far_a[...])
+        loss_b, grad_b = image_side(scal, images_ref[...], far_b[...])
+        loss_ref[...] = loss_in[...] + loss_a + loss_b
+        igrad_ref[...] = igrad_in[...] + grad_a + grad_b
+        tgrad_ref[...] = tgrad_in[...]
+
+    @pl.when(role[0] == 0)
+    def _():
+        loss_ref[...] = loss_in[...]
+        igrad_ref[...] = igrad_in[...]
+        grad = text_side(scal, texts_ref[...], far_a[...])
+        tgrad_ref[...] = tgrad_in[...] + grad + text_side(scal, texts_ref[...], far_b[...])
+
+
+def last_kernel(
+    scal, images_ref, texts_ref, far_texts_ref, far_images_ref, loss_in, igrad_in, tgrad_in,
+    loss_ref, igrad_out, tgrad_out, igrad_ref, tgrad_ref, sems,
+):
     loss, grad = image_side(scal, images_ref[...], far_texts_ref[...])
-    loss_ref[...] = loss_in[...] + loss
-    igrad_ref[...] = igrad_in[...] + grad
-
-
-def chip_kernel(
-    scal, role, images_ref, texts_ref, far_ref, loss_in, igrad_in, tgrad_in,
-    loss_ref, igrad_out, tgrad_ref, igrad_ref, sem,
-):
-    def send():
-        return pltpu.make_async_copy(igrad_ref, igrad_out, sem)
-
-    @pl.when(role[0] != 0)
-    def _():
-        loss, grad = image_side(scal, images_ref[...], far_ref[...])
-        loss_ref[...] = loss_in[...] + loss
-        igrad_ref[...] = (igrad_in[...] + grad).astype(BF16)
-        send().start()
-        tgrad_ref[...] = tgrad_in[...]
-
-    @pl.when(role[0] == 0)
-    def _():
-        loss_ref[...] = loss_in[...]
-        igrad_ref[...] = igrad_in[...].astype(BF16)
-        send().start()
-        tgrad_ref[...] = tgrad_in[...] + text_side(scal, texts_ref[...], far_ref[...])
-
-    send().wait()
-
-
-def last_kernel(scal, texts_ref, far_images_ref, loss_in, tgrad_in, loss_ref, tgrad_ref):
-    loss_ref[...] = loss_in[...] / (3.0 * loss_in.shape[1])
+    loss_ref[...] = (loss_in[...] + loss) / (3.0 * loss_in.shape[1])
+    igrad_ref[...] = (igrad_in[...] + grad).astype(BF16)
+    image_copy = pltpu.make_async_copy(igrad_ref, igrad_out, sems.at[0])
+    image_copy.start()
     grad = text_side(scal, texts_ref[...], far_images_ref[...])
     tgrad_ref[...] = (tgrad_in[...] + grad).astype(BF16)
-
-
-def call(kernel, outs, scalars, *args, in_specs=None, out_specs=None, scratch=(), room=40):
+    text_copy = pltpu.make_async_copy(tgrad_ref, tgrad_out, sems.at[1])
+    text_copy.start()
+    image_copy.wait()
+    text_copy.wait()
+
+
+def call(kernel, outs, scalars, *args, in_specs=None, out_specs=None, scratch=()):
     return pl.pallas_call(
         kernel,
         out_shape=outs,
         in_specs=[SMEM] * len(scalars) + (in_specs or [VMEM] * len(args)),
         out_specs=out_specs or [VMEM] * len(outs),
         scratch_shapes=scratch,
-        compiler_params=pltpu.CompilerParams(vmem_limit_bytes=room * 1024 * 1024),
+        compiler_params=pltpu.CompilerParams(vmem_limit_bytes=40 * 1024 * 1024),
         cost_estimate=pl.CostEstimate(flops=1000, bytes_accessed=1000, transcendentals=0),
     )(*scalars, *args)
 
@@ -168,29 +168,25 @@
 
     (over_link,) = call(
         pick_kernel, [narrow], [role], images, texts,
-        in_specs=[away, away], scratch=[pltpu.SemaphoreType.DMA(())], room=40,
+        in_specs=[away, away], scratch=[pltpu.SemaphoreType.DMA(())],
     )
     over_link, texts, images = lax.optimization_barrier((over_link, texts, images))
     link = swap(over_link, 1)
     cycle_text = passed_along(texts, "dp", 1)
-    chip = swap(jnp.where(core == 0, texts, images), 0)
+    cut = rows // 2
+    over_chip = jnp.where(core == 0, texts, images)
+    chip = [swap(x, 0) for x in (over_chip[:cut], over_chip[cut:])]
     cycle_images = passed_along(images, "dp", -1)
 
     sums = call(own_kernel, [loss_shape, wide, wide], [scal], positive_index, images, texts)
+    sums = call(link_kernel, [loss_shape, wide, wide], [scal, role], images, texts, link, *sums)
+    sums = call(chip_kernel, [loss_shape, wide, wide], [scal, role], images, texts, *chip, *sums)
+    held = pltpu.VMEM((rows, width), BF16)
     loss, igrad, tgrad = call(
-        link_kernel, [loss_shape, wide, wide], [scal, role], images, texts, link, *sums
-    )
-    loss, igrad = call(
-        dp_text_kernel, [loss_shape, wide], [scal], images, cycle_text, loss, igrad
-    )
-    loss, igrad, tgrad = call(
-        chip_kernel, [loss_shape, narrow, wide], [scal, role],
-        images, texts, chip, loss, igrad, tgrad,
-        out_specs=[VMEM, away, VMEM],
-        scratch=[pltpu.VMEM((rows, width), BF16), pltpu.SemaphoreType.DMA(())],
-    )
-    loss, tgrad = call(
-        last_kernel, [loss_shape, narrow], [scal], texts, cycle_images, loss, tgrad
+        last_kernel, [loss_shape, narrow, narrow], [scal],
+        images, texts, cycle_text, cycle_images, *sums,
+        out_specs=[VMEM, away, away],
+        scratch=[held, held, pltpu.SemaphoreType.DMA((2,))],
     )
     return loss.reshape(rows), igrad, tgrad
 

time: 126 us -> 123 us (0.976)
  the two profiles are of different devices: /device:TPU:63 before, /device:TPU:32 now
where the time goes in v11:
time: 123 us
  waiting for transfers between devices  79.5 us (65%)
  Pallas kernels  20.3 us (17%)
  starting transfers between devices  19.2 us (16%)
  between operations  2.24 us (2%)
  other arithmetic  1.42 us (1%)
    ppermute x3, waiting for transfers between devices, swap(): return lax.ppermute(x, 'outer', pairs + [(b, a) for a, b in pairs])  52.4 us
    ppermute x2, waiting for transfers between devices, passed_along(): lax.ppermute(x, axis, [(i, (i + by) % devices) for i in range(devices)])  27 us
    pallas_call x5, Pallas kernels, call(): pl.pallas_call(kernel, out_shape=outs, in_specs=[SMEM] * len(scalars) + (...  20.3 us
    ppermute x2, starting transfers between devices, passed_along(): lax.ppermute(x, axis, [(i, (i + by) % devices) for i in range(devices)])  10.4 us
    ppermute x3, starting transfers between devices, swap(): return lax.ppermute(x, 'outer', pairs + [(b, a) for a, b in pairs])  8.77 us
  transfers between devices with their start and end apart: 5, of which 2 were waited for; matrix products, arithmetic and copies ran while one was open for 1% of the time, Pallas kernels for 10%

profile of v11, /device:TPU:32, one launch (start us, length us, event | category | flops | bytes accessed | tf_op | source)
XLA Modules:
  0.0 122.7 jit_solution(2127442676341753949)
XLA Ops:
  0.6 1.2 %shard_map.76 = bf16[448,1152]{1,0:T(8,128)(2,1)S(1)} custom-call(s32[1]{0:T(128)} %bitcast.role, bf16[448,1152]{1,0:T(8,128)(2,1)} %images_ref.5, bf16[448,1152]{1,0:T(8,128)(2,1)} %texts_ref.5), custom_call_target="tpu_custom_call" | custom-call | flops 1000 | bytes 1000 | tf_op jit(solution)/shard_map/pallas_call | solution.py:143
  1.9 4.4 %collective-permute-start.4 = (bf16[448,1152]{1,0:T(8,128)(2,1)S(1)}, bf16[448,1152]{1,0:T(8,128)(2,1)}, u32[]{:S(2)}, u32[]{:S(2)}) collective-permute-start(bf16[448,1152]{1,0:T(8,128)(2,1)S(1)} %shard_map.76), channel_id=1, source_target_pairs={{1,2},{3,4},{5,6},{7,8},{9,10},{11,12},{13,14},{15,16},{17,18},{19... | collective-permute-start | bytes 3096584 | tf_op jit(solution)/shard_map/ppermute | solution.py:167
  6.3 6.5 %collective-permute-start = (bf16[448,1152]{1,0:T(8,128)(2,1)}, bf16[448,1152]{1,0:T(8,128)(2,1)S(1)}, u32[]{:S(2)}, u32[]{:S(2)}) collective-permute-start(bf16[448,1152]{1,0:T(8,128)(2,1)} %texts_ref.5), channel_id=1, source_target_pairs={{0,32},{32,64},{64,96},{96,128},{128,160},{160,192},{192,224},{224... | collective-permute-start | bytes 3096584 | tf_op jit(solution)/shard_map/ppermute | solution.py:16
  12.9 3.9 %collective-permute-start.1 = (bf16[448,1152]{1,0:T(8,128)(2,1)}, bf16[448,1152]{1,0:T(8,128)(2,1)S(1)}, u32[]{:S(2)}, u32[]{:S(2)}) collective-permute-start(bf16[448,1152]{1,0:T(8,128)(2,1)} %images_ref.5), channel_id=1, source_target_pairs={{0,736},{32,0},{64,32},{96,64},{128,96},{160,128},{192,160},{224,1... | collective-permute-start | bytes 3096584 | tf_op jit(solution)/shard_map/ppermute | solution.py:16
  16.8 0.0 copy-start
  16.8 1.3 %broadcast_select_fusion = bf16[448,1152]{1,0:T(8,128)(2,1)S(1)} fusion(bf16[448,1152]{1,0:T(8,128)(2,1)} %texts_ref.5, bf16[448,1152]{1,0:T(8,128)(2,1)} %images_ref.5, pred[]{:T(512)S(6)} %eq.5), kind=kLoop, calls=%fused_computation | loop fusion | flops 516096 | bytes 3096577 | tf_op jit(solution)/shard_map/jit(_where)/select_n | solution.py:177
  18.1 0.1 fusion
  18.2 1.9 %collective-permute-start.2 = (bf16[224,1152]{1,0:T(8,128)(2,1)S(1)}, bf16[224,1152]{1,0:T(8,128)(2,1)S(1)}, u32[]{:S(2)}, u32[]{:S(2)}) collective-permute-start(bf16[224,1152]{1,0:T(8,128)(2,1)S(1)} %get-tuple-element.34), channel_id=1, source_target_pairs={{0,1},{2,3},{4,5},{6,7},{8,9},{10,11},{12,13},{14,15},{16,17},{18,... | collective-permute-start | bytes 1548296 | tf_op jit(solution)/shard_map/ppermute | solution.py:167
  20.2 2.4 %collective-permute-start.3 = (bf16[224,1152]{1,0:T(8,128)(2,1)S(1)}, bf16[224,1152]{1,0:T(8,128)(2,1)S(1)}, u32[]{:S(2)}, u32[]{:S(2)}) collective-permute-start(bf16[224,1152]{1,0:T(8,128)(2,1)S(1)} %get-tuple-element.33), channel_id=1, source_target_pairs={{0,1},{2,3},{4,5},{6,7},{8,9},{10,11},{12,13},{14,15},{16,17},{18,... | collective-permute-start | bytes 1548296 | tf_op jit(solution)/shard_map/ppermute | solution.py:167
  23.9 0.1 pad_maximum_fusion.scal
  24.0 0.0 copy-done
  24.0 4.4 %shard_map.77 = (f32[1,448]{1,0:T(1,128)S(1)}, f32[448,1152]{1,0:T(8,128)S(1)}, f32[448,1152]{1,0:T(8,128)S(1)}) custom-call(f32[2]{0:T(128)S(1)} %pad_maximum_fusion.scal, s32[1,448]{1,0:T(1,128)S(1)} %copy-done, bf16[448,1152]{1,0:T(8,128)(2,1)} %images_ref.5, bf16[448,1152]{1,0:T(8,128)(2,1)} %texts_ref.5), custom_call_target="tpu_custom_call" | custom-call | flops 1000 | bytes 1000 | tf_op jit(solution)/shard_map/pallas_call | solution.py:143
  28.4 52.4 %collective-permute-done.4.far_ref = bf16[448,1152]{1,0:T(8,128)(2,1)} collective-permute-done((bf16[448,1152]{1,0:T(8,128)(2,1)S(1)}, bf16[448,1152]{1,0:T(8,128)(2,1)}, u32[]{:S(2)}, u32[]{:S(2)}) %collective-permute-start.4) | collective-permute-done | bytes 1032224 | tf_op jit(solution)/shard_map/ppermute | solution.py:167
  80.8 4.0 %shard_map.78 = (f32[1,448]{1,0:T(1,128)S(1)}, f32[448,1152]{1,0:T(8,128)S(1)}, f32[448,1152]{1,0:T(8,128)S(1)}) custom-call(f32[2]{0:T(128)S(1)} %pad_maximum_fusion.scal, s32[1]{0:T(128)} %bitcast.role, bf16[448,1152]{1,0:T(8,128)(2,1)} %images_ref.5, bf16[448,1152]{1,0:T(8,128)(2,1)} %texts_ref.5, bf16[448,1152]{1,0:T(8,128)(2,1)} %collective-permute-done.4.far_ref, ...), custom_call_target="tpu_custom_call" | custom-call | flops 1000 | bytes 1000 | tf_op jit(solution)/shard_map/pallas_call | solution.py:143
  84.8 0.0 collective-permute-done.2.far_a
  84.8 0.0 collective-permute-done.3.far_b
  84.8 4.0 %shard_map.79 = (f32[1,448]{1,0:T(1,128)S(1)}, f32[448,1152]{1,0:T(8,128)S(1)}, f32[448,1152]{1,0:T(8,128)S(1)}) custom-call(f32[2]{0:T(128)S(1)} %pad_maximum_fusion.scal, s32[1]{0:T(128)} %bitcast.role, bf16[448,1152]{1,0:T(8,128)(2,1)} %images_ref.5, bf16[448,1152]{1,0:T(8,128)(2,1)} %texts_ref.5, bf16[224,1152]{1,0:T(8,128)(2,1)S(1)} %collective-permute-done.2.far_a, ...), custom_call_target="tpu_custom_call" | custom-call | flops 1000 | bytes 1000 | tf_op jit(solution)/shard_map/pallas_call | solution.py:143
  88.9 27.0 %collective-permute-done.far_texts_ref = bf16[448,1152]{1,0:T(8,128)(2,1)S(1)} collective-permute-done((bf16[448,1152]{1,0:T(8,128)(2,1)}, bf16[448,1152]{1,0:T(8,128)(2,1)S(1)}, u32[]{:S(2)}, u32[]{:S(2)}) %collective-permute-start) | collective-permute-done | bytes 1032224 | tf_op jit(solution)/shard_map/ppermute | solution.py:16
  115.9 0.0 collective-permute-done.1.far_images_ref
  115.9 6.6 %shard_map.80 = (f32[1,448]{1,0:T(1,128)}, bf16[448,1152]{1,0:T(8,128)(2,1)}, bf16[448,1152]{1,0:T(8,128)(2,1)}) custom-call(f32[2]{0:T(128)S(1)} %pad_maximum_fusion.scal, bf16[448,1152]{1,0:T(8,128)(2,1)} %images_ref.5, bf16[448,1152]{1,0:T(8,128)(2,1)} %texts_ref.5, bf16[448,1152]{1,0:T(8,128)(2,1)S(1)} %collective-permute-done.far_texts_ref, ...), custom_call_target="tpu_custom_call" | custom-call | flops 1000 | bytes 1000 | tf_op jit(solution)/shard_map/pallas_call | solution.py:143
Async XLA Ops:
  1.9 78.9 %collective-permute-start.4 = (bf16[448,1152]{1,0:T(8,128)(2,1)S(1)}, bf16[448,1152]{1,0:T(8,128)(2,1)}, u32[]{:S(2)}, u32[]{:S(2)}) collective-permute-start(bf16[448,1152]{1,0:T(8,128)(2,1)S(1)} %shard_map.76), channel_id=1, source_target_pairs={{1,2},{3,4},{5,6},{7,8},{9,10},{11,12},{13,14},{15,16},{17,18},{19... | collective-permute-start | bytes 3096584 | tf_op jit(solution)/shard_map/ppermute | solution.py:167
  6.3 109.6 %collective-permute-start = (bf16[448,1152]{1,0:T(8,128)(2,1)}, bf16[448,1152]{1,0:T(8,128)(2,1)S(1)}, u32[]{:S(2)}, u32[]{:S(2)}) collective-permute-start(bf16[448,1152]{1,0:T(8,128)(2,1)} %texts_ref.5), channel_id=1, source_target_pairs={{0,32},{32,64},{64,96},{96,128},{128,160},{160,192},{192,224},{224... | collective-permute-start | bytes 3096584 | tf_op jit(solution)/shard_map/ppermute | solution.py:16
  12.9 103.0 %collective-permute-start.1 = (bf16[448,1152]{1,0:T(8,128)(2,1)}, bf16[448,1152]{1,0:T(8,128)(2,1)S(1)}, u32[]{:S(2)}, u32[]{:S(2)}) collective-permute-start(bf16[448,1152]{1,0:T(8,128)(2,1)} %images_ref.5), channel_id=1, source_target_pairs={{0,736},{32,0},{64,32},{96,64},{128,96},{160,128},{192,160},{224,1... | collective-permute-start | bytes 3096584 | tf_op jit(solution)/shard_map/ppermute | solution.py:16
  16.8 7.2 %copy-start = (s32[1,448]{1,0:T(1,128)S(1)}, s32[1,448]{1,0:T(1,128)}, u32[]{:S(2)}) copy-start(s32[1,448]{1,0:T(1,128)} %pos_ref.1) | copy-start | bytes 5380
  18.2 66.6 %collective-permute-start.2 = (bf16[224,1152]{1,0:T(8,128)(2,1)S(1)}, bf16[224,1152]{1,0:T(8,128)(2,1)S(1)}, u32[]{:S(2)}, u32[]{:S(2)}) collective-permute-start(bf16[224,1152]{1,0:T(8,128)(2,1)S(1)} %get-tuple-element.34), channel_id=1, source_target_pairs={{0,1},{2,3},{4,5},{6,7},{8,9},{10,11},{12,13},{14,15},{16,17},{18,... | collective-permute-start | bytes 1548296 | tf_op jit(solution)/shard_map/ppermute | solution.py:167
  20.2 64.7 %collective-permute-start.3 = (bf16[224,1152]{1,0:T(8,128)(2,1)S(1)}, bf16[224,1152]{1,0:T(8,128)(2,1)S(1)}, u32[]{:S(2)}, u32[]{:S(2)}) collective-permute-start(bf16[224,1152]{1,0:T(8,128)(2,1)S(1)} %get-tuple-element.33), channel_id=1, source_target_pairs={{0,1},{2,3},{4,5},{6,7},{8,9},{10,11},{12,13},{14,15},{16,17},{18,... | collective-permute-start | bytes 1548296 | tf_op jit(solution)/shard_map/ppermute | solution.py:167

commit v12 on v11

--- a/solution.py
+++ b/solution.py
@@ -57,8 +57,12 @@
     return nn(coeff, far_images)
 
 
-def own_kernel(scal, pos_ref, images_ref, texts_ref, loss_ref, igrad_ref, tgrad_ref):
+def own_kernel(
+    scal, pos_ref, images_ref, texts_ref, loss_ref, igrad_ref, tgrad_ref, images_kept, texts_kept
+):
     images, texts = images_ref[...], texts_ref[...]
+    images_kept[...] = images
+    texts_kept[...] = texts
     logits = tile_logits(scal, texts, images)
     mask = pos_ref[...] == lax.broadcasted_iota(jnp.int32, logits.shape, 0)
     e = small(logits)
@@ -178,7 +182,10 @@
     chip = [swap(x, 0) for x in (over_chip[:cut], over_chip[cut:])]
     cycle_images = passed_along(images, "dp", -1)
 
-    sums = call(own_kernel, [loss_shape, wide, wide], [scal], positive_index, images, texts)
+    *sums, images, texts = call(
+        own_kernel, [loss_shape, wide, wide, narrow, narrow], [scal],
+        positive_index, images, texts,
+    )
     sums = call(link_kernel, [loss_shape, wide, wide], [scal, role], images, texts, link, *sums)
     sums = call(chip_kernel, [loss_shape, wide, wide], [scal, role], images, texts, *chip, *sums)
     held = pltpu.VMEM((rows, width), BF16)

time: 123 us -> 122 us (level)
  Pallas kernels: 20.3 us -> 17.7 us
  waiting for transfers between devices: 79.5 us -> 81.1 us
    pallas_call x5, Pallas kernels: 20.3 us -> 17.7 us  [call(): pl.pallas_call(kernel, out_shape=outs, in_specs=[SMEM] * len(scalars) + (...]
    ppermute x2, waiting for transfers between devices: 27 us -> 28.6 us  [passed_along(): lax.ppermute(x, axis, [(i, (i + by) % devices) for i in range(devices)])]
  transfers between devices with their start and end apart: 5 -> 5, of which waited for: 2 -> 2; matrix products, arithmetic and copies ran while one was open for 1% -> 1% of each run, Pallas kernels for 10% -> 9%
where the time goes in v12:
time: 122 us
  waiting for transfers between devices  81.1 us (66%)
  starting transfers between devices  19.2 us (16%)
  Pallas kernels  17.7 us (15%)
  between operations  2.24 us (2%)
  other arithmetic  1.42 us (1%)
    ppermute x3, waiting for transfers between devices, swap(): return lax.ppermute(x, 'outer', pairs + [(b, a) for a, b in pairs])  52.4 us
    ppermute x2, waiting for transfers between devices, passed_along(): lax.ppermute(x, axis, [(i, (i + by) % devices) for i in range(devices)])  28.6 us
    pallas_call x5, Pallas kernels, call(): pl.pallas_call(kernel, out_shape=outs, in_specs=[SMEM] * len(scalars) + (...  17.7 us
    ppermute x2, starting transfers between devices, passed_along(): lax.ppermute(x, axis, [(i, (i + by) % devices) for i in range(devices)])  10.4 us
    ppermute x3, starting transfers between devices, swap(): return lax.ppermute(x, 'outer', pairs + [(b, a) for a, b in pairs])  8.77 us
  transfers between devices with their start and end apart: 5, of which 2 were waited for; matrix products, arithmetic and copies ran while one was open for 1% of the time, Pallas kernels for 9%

profile of v12, /device:TPU:32, one launch (start us, length us, event | category | flops | bytes accessed | tf_op | source)
XLA Modules:
  0.0 121.7 jit_solution(3597061492287751503)
XLA Ops:
  0.6 1.2 %shard_map.76 = bf16[448,1152]{1,0:T(8,128)(2,1)S(1)} custom-call(s32[1]{0:T(128)} %bitcast.role, bf16[448,1152]{1,0:T(8,128)(2,1)} %images_ref.2, bf16[448,1152]{1,0:T(8,128)(2,1)} %texts_ref.2), custom_call_target="tpu_custom_call" | custom-call | flops 1000 | bytes 1000 | tf_op jit(solution)/shard_map/pallas_call | solution.py:147
  1.9 4.4 %collective-permute-start.4 = (bf16[448,1152]{1,0:T(8,128)(2,1)S(1)}, bf16[448,1152]{1,0:T(8,128)(2,1)}, u32[]{:S(2)}, u32[]{:S(2)}) collective-permute-start(bf16[448,1152]{1,0:T(8,128)(2,1)S(1)} %shard_map.76), channel_id=1, source_target_pairs={{1,2},{3,4},{5,6},{7,8},{9,10},{11,12},{13,14},{15,16},{17,18},{19... | collective-permute-start | bytes 3096584 | tf_op jit(solution)/shard_map/ppermute | solution.py:171
  6.3 6.5 %collective-permute-start = (bf16[448,1152]{1,0:T(8,128)(2,1)}, bf16[448,1152]{1,0:T(8,128)(2,1)S(1)}, u32[]{:S(2)}, u32[]{:S(2)}) collective-permute-start(bf16[448,1152]{1,0:T(8,128)(2,1)} %texts_ref.2), channel_id=1, source_target_pairs={{0,32},{32,64},{64,96},{96,128},{128,160},{160,192},{192,224},{224... | collective-permute-start | bytes 3096584 | tf_op jit(solution)/shard_map/ppermute | solution.py:16
  12.9 3.9 %collective-permute-start.1 = (bf16[448,1152]{1,0:T(8,128)(2,1)}, bf16[448,1152]{1,0:T(8,128)(2,1)S(1)}, u32[]{:S(2)}, u32[]{:S(2)}) collective-permute-start(bf16[448,1152]{1,0:T(8,128)(2,1)} %images_ref.2), channel_id=1, source_target_pairs={{0,736},{32,0},{64,32},{96,64},{128,96},{160,128},{192,160},{224,1... | collective-permute-start | bytes 3096584 | tf_op jit(solution)/shard_map/ppermute | solution.py:16
  16.8 0.0 copy-start
  16.8 1.3 %broadcast_select_fusion = bf16[448,1152]{1,0:T(8,128)(2,1)S(1)} fusion(bf16[448,1152]{1,0:T(8,128)(2,1)} %texts_ref.2, bf16[448,1152]{1,0:T(8,128)(2,1)} %images_ref.2, pred[]{:T(512)S(6)} %eq.5), kind=kLoop, calls=%fused_computation | loop fusion | flops 516096 | bytes 3096577 | tf_op jit(solution)/shard_map/jit(_where)/select_n | solution.py:181
  18.1 0.1 fusion
  18.2 1.9 %collective-permute-start.2 = (bf16[224,1152]{1,0:T(8,128)(2,1)S(1)}, bf16[224,1152]{1,0:T(8,128)(2,1)S(1)}, u32[]{:S(2)}, u32[]{:S(2)}) collective-permute-start(bf16[224,1152]{1,0:T(8,128)(2,1)S(1)} %get-tuple-element.38), channel_id=1, source_target_pairs={{0,1},{2,3},{4,5},{6,7},{8,9},{10,11},{12,13},{14,15},{16,17},{18,... | collective-permute-start | bytes 1548296 | tf_op jit(solution)/shard_map/ppermute | solution.py:171
  20.2 2.4 %collective-permute-start.3 = (bf16[224,1152]{1,0:T(8,128)(2,1)S(1)}, bf16[224,1152]{1,0:T(8,128)(2,1)S(1)}, u32[]{:S(2)}, u32[]{:S(2)}) collective-permute-start(bf16[224,1152]{1,0:T(8,128)(2,1)S(1)} %get-tuple-element.37), channel_id=1, source_target_pairs={{0,1},{2,3},{4,5},{6,7},{8,9},{10,11},{12,13},{14,15},{16,17},{18,... | collective-permute-start | bytes 1548296 | tf_op jit(solution)/shard_map/ppermute | solution.py:171
  23.9 0.1 pad_maximum_fusion.scal
  24.0 0.0 copy-done
  24.0 4.4 %shard_map.77 = (f32[1,448]{1,0:T(1,128)S(1)}, f32[448,1152]{1,0:T(8,128)S(1)}, f32[448,1152]{1,0:T(8,128)S(1)}, bf16[448,1152]{1,0:T(8,128)(2,1)S(1)}, bf16[448,1152]{1,0:T(8,128)(2,1)S(1)}) custom-call(f32[2]{0:T(128)S(1)} %pad_maximum_fusion.scal, s32[1,448]{1,0:T(1,128)S(1)} %copy-done, bf16[448,1152]{1,0:T(8,128)(2,1)} %images_ref.2, ...), custom_call_target="tpu_custom_call" | custom-call | flops 1000 | bytes 1000 | tf_op jit(solution)/shard_map/pallas_call | solution.py:147
  28.4 52.4 %collective-permute-done.4.far_ref = bf16[448,1152]{1,0:T(8,128)(2,1)} collective-permute-done((bf16[448,1152]{1,0:T(8,128)(2,1)S(1)}, bf16[448,1152]{1,0:T(8,128)(2,1)}, u32[]{:S(2)}, u32[]{:S(2)}) %collective-permute-start.4) | collective-permute-done | bytes 1032224 | tf_op jit(solution)/shard_map/ppermute | solution.py:171
  80.8 3.3 %shard_map.78 = (f32[1,448]{1,0:T(1,128)S(1)}, f32[448,1152]{1,0:T(8,128)S(1)}, f32[448,1152]{1,0:T(8,128)S(1)}) custom-call(f32[2]{0:T(128)S(1)} %pad_maximum_fusion.scal, s32[1]{0:T(128)} %bitcast.role, bf16[448,1152]{1,0:T(8,128)(2,1)S(1)} %get-tuple-element.22.images_ref, bf16[448,1152]{1,0:T(8,128)(2,1)S(1)} %get-tuple-element.23.texts_ref, ...), custom_call_target="tpu_custom_call" | custom-call | flops 1000 | bytes 1000 | tf_op jit(solution)/shard_map/pallas_call | solution.py:147
  84.2 0.0 collective-permute-done.2.far_a
  84.2 0.0 collective-permute-done.3.far_b
  84.2 3.1 %shard_map.79 = (f32[1,448]{1,0:T(1,128)S(1)}, f32[448,1152]{1,0:T(8,128)S(1)}, f32[448,1152]{1,0:T(8,128)S(1)}) custom-call(f32[2]{0:T(128)S(1)} %pad_maximum_fusion.scal, s32[1]{0:T(128)} %bitcast.role, bf16[448,1152]{1,0:T(8,128)(2,1)S(1)} %get-tuple-element.22.images_ref, bf16[448,1152]{1,0:T(8,128)(2,1)S(1)} %get-tuple-element.23.texts_ref, ...), custom_call_target="tpu_custom_call" | custom-call | flops 1000 | bytes 1000 | tf_op jit(solution)/shard_map/pallas_call | solution.py:147
  87.3 28.6 %collective-permute-done.far_texts_ref = bf16[448,1152]{1,0:T(8,128)(2,1)S(1)} collective-permute-done((bf16[448,1152]{1,0:T(8,128)(2,1)}, bf16[448,1152]{1,0:T(8,128)(2,1)S(1)}, u32[]{:S(2)}, u32[]{:S(2)}) %collective-permute-start) | collective-permute-done | bytes 1032224 | tf_op jit(solution)/shard_map/ppermute | solution.py:16
  115.9 0.0 collective-permute-done.1.far_images_ref
  115.9 5.7 %shard_map.80 = (f32[1,448]{1,0:T(1,128)}, bf16[448,1152]{1,0:T(8,128)(2,1)}, bf16[448,1152]{1,0:T(8,128)(2,1)}) custom-call(f32[2]{0:T(128)S(1)} %pad_maximum_fusion.scal, bf16[448,1152]{1,0:T(8,128)(2,1)S(1)} %get-tuple-element.22.images_ref, bf16[448,1152]{1,0:T(8,128)(2,1)S(1)} %get-tuple-element.23.texts_ref, ...), custom_call_target="tpu_custom_call" | custom-call | flops 1000 | bytes 1000 | tf_op jit(solution)/shard_map/pallas_call | solution.py:147
Async XLA Ops:
  1.9 78.9 %collective-permute-start.4 = (bf16[448,1152]{1,0:T(8,128)(2,1)S(1)}, bf16[448,1152]{1,0:T(8,128)(2,1)}, u32[]{:S(2)}, u32[]{:S(2)}) collective-permute-start(bf16[448,1152]{1,0:T(8,128)(2,1)S(1)} %shard_map.76), channel_id=1, source_target_pairs={{1,2},{3,4},{5,6},{7,8},{9,10},{11,12},{13,14},{15,16},{17,18},{19... | collective-permute-start | bytes 3096584 | tf_op jit(solution)/shard_map/ppermute | solution.py:171
  6.3 109.6 %collective-permute-start = (bf16[448,1152]{1,0:T(8,128)(2,1)}, bf16[448,1152]{1,0:T(8,128)(2,1)S(1)}, u32[]{:S(2)}, u32[]{:S(2)}) collective-permute-start(bf16[448,1152]{1,0:T(8,128)(2,1)} %texts_ref.2), channel_id=1, source_target_pairs={{0,32},{32,64},{64,96},{96,128},{128,160},{160,192},{192,224},{224... | collective-permute-start | bytes 3096584 | tf_op jit(solution)/shard_map/ppermute | solution.py:16
  12.9 103.0 %collective-permute-start.1 = (bf16[448,1152]{1,0:T(8,128)(2,1)}, bf16[448,1152]{1,0:T(8,128)(2,1)S(1)}, u32[]{:S(2)}, u32[]{:S(2)}) collective-permute-start(bf16[448,1152]{1,0:T(8,128)(2,1)} %images_ref.2), channel_id=1, source_target_pairs={{0,736},{32,0},{64,32},{96,64},{128,96},{160,128},{192,160},{224,1... | collective-permute-start | bytes 3096584 | tf_op jit(solution)/shard_map/ppermute | solution.py:16
  16.8 7.2 %copy-start = (s32[1,448]{1,0:T(1,128)S(1)}, s32[1,448]{1,0:T(1,128)}, u32[]{:S(2)}) copy-start(s32[1,448]{1,0:T(1,128)} %pos_ref.1) | copy-start | bytes 5380
  18.2 65.9 %collective-permute-start.2 = (bf16[224,1152]{1,0:T(8,128)(2,1)S(1)}, bf16[224,1152]{1,0:T(8,128)(2,1)S(1)}, u32[]{:S(2)}, u32[]{:S(2)}) collective-permute-start(bf16[224,1152]{1,0:T(8,128)(2,1)S(1)} %get-tuple-element.38), channel_id=1, source_target_pairs={{0,1},{2,3},{4,5},{6,7},{8,9},{10,11},{12,13},{14,15},{16,17},{18,... | collective-permute-start | bytes 1548296 | tf_op jit(solution)/shard_map/ppermute | solution.py:171
  20.2 64.0 %collective-permute-start.3 = (bf16[224,1152]{1,0:T(8,128)(2,1)S(1)}, bf16[224,1152]{1,0:T(8,128)(2,1)S(1)}, u32[]{:S(2)}, u32[]{:S(2)}) collective-permute-start(bf16[224,1152]{1,0:T(8,128)(2,1)S(1)} %get-tuple-element.37), channel_id=1, source_target_pairs={{0,1},{2,3},{4,5},{6,7},{8,9},{10,11},{12,13},{14,15},{16,17},{18,... | collective-permute-start | bytes 1548296 | tf_op jit(solution)/shard_map/ppermute | solution.py:171
